TPU v7x, 512 devices: a whole 4x8x8 slice. The times are simulated.
512 devices in a mesh: tile: 64 (over z, y), group: 8 (over x, core).
Axes of the slice: x: 4, y: 8, z: 8, core: 2. Of those that a mesh axis runs over, the one named last changes fastest.
Arguments:
- object_field: float32 [2, 2048, 16384], P(None, None, 'tile'), may hold values from -6 to 6
- probe: float32 [2, 256, 256], replicated, may hold values from -6 to 6
- amplitudes: bfloat16 [3072, 256, 256], P(('tile', 'group')), may hold values from 0.5 to 3
- row_offset: int32 [3072], P(('tile', 'group')), may hold values from 0 to 1792
- col_offset: int32 [3072], P(('tile', 'group')), may hold values from 0 to 255
- counts: int32 [512], P(('tile', 'group')), may hold values from 1 to 6, as said below
Outputs:
- updated_object: float32 [2, 2048, 16384], P(None, None, 'tile')
Inputs may be any that keep to these rules, and one draw needn't show every extreme that they name: counts[s] live patterns are the first slots of slot set s; the slots after them are ignored.
All inputs are finite; a program needn't handle non-finite values.
Results may differ from a plain program's by a relative error of at most 0.0003.
Values sent between devices are 32-bit elements; how exact they have to be, the bound alone decides.
No kernel may reach another device: no remote copies, remote signals or barrier semaphores. Data moves between devices by JAX's collectives and lax.ppermute only.
A program may use at most 128 MiB of HBM per device.

v0:
```python
import math

import jax
import jax.numpy as jnp
from jax import lax
from jax.sharding import PartitionSpec as P

FLOOR = 0.25
REG = 0.5
HIGH = lax.Precision.HIGHEST


def passed_along(x, axis, by):
    devices = lax.axis_size(axis)
    pairs = [(i, i + by) for i in range(devices) if 0 <= i + by < devices]
    return lax.ppermute(x, axis, pairs)


def tables(length):
    steps = lax.iota(jnp.int32, length)
    product = steps[:, None] * steps[None, :] % length
    angle = product.astype(jnp.float32) * (2.0 * math.pi / length)
    factor = 1.0 / math.sqrt(length)
    return (jnp.cos(angle) * factor, jnp.sin(angle) * factor)


def complex_dot(left_re, left_im, right_re, right_im):
    real_part = jnp.dot(left_re, right_re, precision=HIGH) - jnp.dot(
        left_im, right_im, precision=HIGH
    )
    imag_part = jnp.dot(left_re, right_im, precision=HIGH) + jnp.dot(
        left_im, right_re, precision=HIGH
    )
    return (real_part, imag_part)


def transform(field_re, field_im, table_re, table_im):
    inner_re, inner_im = complex_dot(table_re, table_im, field_re, field_im)
    return complex_dot(inner_re, inner_im, table_re, table_im)


def reduce_group(maps):
    return lax.psum(maps, "group")


def body(object_field, probe, amplitudes, row_offset, col_offset, counts):
    length = probe.shape[1]
    rows = object_field.shape[1]
    tile_width = object_field.shape[2]
    rim = passed_along(object_field, "tile", -1)
    extended = jnp.concatenate([object_field, rim], axis=2)
    cos_table, sin_table = tables(length)
    probe_re = probe[0]
    probe_im = probe[1]
    intensity = probe_re * probe_re + probe_im * probe_im
    zero = jnp.zeros((), jnp.int32)
    channels = 3
    maps_start = jnp.zeros((channels, rows, tile_width + length), jnp.float32)

    def step(index, maps):
        row = row_offset[index]
        col = col_offset[index]
        window = lax.dynamic_slice(extended, (zero, row, col), (2, length, length))
        exit_re = probe_re * window[0] - probe_im * window[1]
        exit_im = probe_re * window[1] + probe_im * window[0]
        far_re, far_im = transform(exit_re, exit_im, cos_table, -sin_table)
        magnitude = jnp.sqrt(far_re * far_re + far_im * far_im)
        factor = amplitudes[index].astype(jnp.float32) / jnp.maximum(magnitude, FLOOR) - 1.0
        back_re, back_im = transform(far_re * factor, far_im * factor, cos_table, sin_table)
        grad_re = probe_re * back_re + probe_im * back_im
        grad_im = probe_re * back_im - probe_im * back_re
        contrib = jnp.stack([grad_re, grad_im, intensity])
        current = lax.dynamic_slice(maps, (zero, row, col), (channels, length, length))
        return lax.dynamic_update_slice(maps, current + contrib, (zero, row, col))

    maps = lax.fori_loop(jnp.int32(0), counts[0], step, maps_start)
    widths = ((0, 0), (0, 0), (0, tile_width - length))
    spill = passed_along(maps[:, :, tile_width:], "tile", 1)
    summed = reduce_group(maps[:, :, :tile_width] + spill)
    illum = summed[2:3]
    return object_field + summed[0:2] / (illum + REG)


def solution(mesh):
    in_specs = (
        P(None, None, "tile"),
        P(),
        P(("tile", "group"), None, None),
        P(("tile", "group")),
        P(("tile", "group")),
        P(("tile", "group")),
    )
    out_specs = P(None, None, "tile")
    return jax.shard_map(body, mesh=mesh, in_specs=in_specs, out_specs=out_specs, check_vma=False)
```

profile of v0, /device:TPU:449, one launch (start us, length us, event | category | flops | bytes accessed | tf_op | source)
XLA Modules:
  0.0 630.0 jit_solution(17805034328937076720)
XLA Ops:
  6.5 0.0 all-reduce.2.cloned.1.call-start
  6.5 5.1 collective-permute-start
  11.6 1.1 multiply_add_fusion.1
  12.7 1.1 slice_bitcast_fusion
  13.8 87.4 %collective-permute-done = f32[2,2048,256]{2,1,0:T(8,128)} collective-permute-done((f32[2,2048,256]{2,1,0:T(8,128)}, f32[2,2048,256]{2,1,0:T(8,128)}, u32[]{:S(2)}, u32[]{:S(2)}) %collective-permute-start) | collective-permute-done | bytes 4194336 | tf_op jit(solution)/shard_map/ppermute | solution.py:16
  101.2 7.8 %pad_maximum_fusion = f32[2,2048,512]{2,1,0:T(8,128)} fusion(f32[2,2048,256]{2,1,0:T(8,128)} %collective-permute-done, f32[2,2048,256]{2,1,0:T(8,128)} %param.8), kind=kLoop, calls=%fused_computation.125 | loop fusion | flops 2097152 | bytes 16777216 | tf_op jit(solution)/shard_map/concatenate | solution.py:51
  109.0 0.0 copy-start.2
  109.0 0.0 copy-start.3
  109.0 0.0 copy-start.4
  109.0 6.1 broadcast_in_dim.2
  115.1 0.0 copy-done.2
  115.1 0.0 copy-done.3
  115.1 0.0 copy-done.4
  115.1 43.8 %while.14 = (s32[]{:T(128)}, f32[3,2048,512]{2,1,0:T(8,128)}, s32[]{:T(128)}, s32[6]{0:T(128)S(1)}, s32[6]{0:T(128)S(1)}, /*index=5*/f32[2,2048,512]{2,1,0:T(8,1...) while((s32[]{:T(128)}, f32[3,2048,512]{2,1,0:T(8,128)}, ...), condition=%wide.region_1.2_spmd.clone.clone, body=%wide.region_0.1_spmd.clone.clone.sunk | while | flops 3241213952 | bytes 18612560 | solution.py:76
  115.8 0.7 dynamic_slice.59
  118.6 0.7 dynamic_slice.60
  121.3 1.3 multiply_add_fusion.3
  122.7 1.5 fusion.173
  124.1 1.5 convolution_subtract_fusion.7
  125.6 1.5 fusion.175
  127.1 1.5 convolution_add_fusion.8
  128.6 1.5 fusion.176
  130.1 1.5 convolution_add_fusion.9
  131.5 1.5 fusion.174
  133.0 1.5 convolution_subtract_fusion.8
  134.5 1.6 fusion.179
  136.1 1.6 convolution_add_fusion.10
  137.7 1.6 fusion.177
  139.4 1.6 convolution_subtract_fusion.9
  141.0 1.5 fusion.180
  142.5 1.5 fusion.178
  144.0 1.5 convolution_add_fusion.11
  145.4 1.5 add_bitcast_fusion.2
  146.9 1.6 maximum_add_fusion.2
  148.5 9.6 %dynamic_update_slice.9 = f32[3,2048,512]{2,1,0:T(8,128)} dynamic-update-slice(f32[3,2048,512]{2,1,0:T(8,128)} %get-tuple-element.388, f32[3,256,256]{2,1,0:T(8,128)S(1)} %maximum_add_fusion.2, s32[]{:T(128)} %constant.53.clone.1..sunk, s32[]{:T(128)S(6)} %select_n.151, s32[]{:T(128)S(6)} %select_n.152) | dynamic-update-slice | bytes 1572868 | tf_op jit(solution)/shard_map/while/body/dynamic_update_slice | solution.py:74
  159.0 0.0 copy-start
  159.0 3.4 slice.35
  162.3 44.4 %collective-permute-start.1 = (f32[3,2048,256]{2,1,0:T(8,128)S(1)}, f32[3,2048,256]{2,1,0:T(8,128)}, u32[]{:S(2)}, u32[]{:S(2)}) collective-permute-start(f32[3,2048,256]{2,1,0:T(8,128)S(1)} %slice.35), channel_id=1, source_target_pairs={{0,8},{8,16},{16,24},{24,32},{32,40},{40,48},{48,56},{56,64},{64,7... | collective-permute-start | bytes 18874376 | tf_op jit(solution)/shard_map/ppermute | solution.py:16
  206.8 132.2 %collective-permute-done.1 = f32[3,2048,256]{2,1,0:T(8,128)} collective-permute-done((f32[3,2048,256]{2,1,0:T(8,128)S(1)}, f32[3,2048,256]{2,1,0:T(8,128)}, u32[]{:S(2)}, u32[]{:S(2)}) %collective-permute-start.1) | collective-permute-done | bytes 6291488 | tf_op jit(solution)/shard_map/ppermute | solution.py:16
  339.0 0.0 copy-done
  339.0 7.0 %slice_add_fusion = f32[3,2048,256]{2,1,0:T(8,128)} fusion(f32[3,2048,256]{2,1,0:T(8,128)} %collective-permute-done.1, f32[3,2048,512]{2,1,0:T(8,128)S(1)} %copy-done), kind=kLoop, calls=%fused_computation.126 | loop fusion | flops 1572864 | bytes 18874368 | tf_op jit(solution)/shard_map/add | solution.py:79
  346.1 0.0 all-reduce.2.cloned.1.call-update
  346.1 269.4 %all-reduce.2.cloned.1.call-done = f32[3,2048,256]{2,1,0:T(8,128)} async-done(((f32[3,2048,256]{2,1,0:T(8,128)}), f32[3,2048,256]{2,1,0:T(8,128)}) %all-reduce.2.cloned.1.call-update) | async-done | bytes 6291472 | tf_op jit(solution)/shard_map/psum | solution.py:43
  615.5 0.0 copy-start.1
  615.5 1.9 fusion.112
  617.4 0.9 copy-done.1
  618.3 4.9 fusion.111
Async XLA Ops:
  6.5 609.0 %all-reduce.2.cloned.1.call-start = ((), (), s32[]{:S(2)}) async-start(), calls=%async_computation | async-start | bytes 12582912 | tf_op jit(solution)/shard_map/psum | solution.py:43
  6.5 94.6 %collective-permute-start = (f32[2,2048,256]{2,1,0:T(8,128)}, f32[2,2048,256]{2,1,0:T(8,128)}, u32[]{:S(2)}, u32[]{:S(2)}) collective-permute-start(f32[2,2048,256]{2,1,0:T(8,128)} %param.8), channel_id=1, source_target_pairs={{8,0},{16,8},{24,16},{32,24},{40,32},{48,40},{56,48},{64,56},{72,6... | collective-permute-start | bytes 12582920 | tf_op jit(solution)/shard_map/ppermute | solution.py:16
  109.0 6.1 copy-start.2
  109.0 6.1 copy-start.3
  109.0 6.2 copy-start.4
  159.0 180.1 %copy-start = (f32[3,2048,512]{2,1,0:T(8,128)S(1)}, f32[3,2048,512]{2,1,0:T(8,128)}, u32[]{:S(2)}) copy-start(f32[3,2048,512]{2,1,0:T(8,128)} %get-tuple-element.202) | copy-start | bytes 37748740
  162.3 176.7 %collective-permute-start.1 = (f32[3,2048,256]{2,1,0:T(8,128)S(1)}, f32[3,2048,256]{2,1,0:T(8,128)}, u32[]{:S(2)}, u32[]{:S(2)}) collective-permute-start(f32[3,2048,256]{2,1,0:T(8,128)S(1)} %slice.35), channel_id=1, source_target_pairs={{0,8},{8,16},{16,24},{24,32},{32,40},{40,48},{48,56},{56,64},{64,7... | collective-permute-start | bytes 18874376 | tf_op jit(solution)/shard_map/ppermute | solution.py:16
  615.5 2.8 copy-start.1
Sparse Core Ops, SparseCore 0:
  346.2 269.2 all-reduce.1
where the time goes:
time: 639 us; the launch traced here: 630 us
  waiting for transfers between devices  489 us (77%)
  starting transfers between devices  49.5 us (8%)
  other arithmetic  25.6 us (4%)
  matrix products  24.2 us (4%)
  local copies, waits for them, and re-layouts  22.4 us (4%)
  between operations  13.5 us (2%)
    psum x1, waiting for transfers between devices, reduce_group(): return lax.psum(maps, 'group')  269 us
    ppermute x2, waiting for transfers between devices, passed_along(): return lax.ppermute(x, axis, pairs)  220 us
    ppermute x2, starting transfers between devices, passed_along(): return lax.ppermute(x, axis, pairs)  49.5 us
  transfers between devices with their start and end apart: 3, of which 3 were waited for; matrix products, arithmetic and copies ran while one was open for 0% of the time, Pallas kernels for 0%

commit v1 on v0

v1 whole, which is shorter than its diff:
```python
import functools
import math

import jax
import jax.numpy as jnp
import numpy as np
from jax import lax
from jax.experimental import pallas as pl
from jax.experimental.pallas import tpu as pltpu
from jax.sharding import PartitionSpec as P

FLOOR = 0.25
REG = 0.5
SUB = 8
MIB = 2**20

STEPS = (0, -2, 2, 4)


def tables(length):
    steps = np.arange(length)
    angle = (steps[:, None] * steps[None, :] % length) * (2.0 * math.pi / length)
    factor = 1.0 / math.sqrt(length)
    cos, sin = np.cos(angle) * factor, np.sin(angle) * factor
    parts = []
    for table in (cos, cos - sin, cos + sin):
        table = table.astype(np.float32)
        high = table.astype(jnp.bfloat16)
        low = (table - high.astype(np.float32)).astype(jnp.bfloat16)
        parts += [high, low]
    return np.stack(parts)


def split(x):
    high = x.astype(jnp.bfloat16)
    return high, (x - high.astype(jnp.float32)).astype(jnp.bfloat16)


def dot(a, b):
    return jnp.dot(a, b, preferred_element_type=jnp.float32)


def right(x, tab, which):
    high, low = split(x)
    th, tl = tab[2 * which], tab[2 * which + 1]
    return dot(high, th) + dot(low, th) + dot(high, tl)


def left(x, tab, which):
    high, low = split(x)
    th, tl = tab[2 * which], tab[2 * which + 1]
    return dot(th, high) + dot(th, low) + dot(tl, high)


def forward(mul, a, b, tab):
    both = mul(a + b, tab, 0)
    return both - mul(b, tab, 1), both - mul(a, tab, 2)


def inverse(mul, a, b, tab):
    both = mul(a + b, tab, 0)
    return both - mul(b, tab, 2), both - mul(a, tab, 1)


def class_of(group, step, other, parts):
    index = (group + step) & (parts - 1)
    return index ^ 1 if other else index


def patterns_kernel(size, rows, parts, slots, group_ref, row_ref, col_ref, count_ref, own_ref, probe_hbm, amp_hbm, tab_hbm, *refs):
    pieces, refs = refs[:parts], refs[parts:]
    out_ref, own_buf, rim_buf, probe_ref, amp_ref, tab_ref, stage, own_sems, fixed_sems, piece_sems, store_sems = refs
    group, count = group_ref[0], count_ref[0]
    span = size + SUB
    depth = size // parts

    def start_of(p):
        return pl.multiple_of(row_ref[p] & -SUB, SUB)

    def first_of(p):
        return pl.multiple_of(jnp.minimum(start_of(p), rows - span), SUB)

    def load(p):
        slot = lax.rem(p, 2)
        return pltpu.make_async_copy(own_ref.at[:, pl.ds(first_of(p), span)], own_buf.at[slot], own_sems.at[slot])

    def store(p):
        where = pl.ds(pl.multiple_of(p * 2 * depth, 2 * depth), 2 * depth)
        return pltpu.make_async_copy(stage.at[:, where], out_ref.at[:, where], store_sems.at[p])

    fixed = [
        pltpu.make_async_copy(a, b, fixed_sems.at[n])
        for n, (a, b) in enumerate(((probe_hbm, probe_ref), (tab_hbm, tab_ref), (amp_hbm, amp_ref)))
    ]
    rims = []
    for n, piece in enumerate(pieces):
        index = class_of(group, STEPS[n // 2], n % 2, parts)
        rims.append(pltpu.make_async_copy(piece, rim_buf.at[:, :, index], piece_sems.at[n]))
    load(0).start()
    for copy in rims + fixed:
        copy.start()

    lane = lax.broadcasted_iota(jnp.int32, (SUB, size), 1)
    head_row = lax.broadcasted_iota(jnp.int32, (SUB, size), 0)
    column = lax.broadcasted_iota(jnp.int32, (size, size), 1)
    note = jnp.where(lane == 2 * slots, count, 0)
    for p in range(slots):
        note = jnp.where(lane == p, row_ref[p], note)
        note = jnp.where(lane == slots + p, col_ref[p], note)
    note = note.astype(jnp.float32)
    for part in range(parts):
        stage[part, slots * 2 * depth :] = note
    notes = pl.ds(slots * 2 * depth, SUB)
    last = pltpu.make_async_copy(stage.at[:, notes], out_ref.at[:, notes], store_sems.at[slots])
    last.start()
    for copy in fixed + rims:
        copy.wait()
    rim = rim_buf.reshape(2, rows, size)

    def pattern(p, _):
        slot = lax.rem(p, 2)
        row, col = row_ref[p], col_ref[p]
        base = start_of(p)
        shift = row - base

        @pl.when(p + 1 < count)
        def _():
            load(p + 1).start()

        pr, pi = [pltpu.roll(pltpu.roll(probe_ref[ch], shift, 0), col, 1) for ch in range(2)]
        mine = column >= col
        load(p).wait()
        lead = pl.multiple_of(base - first_of(p), SUB)
        tail = pl.multiple_of(jnp.minimum(lead + size, size), SUB)
        tail_rim = pl.multiple_of(jnp.minimum(base + size, rows - SUB), SUB)

        def window(ch):
            full = jnp.where(mine, own_buf[slot, ch, pl.ds(lead, size)], rim[ch, pl.ds(base, size)])
            wrap = jnp.where(mine[:SUB], own_buf[slot, ch, pl.ds(tail, SUB)], rim[ch, pl.ds(tail_rim, SUB)])
            head = jnp.where(head_row >= shift, full[:SUB], wrap)
            return jnp.concatenate([head, full[SUB:]], axis=0)

        o_re, o_im = window(0), window(1)
        a = pr * o_re - pi * o_im
        b = pr * o_im + pi * o_re
        a, b = forward(right, a, b, tab_ref)
        a, b = forward(left, a, b, tab_ref)
        factor = amp_ref[p].astype(jnp.float32) * lax.rsqrt(jnp.maximum(a * a + b * b, FLOOR * FLOOR)) - 1.0
        a, b = a * factor, b * factor
        a, b = inverse(left, a, b, tab_ref)
        a, b = inverse(right, a, b, tab_ref)
        for ch, g in enumerate((pr * a + pi * b, pr * b - pi * a)):
            for t in range(parts):
                index = ((base >> 3) + t) & (parts - 1)
                for m in range(depth // SUB):
                    at = pl.multiple_of((2 * p + ch) * depth + SUB * m, SUB)
                    block = SUB * (parts * m + t)
                    stage[index, pl.ds(at, SUB)] = g[block : block + SUB]
        store(p).start()
        return 0

    lax.fori_loop(0, count, pattern, 0)

    def stored(p, _):
        store(p).wait()
        return 0

    last.wait()
    lax.fori_loop(0, count, stored, 0)


def patterns(group, own, pieces, probe, amplitudes, row, col, count):
    rows, size = own.shape[1:]
    slots, parts = amplitudes.shape[0], len(pieces)
    depth = size // parts
    length = slots * 2 * depth + SUB
    smem = pl.BlockSpec(memory_space=pltpu.SMEM)
    hbm = pl.BlockSpec(memory_space=pl.ANY)
    tab = jnp.asarray(tables(size))
    return pl.pallas_call(
        functools.partial(patterns_kernel, size, rows, parts, slots),
        out_shape=jax.ShapeDtypeStruct((parts, length, size), jnp.float32),
        in_specs=[smem] * 4 + [hbm] * (4 + parts),
        out_specs=hbm,
        scratch_shapes=[
            pltpu.VMEM((2, 2, size + SUB, size), jnp.float32),
            pltpu.VMEM((2, rows // (SUB * parts), parts, SUB, size), jnp.float32),
            pltpu.VMEM(probe.shape, jnp.float32),
            pltpu.VMEM(amplitudes.shape, amplitudes.dtype),
            pltpu.VMEM(tab.shape, tab.dtype),
            pltpu.VMEM((parts, length, size), jnp.float32),
            pltpu.SemaphoreType.DMA((2,)),
            pltpu.SemaphoreType.DMA((3,)),
            pltpu.SemaphoreType.DMA((parts,)),
            pltpu.SemaphoreType.DMA((slots + 1,)),
        ],
        compiler_params=pltpu.CompilerParams(vmem_limit_bytes=40 * MIB),
        cost_estimate=pl.CostEstimate(flops=36 * 2 * size**3 * slots, bytes_accessed=12 * MIB, transcendentals=0),
        name="patterns",
    )(group, row, col, count, own, probe, amplitudes, tab, *pieces)


def place(row, group, parts):
    block = row >> 3
    first = (group - block) & (parts - 1)
    local = (block + first - group) >> (parts.bit_length() - 1)
    return first, pl.multiple_of(local * SUB, SUB), jnp.where(first == 0, row & (SUB - 1), 0)


def each_live(notes_ref, slots, step):
    def device(d, _):
        def pattern(p, _):
            step(d, p, notes_ref[d, p], notes_ref[d, slots + p])
            return 0

        return lax.fori_loop(0, notes_ref[d, 2 * slots], pattern, 0)

    lax.fori_loop(0, notes_ref.shape[0], device, 0)


def gather_kernel(size, parts, slots, group_ref, notes_ref, got_ref, here_ref, next_ref, total):
    depth = size // parts
    group = group_ref[0]
    total[...] = jnp.zeros_like(total)
    column = lax.broadcasted_iota(jnp.int32, (depth, size), 1)
    head_row = lax.broadcasted_iota(jnp.int32, (SUB, size), 0)

    def step(d, p, row, col):
        _, at, shift = place(row, group, parts)
        mine = column >= col
        for ch in range(2):
            block = got_ref[d, pl.ds(pl.multiple_of((2 * p + ch) * depth, depth), depth)]
            for side in range(2):
                part = jnp.where(mine if side == 0 else jnp.logical_not(mine), block, 0.0)
                head = part[:SUB]
                total[side, ch, pl.ds(at, SUB)] += jnp.where(head_row >= shift, head, 0.0)
                total[side, ch, pl.ds(at + SUB, depth - SUB)] += part[SUB:]
                total[side, ch, pl.ds(at + depth, SUB)] += jnp.where(head_row < shift, head, 0.0)

    each_live(notes_ref, slots, step)
    kept = here_ref.shape[1]
    here_ref[...] = total[0, :, :kept]
    next_ref[...] = total[1, :, :kept]


def gathered(group, notes, got, slots, kept):
    parts, length, size = got.shape
    smem = pl.BlockSpec(memory_space=pltpu.SMEM)
    vmem = pl.BlockSpec(memory_space=pltpu.VMEM)
    shape = jax.ShapeDtypeStruct((2, kept, size), jnp.float32)
    return pl.pallas_call(
        functools.partial(gather_kernel, size, parts, slots),
        out_shape=(shape, shape),
        in_specs=[smem, smem, vmem],
        out_specs=(vmem, vmem),
        scratch_shapes=[pltpu.VMEM((2, 2, kept + SUB, size), jnp.float32)],
        compiler_params=pltpu.CompilerParams(vmem_limit_bytes=24 * MIB),
        cost_estimate=pl.CostEstimate(flops=2**22, bytes_accessed=6 * MIB, transcendentals=0),
        name="gathered",
    )(group, notes, got)


def illumination_kernel(size, parts, slots, group_ref, here_ref, before_ref, probe_ref, out_ref, intensity, total):
    depth = size // parts
    group = group_ref[0]
    square = probe_ref[0] * probe_ref[0] + probe_ref[1] * probe_ref[1]
    intensity[:SUB] = square[size - SUB :]
    intensity[SUB:] = square
    total[...] = jnp.zeros_like(total)
    column = lax.broadcasted_iota(jnp.int32, (depth, size), 1)
    head_row = lax.broadcasted_iota(jnp.int32, (SUB, size), 0)

    for side, ref in enumerate((here_ref, before_ref)):

        def step(d, p, row, col):
            first, at, shift = place(row, group, parts)
            down = row & (SUB - 1)
            blocks = []
            for m in range(depth // SUB):
                start = pl.multiple_of((parts * m + first) * SUB, SUB)
                above, below = [pltpu.roll(intensity[pl.ds(start + n * SUB, SUB)], down, 0) for n in range(2)]
                blocks.append(jnp.where(head_row >= down, below, above))
            placed = pltpu.roll(jnp.concatenate(blocks, axis=0), col, 1)
            part = jnp.where(column >= col if side == 0 else column < col, placed, 0.0)
            head = part[:SUB]
            total[pl.ds(at, SUB)] += jnp.where(head_row >= shift, head, 0.0)
            total[pl.ds(at + SUB, depth - SUB)] += part[SUB:]
            total[pl.ds(at + depth, SUB)] += jnp.where(head_row < shift, head, 0.0)

        each_live(ref, slots, step)
    out_ref[...] = total[: out_ref.shape[0]] + REG


def illumination(group, here, before, probe, slots, kept):
    size = probe.shape[1]
    parts = here.shape[0]
    smem = pl.BlockSpec(memory_space=pltpu.SMEM)
    vmem = pl.BlockSpec(memory_space=pltpu.VMEM)
    return pl.pallas_call(
        functools.partial(illumination_kernel, size, parts, slots),
        out_shape=jax.ShapeDtypeStruct((kept, size), jnp.float32),
        in_specs=[smem, smem, smem, vmem],
        out_specs=vmem,
        scratch_shapes=[
            pltpu.VMEM((size + SUB, size), jnp.float32),
            pltpu.VMEM((kept + SUB, size), jnp.float32),
        ],
        compiler_params=pltpu.CompilerParams(vmem_limit_bytes=16 * MIB),
        cost_estimate=pl.CostEstimate(flops=2**22, bytes_accessed=8 * MIB, transcendentals=0),
        name="illumination",
    )(group, here, before, probe)


def assemble_kernel(parts, group_ref, *refs):
    pieces, out_ref, sems = refs[:-2], refs[-2], refs[-1]
    group = group_ref[0]
    copies = []
    for n, piece in enumerate(pieces):
        whole = n < 6
        index = class_of(group, STEPS[n // 2] if whole else STEPS[3], n % 2, parts)
        place = out_ref.at[:, :, index] if whole else out_ref.at[(n - 6) // 2, :, index]
        copies.append(pltpu.make_async_copy(piece, place, sems.at[n]))
    for copy in copies:
        copy.start()
    for copy in copies:
        copy.wait()


def assembled(group, pieces, shape):
    parts = shape[2]
    return pl.pallas_call(
        functools.partial(assemble_kernel, parts),
        out_shape=jax.ShapeDtypeStruct(shape, jnp.float32),
        in_specs=[pl.BlockSpec(memory_space=pltpu.SMEM)] + [pl.BlockSpec(memory_space=pl.ANY)] * len(pieces),
        out_specs=pl.BlockSpec(memory_space=pl.ANY),
        scratch_shapes=[pltpu.SemaphoreType.DMA((len(pieces),))],
        cost_estimate=pl.CostEstimate(flops=0, bytes_accessed=8 * MIB, transcendentals=0),
        name="assembled",
    )(group, *pieces)


def passed_along(x, axis, by):
    devices = lax.axis_size(axis)
    pairs = [(i, i + by) for i in range(devices) if 0 <= i + by < devices]
    return lax.ppermute(x, axis, pairs)


def to_chip(x, by):
    devices = lax.axis_size("group")
    return lax.ppermute(x, "group", [(i, (i + 2 * by) % devices) for i in range(devices)])


def to_core(x):
    return lax.ppermute(x, "group", [(i, i ^ 1) for i in range(lax.axis_size("group"))])


def body(object_field, probe, amplitudes, row_offset, col_offset, counts):
    parts = lax.axis_size("group")
    index = lax.axis_index("group")
    group = index[None]
    rows, size = object_field.shape[1:]
    slots = amplitudes.shape[0]
    kept = rows // parts
    blocks = object_field.reshape(2, kept // SUB, parts, SUB, size)

    def share(which):
        return lax.dynamic_index_in_dim(blocks, which, 2, keepdims=False)

    mine = share(index)
    near = passed_along(mine, "tile", -1)
    near, opposite = lax.optimization_barrier((near, share((index + 4) % parts)))
    opposite = passed_along(opposite, "tile", -1)
    before, after = to_chip(near, 1), to_chip(near, -1)
    pieces = []
    for piece in (near, before, after, opposite):
        pieces += [piece, to_core(piece)]
    sent = patterns(group, object_field, pieces, probe, amplitudes, row_offset, col_offset, counts)
    got = lax.all_to_all(sent, "group", 0, 0)
    notes = got[:, slots * 2 * (size // parts), : 2 * slots + 1].astype(jnp.int32)
    notes_before = passed_along(notes, "tile", 1)
    here, spill = gathered(group, notes, got, slots, kept)
    spill = passed_along(spill, "tile", 1)
    weight = illumination(group, notes, notes_before, probe, slots, kept)
    result = mine + ((here + spill) / weight).reshape(mine.shape)
    before, after = to_chip(result, 1), to_chip(result, -1)
    upper, lower = to_chip(before[0], 1), to_chip(after[1], -1)
    pieces = []
    for piece in (result, before, after, upper, lower):
        pieces += [piece, to_core(piece)]
    return assembled(group, pieces, blocks.shape).reshape(object_field.shape)


def solution(mesh):
    in_specs = (
        P(None, None, "tile"),
        P(),
        P(("tile", "group"), None, None),
        P(("tile", "group")),
        P(("tile", "group")),
        P(("tile", "group")),
    )
    out_specs = P(None, None, "tile")
    return jax.shard_map(body, mesh=mesh, in_specs=in_specs, out_specs=out_specs, check_vma=False)
```

time: 639 us -> 306 us (0.48); the launches traced: 630 us -> 304 us
  waiting for transfers between devices: 489 us -> 35.5 us
  Pallas kernels: 0 us -> 141 us
  blocking collectives: 0 us -> 51.3 us
  other arithmetic: 25.6 us -> 0.13 us
  matrix products: 24.2 us -> 0 us
  starting transfers between devices: 49.5 us -> 66 us
  local copies, waits for them, and re-layouts: 22.4 us -> 8.99 us
  between operations: 13.5 us -> 1.04 us
    psum x1 -> x0, waiting for transfers between devices: 269 us -> none  [reduce_group(): return lax.psum(maps, 'group')]
    ppermute x2 -> x4, waiting for transfers between devices: 220 us -> 23.5 us  [passed_along(): return lax.ppermute(x, axis, pairs)]
    pallas_call x0 -> x4, Pallas kernels: none -> 141 us  [the longest x1 128 us: assembled(): pl.pallas_call(functools.partial(assemble_kernel, parts), out_shape=jax.S...]
    all_to_all x0 -> x1, blocking collectives: none -> 51.3 us  [body(): got = lax.all_to_all(sent, 'group', 0, 0)]
    ppermute x0 -> x15, starting transfers between devices: none -> 50.9 us  [the longest x9 33.4 us: to_core(): lax.ppermute(x, 'group', [(i, i ^ 1) for i in range(lax.axis_size('group'...]
    ppermute x2 -> x4, starting transfers between devices: 49.5 us -> 15.1 us  [passed_along(): return lax.ppermute(x, axis, pairs)]
    dot_general x16 -> x0, matrix products: 24.2 us -> none  [the longest x4 6.07 us: complex_dot(): jnp.dot(left_im, right_im, precision=HIGH)]
    add x5 -> x1, other arithmetic: 15.9 us -> 0.12 us  [body(): result = mine + ((here + spill) / weight).reshape(mine.shape)]
  transfers between devices with their start and end apart: 3 -> 19, of which waited for: 3 -> 7; matrix products, arithmetic and copies ran while one was open for 0% -> 0% of each run, Pallas kernels for 0% -> 1%
where the time goes in v1:
time: 306 us; the launch traced here: 304 us
  Pallas kernels  141 us (46%)
  starting transfers between devices  66 us (22%)
  blocking collectives  51.3 us (17%)
  waiting for transfers between devices  35.5 us (12%)
  local copies, waits for them, and re-layouts  8.99 us (3%)
    pallas_call x1, Pallas kernels, assembled(): pl.pallas_call(functools.partial(assemble_kernel, parts), out_shape=jax.S...  128 us
    all_to_all x1, blocking collectives, body(): got = lax.all_to_all(sent, 'group', 0, 0)  51.3 us
    ppermute x9, starting transfers between devices, to_core(): lax.ppermute(x, 'group', [(i, i ^ 1) for i in range(lax.axis_size('group'...  33.4 us
    ppermute x4, waiting for transfers between devices, passed_along(): return lax.ppermute(x, axis, pairs)  23.5 us
    ppermute x6, starting transfers between devices, to_chip(): lax.ppermute(x, 'group', [(i, (i + 2 * by) % devices) for i in range(devi...  17.5 us
    ppermute x4, starting transfers between devices, passed_along(): return lax.ppermute(x, axis, pairs)  15.1 us
    ppermute x6, waiting for transfers between devices, to_chip(): lax.ppermute(x, 'group', [(i, (i + 2 * by) % devices) for i in range(devi...  10.8 us
    unnamed x30, local copies, waits for them, and re-layouts  7.67 us
  transfers between devices with their start and end apart: 19, of which 7 were waited for; matrix products, arithmetic and copies ran while one was open for 0% of the time, Pallas kernels for 1%

profile of v1, /device:TPU:449, one launch (start us, length us, event | category | flops | bytes accessed | tf_op | source)
XLA Modules:
  0.0 303.8 jit_solution(18425468627025966624)
XLA Ops:
  0.0 1.3 dynamic-slice_bitcast_fusion
  1.3 5.1 %collective-permute-start = (f32[2,32,8,256]{3,2,1,0:T(8,128)S(1)}, f32[2,32,8,256]{3,2,1,0:T(8,128)S(1)}, u32[]{:S(2)}, u32[]{:S(2)}) collective-permute-start(f32[2,32,8,256]{3,2,1,0:T(8,128)S(1)} %get-tuple-element.14), channel_id=1, source_target_pairs={{8,0},{16,8},{24,16},{32,24},{40,32},{48,40},{56,48},{64,56},{72,6... | collective-permute-start | bytes 1572872 | tf_op jit(solution)/shard_map/ppermute | solution.py:345
  6.4 10.6 %collective-permute-done.refs_0_ = f32[2,32,8,256]{3,2,1,0:T(8,128)S(1)} collective-permute-done((f32[2,32,8,256]{3,2,1,0:T(8,128)S(1)}, f32[2,32,8,256]{3,2,1,0:T(8,128)S(1)}, u32[]{:S(2)}, u32[]{:S(2)}) %collective-permute-start) | collective-permute-done | bytes 524320 | tf_op jit(solution)/shard_map/ppermute | solution.py:345
  17.0 6.2 %collective-permute-start.6 = (f32[2,32,8,256]{3,2,1,0:T(8,128)S(1)}, f32[2,32,8,256]{3,2,1,0:T(8,128)S(1)}, u32[]{:S(2)}, u32[]{:S(2)}) collective-permute-start(f32[2,32,8,256]{3,2,1,0:T(8,128)S(1)} %get-tuple-element.10), channel_id=1, source_target_pairs={{8,0},{16,8},{24,16},{32,24},{40,32},{48,40},{56,48},{64,56},{72,6... | collective-permute-start | bytes 1572872 | tf_op jit(solution)/shard_map/ppermute | solution.py:345
  23.2 4.4 %collective-permute-start.4 = (f32[2,32,8,256]{3,2,1,0:T(8,128)S(1)}, f32[2,32,8,256]{3,2,1,0:T(8,128)S(1)}, u32[]{:S(2)}, u32[]{:S(2)}) collective-permute-start(f32[2,32,8,256]{3,2,1,0:T(8,128)S(1)} %collective-permute-done.refs_0_), channel_id=1, source_target_pairs={{0,6},{1,7},{2,0},{3,1},{4,2},{5,3},{6,4},{7,5},{8,14},{9,15},{10,... | collective-permute-start | bytes 1572872 | tf_op jit(solution)/shard_map/ppermute | solution.py:350
  27.6 1.9 collective-permute-start.2
  29.5 4.0 %collective-permute-start.1 = (f32[2,32,8,256]{3,2,1,0:T(8,128)S(1)}, f32[2,32,8,256]{3,2,1,0:T(8,128)S(1)}, u32[]{:S(2)}, u32[]{:S(2)}) collective-permute-start(f32[2,32,8,256]{3,2,1,0:T(8,128)S(1)} %collective-permute-done.refs_0_), channel_id=1, source_target_pairs={{0,1},{1,0},{2,3},{3,2},{4,5},{5,4},{6,7},{7,6},{8,9},{9,8},{10,11... | collective-permute-start | bytes 1572872 | tf_op jit(solution)/shard_map/ppermute | solution.py:354
  33.5 0.0 collective-permute-done.6.refs_6_
  33.5 3.7 %collective-permute-start.7 = (f32[2,32,8,256]{3,2,1,0:T(8,128)S(1)}, f32[2,32,8,256]{3,2,1,0:T(8,128)S(1)}, u32[]{:S(2)}, u32[]{:S(2)}) collective-permute-start(f32[2,32,8,256]{3,2,1,0:T(8,128)S(1)} %collective-permute-done.6.refs_6_), channel_id=1, source_target_pairs={{0,1},{1,0},{2,3},{3,2},{4,5},{5,4},{6,7},{7,6},{8,9},{9,8},{10,11... | collective-permute-start | bytes 1572872 | tf_op jit(solution)/shard_map/ppermute | solution.py:354
  37.2 0.0 collective-permute-done.4.refs_4_
  37.2 4.4 %collective-permute-start.5 = (f32[2,32,8,256]{3,2,1,0:T(8,128)S(1)}, f32[2,32,8,256]{3,2,1,0:T(8,128)S(1)}, u32[]{:S(2)}, u32[]{:S(2)}) collective-permute-start(f32[2,32,8,256]{3,2,1,0:T(8,128)S(1)} %collective-permute-done.4.refs_4_), channel_id=1, source_target_pairs={{0,1},{1,0},{2,3},{3,2},{4,5},{5,4},{6,7},{7,6},{8,9},{9,8},{10,11... | collective-permute-start | bytes 1572872 | tf_op jit(solution)/shard_map/ppermute | solution.py:354
  41.6 0.4 collective-permute-done.2.refs_2_
  42.0 4.9 %collective-permute-start.3 = (f32[2,32,8,256]{3,2,1,0:T(8,128)S(1)}, f32[2,32,8,256]{3,2,1,0:T(8,128)S(1)}, u32[]{:S(2)}, u32[]{:S(2)}) collective-permute-start(f32[2,32,8,256]{3,2,1,0:T(8,128)S(1)} %collective-permute-done.2.refs_2_), channel_id=1, source_target_pairs={{0,1},{1,0},{2,3},{3,2},{4,5},{5,4},{6,7},{7,6},{8,9},{9,8},{10,11... | collective-permute-start | bytes 1572872 | tf_op jit(solution)/shard_map/ppermute | solution.py:354
  47.6 0.0 collective-permute-done.1.refs_1_
  47.6 0.0 collective-permute-done.7.refs_7_
  47.6 0.8 collective-permute-done.3.refs_3_
  48.4 1.0 copy-done
  49.5 2.2 copy-done.1
  51.7 1.1 copy-done.2
  52.8 0.7 copy-done.3
  53.5 0.7 copy-done.4
  54.1 1.1 copy-done.5
  55.2 6.9 %patterns.1 = f32[8,392,256]{2,1,0:T(8,128)S(1)} custom-call(s32[1]{0:T(128)} %bitcast.group_ref, s32[6]{0:T(128)S(1)} %copy-done.3, s32[6]{0:T(128)S(1)} %copy-done.4, s32[1]{0:T(128)S(6)} %copy.12.count_ref, f32[2,2048,256]{2,1,0:T(8,128)S(1)} %copy-done.1, f32[2,256,256]{2,1,0:T(8,128)S(1)} %copy-done, bf16[6,256,256]{2,1,0:T(8,128)(2,1)S(1)} %copy-done.2, ...), custom_call_target="tpu_custom_call" | custom-call | flops 7247757312 | bytes 12582912 | tf_op jit(solution)/shard_map/patterns/pallas_call | solution.py:180
  62.1 51.3 %all_to_all.5.got_ref = f32[8,392,256]{2,1,0:T(8,128)S(1)} all-to-all(f32[8,392,256]{2,1,0:T(8,128)S(1)} %patterns.1), channel_id=1, replica_groups=mesh['tile'=64,'group'=8] {'group'}, dimensions={0} | all-to-all | bytes 6422528 | tf_op jit(solution)/shard_map/all_to_all | solution.py:378
  113.5 1.7 gathered.1
  115.2 1.9 collective-permute-start.8
  117.1 1.9 collective-permute-start.9
  119.0 12.9 %collective-permute-done.9.before_ref = s32[8,13]{1,0:T(8,128)S(1)} collective-permute-done((s32[8,13]{1,0:T(8,128)S(1)}, s32[8,13]{1,0:T(8,128)S(1)}, u32[]{:S(2)}, u32[]{:S(2)}) %collective-permute-start.9) | collective-permute-done | bytes 448 | tf_op jit(solution)/shard_map/ppermute | solution.py:345
  132.0 3.9 %illumination.1 = f32[256,256]{1,0:T(8,128)S(1)} custom-call(s32[1]{0:T(128)} %bitcast.group_ref, s32[8,13]{1,0:T(8,128)S(1)} %bitcast.21, s32[8,13]{1,0:T(8,128)S(1)} %collective-permute-done.9.before_ref, f32[2,256,256]{2,1,0:T(8,128)S(1)} %copy-done), custom_call_target="tpu_custom_call" | custom-call | flops 4194304 | bytes 8388608 | tf_op jit(solution)/shard_map/illumination/pallas_call | solution.py:299
  135.9 0.0 collective-permute-done.8
  135.9 0.1 bitcast_add_fusion.refs_0_
  136.0 2.8 collective-permute-start.13
  138.8 2.5 collective-permute-start.11
  141.3 4.1 %collective-permute-start.10 = (f32[2,32,8,256]{3,2,1,0:T(8,128)S(1)}, f32[2,32,8,256]{3,2,1,0:T(8,128)S(1)}, u32[]{:S(2)}, u32[]{:S(2)}) collective-permute-start(f32[2,32,8,256]{3,2,1,0:T(8,128)S(1)} %bitcast_add_fusion.refs_0_), channel_id=1, source_target_pairs={{0,1},{1,0},{2,3},{3,2},{4,5},{5,4},{6,7},{7,6},{8,9},{9,8},{10,11... | collective-permute-start | bytes 1572872 | tf_op jit(solution)/shard_map/ppermute | solution.py:354
  145.4 4.3 %collective-permute-done.13.refs_4_ = f32[2,32,8,256]{3,2,1,0:T(8,128)S(1)} collective-permute-done((f32[2,32,8,256]{3,2,1,0:T(8,128)S(1)}, f32[2,32,8,256]{3,2,1,0:T(8,128)S(1)}, u32[]{:S(2)}, u32[]{:S(2)}) %collective-permute-start.13) | collective-permute-done | bytes 524320 | tf_op jit(solution)/shard_map/ppermute | solution.py:350
  149.7 4.0 %collective-permute-start.17 = (f32[32,8,256]{2,1,0:T(8,128)S(1)}, f32[32,8,256]{2,1,0:T(8,128)S(1)}, u32[]{:S(2)}, u32[]{:S(2)}) collective-permute-start(f32[32,8,256]{2,1,0:T(8,128)S(1)} %slice_bitcast_fusion), channel_id=1, source_target_pairs={{0,6},{1,7},{2,0},{3,1},{4,2},{5,3},{6,4},{7,5},{8,14},{9,15},{10,... | collective-permute-start | bytes 786440 | tf_op jit(solution)/shard_map/ppermute | solution.py:350
  153.7 4.7 %collective-permute-start.14 = (f32[2,32,8,256]{3,2,1,0:T(8,128)S(1)}, f32[2,32,8,256]{3,2,1,0:T(8,128)S(1)}, u32[]{:S(2)}, u32[]{:S(2)}) collective-permute-start(f32[2,32,8,256]{3,2,1,0:T(8,128)S(1)} %collective-permute-done.13.refs_4_), channel_id=1, source_target_pairs={{0,1},{1,0},{2,3},{3,2},{4,5},{5,4},{6,7},{7,6},{8,9},{9,8},{10,11... | collective-permute-start | bytes 1572872 | tf_op jit(solution)/shard_map/ppermute | solution.py:354
  158.5 0.0 collective-permute-done.11.refs_2_
  158.5 1.9 collective-permute-start.12
  160.5 1.9 collective-permute-start.15
  162.4 2.4 collective-permute-start.18
  164.8 6.1 %collective-permute-done.15.refs_6_ = f32[32,8,256]{2,1,0:T(8,128)S(1)} collective-permute-done((f32[32,8,256]{2,1,0:T(8,128)S(1)}, f32[32,8,256]{2,1,0:T(8,128)S(1)}, u32[]{:S(2)}, u32[]{:S(2)}) %collective-permute-start.15) | collective-permute-done | bytes 262176 | tf_op jit(solution)/shard_map/ppermute | solution.py:350
  170.9 3.2 %collective-permute-start.16 = (f32[32,8,256]{2,1,0:T(8,128)S(1)}, f32[32,8,256]{2,1,0:T(8,128)}, u32[]{:S(2)}, u32[]{:S(2)}) collective-permute-start(f32[32,8,256]{2,1,0:T(8,128)S(1)} %collective-permute-done.15.refs_6_), channel_id=1, source_target_pairs={{0,1},{1,0},{2,3},{3,2},{4,5},{5,4},{6,7},{7,6},{8,9},{9,8},{10,11... | collective-permute-start | bytes 786440 | tf_op jit(solution)/shard_map/ppermute | solution.py:354
  174.2 0.0 collective-permute-done.14.refs_5_
  174.3 0.8 copy-done.14
  175.1 0.4 collective-permute-done.16.refs_7_
  175.5 0.0 copy-done.11
  175.5 128.2 %assembled.1 = f32[2,32,8,8,256]{4,3,2,1,0:T(8,128)} custom-call(s32[1]{0:T(128)} %bitcast.group_ref, f32[2,32,8,256]{3,2,1,0:T(8,128)} %copy-done.6, f32[2,32,8,256]{3,2,1,0:T(8,128)} %copy-done.9, f32[2,32,8,256]{3,2,1,0:T(8,128)} %copy-done.8, f32[2,32,8,256]{3,2,1,0:T(8,128)} %copy-done.11, f32[2,32,8,256]{3,2,1,0:T(8,128)} %copy-done.7, ...), custom_call_target="tpu_custom_call" | custom-call | bytes 8388608 | tf_op jit(solution)/shard_map/assembled/pallas_call | solution.py:331
  (30 shorter events, 0.1 us)
Async XLA Ops:
  1.3 15.7 %collective-permute-start = (f32[2,32,8,256]{3,2,1,0:T(8,128)S(1)}, f32[2,32,8,256]{3,2,1,0:T(8,128)S(1)}, u32[]{:S(2)}, u32[]{:S(2)}) collective-permute-start(f32[2,32,8,256]{3,2,1,0:T(8,128)S(1)} %get-tuple-element.14), channel_id=1, source_target_pairs={{8,0},{16,8},{24,16},{32,24},{40,32},{48,40},{56,48},{64,56},{72,6... | collective-permute-start | bytes 1572872 | tf_op jit(solution)/shard_map/ppermute | solution.py:345
  17.0 16.6 %collective-permute-start.6 = (f32[2,32,8,256]{3,2,1,0:T(8,128)S(1)}, f32[2,32,8,256]{3,2,1,0:T(8,128)S(1)}, u32[]{:S(2)}, u32[]{:S(2)}) collective-permute-start(f32[2,32,8,256]{3,2,1,0:T(8,128)S(1)} %get-tuple-element.10), channel_id=1, source_target_pairs={{8,0},{16,8},{24,16},{32,24},{40,32},{48,40},{56,48},{64,56},{72,6... | collective-permute-start | bytes 1572872 | tf_op jit(solution)/shard_map/ppermute | solution.py:345
  23.2 14.0 %collective-permute-start.4 = (f32[2,32,8,256]{3,2,1,0:T(8,128)S(1)}, f32[2,32,8,256]{3,2,1,0:T(8,128)S(1)}, u32[]{:S(2)}, u32[]{:S(2)}) collective-permute-start(f32[2,32,8,256]{3,2,1,0:T(8,128)S(1)} %collective-permute-done.refs_0_), channel_id=1, source_target_pairs={{0,6},{1,7},{2,0},{3,1},{4,2},{5,3},{6,4},{7,5},{8,14},{9,15},{10,... | collective-permute-start | bytes 1572872 | tf_op jit(solution)/shard_map/ppermute | solution.py:350
  27.6 14.4 %collective-permute-start.2 = (f32[2,32,8,256]{3,2,1,0:T(8,128)S(1)}, f32[2,32,8,256]{3,2,1,0:T(8,128)S(1)}, u32[]{:S(2)}, u32[]{:S(2)}) collective-permute-start(f32[2,32,8,256]{3,2,1,0:T(8,128)S(1)} %collective-permute-done.refs_0_), channel_id=1, source_target_pairs={{0,2},{1,3},{2,4},{3,5},{4,6},{5,7},{6,0},{7,1},{8,10},{9,11},{10,... | collective-permute-start | bytes 1572872 | tf_op jit(solution)/shard_map/ppermute | solution.py:350
  29.5 18.1 %collective-permute-start.1 = (f32[2,32,8,256]{3,2,1,0:T(8,128)S(1)}, f32[2,32,8,256]{3,2,1,0:T(8,128)S(1)}, u32[]{:S(2)}, u32[]{:S(2)}) collective-permute-start(f32[2,32,8,256]{3,2,1,0:T(8,128)S(1)} %collective-permute-done.refs_0_), channel_id=1, source_target_pairs={{0,1},{1,0},{2,3},{3,2},{4,5},{5,4},{6,7},{7,6},{8,9},{9,8},{10,11... | collective-permute-start | bytes 1572872 | tf_op jit(solution)/shard_map/ppermute | solution.py:354
  33.5 14.0 %collective-permute-start.7 = (f32[2,32,8,256]{3,2,1,0:T(8,128)S(1)}, f32[2,32,8,256]{3,2,1,0:T(8,128)S(1)}, u32[]{:S(2)}, u32[]{:S(2)}) collective-permute-start(f32[2,32,8,256]{3,2,1,0:T(8,128)S(1)} %collective-permute-done.6.refs_6_), channel_id=1, source_target_pairs={{0,1},{1,0},{2,3},{3,2},{4,5},{5,4},{6,7},{7,6},{8,9},{9,8},{10,11... | collective-permute-start | bytes 1572872 | tf_op jit(solution)/shard_map/ppermute | solution.py:354
  37.2 10.4 %collective-permute-start.5 = (f32[2,32,8,256]{3,2,1,0:T(8,128)S(1)}, f32[2,32,8,256]{3,2,1,0:T(8,128)S(1)}, u32[]{:S(2)}, u32[]{:S(2)}) collective-permute-start(f32[2,32,8,256]{3,2,1,0:T(8,128)S(1)} %collective-permute-done.4.refs_4_), channel_id=1, source_target_pairs={{0,1},{1,0},{2,3},{3,2},{4,5},{5,4},{6,7},{7,6},{8,9},{9,8},{10,11... | collective-permute-start | bytes 1572872 | tf_op jit(solution)/shard_map/ppermute | solution.py:354
  42.0 6.4 %collective-permute-start.3 = (f32[2,32,8,256]{3,2,1,0:T(8,128)S(1)}, f32[2,32,8,256]{3,2,1,0:T(8,128)S(1)}, u32[]{:S(2)}, u32[]{:S(2)}) collective-permute-start(f32[2,32,8,256]{3,2,1,0:T(8,128)S(1)} %collective-permute-done.2.refs_2_), channel_id=1, source_target_pairs={{0,1},{1,0},{2,3},{3,2},{4,5},{5,4},{6,7},{7,6},{8,9},{9,8},{10,11... | collective-permute-start | bytes 1572872 | tf_op jit(solution)/shard_map/ppermute | solution.py:354
  48.4 1.0 copy-start
  49.5 2.2 copy-start.1
  51.7 1.1 copy-start.2
  52.8 0.7 copy-start.3
  53.4 0.7 copy-start.4
  54.1 1.1 copy-start.5
  115.2 20.7 %collective-permute-start.8 = (f32[2,256,256]{2,1,0:T(8,128)S(1)}, f32[2,256,256]{2,1,0:T(8,128)S(1)}, u32[]{:S(2)}, u32[]{:S(2)}) collective-permute-start(f32[2,256,256]{2,1,0:T(8,128)S(1)} %get-tuple-element.12), channel_id=1, source_target_pairs={{0,8},{8,16},{16,24},{24,32},{32,40},{40,48},{48,56},{56,64},{64,7... | collective-permute-start | bytes 1572872 | tf_op jit(solution)/shard_map/ppermute | solution.py:345
  117.1 14.9 %collective-permute-start.9 = (s32[8,13]{1,0:T(8,128)S(1)}, s32[8,13]{1,0:T(8,128)S(1)}, u32[]{:S(2)}, u32[]{:S(2)}) collective-permute-start(s32[8,13]{1,0:T(8,128)S(1)} %bitcast.20), channel_id=1, source_target_pairs={{0,8},{8,16},{16,24},{24,32},{32,40},{40,48},{48,56},{56,64},{64,7... | collective-permute-start | bytes 1256 | tf_op jit(solution)/shard_map/ppermute | solution.py:345
  136.0 39.5 %copy-start.6 = (f32[2,32,8,256]{3,2,1,0:T(8,128)}, f32[2,32,8,256]{3,2,1,0:T(8,128)S(1)}, u32[]{:S(2)}) copy-start(f32[2,32,8,256]{3,2,1,0:T(8,128)S(1)} %bitcast_add_fusion.refs_0_) | copy-start | bytes 1572868
  136.0 13.7 %collective-permute-start.13 = (f32[2,32,8,256]{3,2,1,0:T(8,128)S(1)}, f32[2,32,8,256]{3,2,1,0:T(8,128)S(1)}, u32[]{:S(2)}, u32[]{:S(2)}) collective-permute-start(f32[2,32,8,256]{3,2,1,0:T(8,128)S(1)} %bitcast_add_fusion.refs_0_), channel_id=1, source_target_pairs={{0,6},{1,7},{2,0},{3,1},{4,2},{5,3},{6,4},{7,5},{8,14},{9,15},{10,... | collective-permute-start | bytes 1572872 | tf_op jit(solution)/shard_map/ppermute | solution.py:350
  138.8 19.7 %collective-permute-start.11 = (f32[2,32,8,256]{3,2,1,0:T(8,128)S(1)}, f32[2,32,8,256]{3,2,1,0:T(8,128)S(1)}, u32[]{:S(2)}, u32[]{:S(2)}) collective-permute-start(f32[2,32,8,256]{3,2,1,0:T(8,128)S(1)} %bitcast_add_fusion.refs_0_), channel_id=1, source_target_pairs={{0,2},{1,3},{2,4},{3,5},{4,6},{5,7},{6,0},{7,1},{8,10},{9,11},{10,... | collective-permute-start | bytes 1572872 | tf_op jit(solution)/shard_map/ppermute | solution.py:350
  141.3 32.9 %collective-permute-start.10 = (f32[2,32,8,256]{3,2,1,0:T(8,128)S(1)}, f32[2,32,8,256]{3,2,1,0:T(8,128)S(1)}, u32[]{:S(2)}, u32[]{:S(2)}) collective-permute-start(f32[2,32,8,256]{3,2,1,0:T(8,128)S(1)} %bitcast_add_fusion.refs_0_), channel_id=1, source_target_pairs={{0,1},{1,0},{2,3},{3,2},{4,5},{5,4},{6,7},{7,6},{8,9},{9,8},{10,11... | collective-permute-start | bytes 1572872 | tf_op jit(solution)/shard_map/ppermute | solution.py:354
  149.7 25.8 %copy-start.7 = (f32[2,32,8,256]{3,2,1,0:T(8,128)}, f32[2,32,8,256]{3,2,1,0:T(8,128)S(1)}, u32[]{:S(2)}) copy-start(f32[2,32,8,256]{3,2,1,0:T(8,128)S(1)} %collective-permute-done.13.refs_4_) | copy-start | bytes 1572868
  149.7 12.7 %collective-permute-start.17 = (f32[32,8,256]{2,1,0:T(8,128)S(1)}, f32[32,8,256]{2,1,0:T(8,128)S(1)}, u32[]{:S(2)}, u32[]{:S(2)}) collective-permute-start(f32[32,8,256]{2,1,0:T(8,128)S(1)} %slice_bitcast_fusion), channel_id=1, source_target_pairs={{0,6},{1,7},{2,0},{3,1},{4,2},{5,3},{6,4},{7,5},{8,14},{9,15},{10,... | collective-permute-start | bytes 786440 | tf_op jit(solution)/shard_map/ppermute | solution.py:350
  153.7 20.5 %collective-permute-start.14 = (f32[2,32,8,256]{3,2,1,0:T(8,128)S(1)}, f32[2,32,8,256]{3,2,1,0:T(8,128)S(1)}, u32[]{:S(2)}, u32[]{:S(2)}) collective-permute-start(f32[2,32,8,256]{3,2,1,0:T(8,128)S(1)} %collective-permute-done.13.refs_4_), channel_id=1, source_target_pairs={{0,1},{1,0},{2,3},{3,2},{4,5},{5,4},{6,7},{7,6},{8,9},{9,8},{10,11... | collective-permute-start | bytes 1572872 | tf_op jit(solution)/shard_map/ppermute | solution.py:354
  158.5 17.0 %copy-start.8 = (f32[2,32,8,256]{3,2,1,0:T(8,128)}, f32[2,32,8,256]{3,2,1,0:T(8,128)S(1)}, u32[]{:S(2)}) copy-start(f32[2,32,8,256]{3,2,1,0:T(8,128)S(1)} %collective-permute-done.11.refs_2_) | copy-start | bytes 1572868
  158.5 15.7 %collective-permute-start.12 = (f32[2,32,8,256]{3,2,1,0:T(8,128)S(1)}, f32[2,32,8,256]{3,2,1,0:T(8,128)S(1)}, u32[]{:S(2)}, u32[]{:S(2)}) collective-permute-start(f32[2,32,8,256]{3,2,1,0:T(8,128)S(1)} %collective-permute-done.11.refs_2_), channel_id=1, source_target_pairs={{0,1},{1,0},{2,3},{3,2},{4,5},{5,4},{6,7},{7,6},{8,9},{9,8},{10,11... | collective-permute-start | bytes 1572872 | tf_op jit(solution)/shard_map/ppermute | solution.py:354
  160.5 10.5 %collective-permute-start.15 = (f32[32,8,256]{2,1,0:T(8,128)S(1)}, f32[32,8,256]{2,1,0:T(8,128)S(1)}, u32[]{:S(2)}, u32[]{:S(2)}) collective-permute-start(f32[32,8,256]{2,1,0:T(8,128)S(1)} %slice_bitcast_fusion.1), channel_id=1, source_target_pairs={{0,2},{1,3},{2,4},{3,5},{4,6},{5,7},{6,0},{7,1},{8,10},{9,11},{10,... | collective-permute-start | bytes 786440 | tf_op jit(solution)/shard_map/ppermute | solution.py:350
  162.4 13.1 %copy-start.12 = (f32[32,8,256]{2,1,0:T(8,128)}, f32[32,8,256]{2,1,0:T(8,128)S(1)}, u32[]{:S(2)}) copy-start(f32[32,8,256]{2,1,0:T(8,128)S(1)} %collective-permute-done.17.refs_8_) | copy-start | bytes 786436
  162.4 11.8 %collective-permute-start.18 = (f32[32,8,256]{2,1,0:T(8,128)S(1)}, f32[32,8,256]{2,1,0:T(8,128)S(1)}, u32[]{:S(2)}, u32[]{:S(2)}) collective-permute-start(f32[32,8,256]{2,1,0:T(8,128)S(1)} %collective-permute-done.17.refs_8_), channel_id=1, source_target_pairs={{0,1},{1,0},{2,3},{3,2},{4,5},{5,4},{6,7},{7,6},{8,9},{9,8},{10,11... | collective-permute-start | bytes 786440 | tf_op jit(solution)/shard_map/ppermute | solution.py:354
  170.9 3.3 %copy-start.13 = (f32[32,8,256]{2,1,0:T(8,128)}, f32[32,8,256]{2,1,0:T(8,128)S(1)}, u32[]{:S(2)}) copy-start(f32[32,8,256]{2,1,0:T(8,128)S(1)} %collective-permute-done.15.refs_6_) | copy-start | bytes 786436
  170.9 4.5 %collective-permute-start.16 = (f32[32,8,256]{2,1,0:T(8,128)S(1)}, f32[32,8,256]{2,1,0:T(8,128)}, u32[]{:S(2)}, u32[]{:S(2)}) collective-permute-start(f32[32,8,256]{2,1,0:T(8,128)S(1)} %collective-permute-done.15.refs_6_), channel_id=1, source_target_pairs={{0,1},{1,0},{2,3},{3,2},{4,5},{5,4},{6,7},{7,6},{8,9},{9,8},{10,11... | collective-permute-start | bytes 786440 | tf_op jit(solution)/shard_map/ppermute | solution.py:354
  174.2 1.3 copy-start.9
  174.2 1.3 copy-start.10
  174.2 1.3 copy-start.11
  174.3 0.8 copy-start.14

commit v2 on v1

--- a/solution.py
+++ b/solution.py
@@ -67,15 +67,14 @@
     return index ^ 1 if other else index
 
 
-def patterns_kernel(size, rows, parts, slots, group_ref, row_ref, col_ref, count_ref, own_ref, probe_hbm, amp_hbm, tab_hbm, *refs):
-    pieces, refs = refs[:parts], refs[parts:]
-    out_ref, own_buf, rim_buf, probe_ref, amp_ref, tab_ref, stage, own_sems, fixed_sems, piece_sems, store_sems = refs
-    group, count = group_ref[0], count_ref[0]
+def patterns_kernel(size, rows, parts, slots, notes_ref, own_ref, probe_hbm, amp_hbm, tab_hbm, held_ref, swapped_ref, out_ref,
+                    own_buf, rim_buf, probe_ref, amp_ref, tab_ref, stage, own_sems, fixed_sems, piece_sems, store_sems):
+    count, group = notes_ref[0, 2 * slots], notes_ref[2, 0]
     span = size + SUB
     depth = size // parts
 
     def start_of(p):
-        return pl.multiple_of(row_ref[p] & -SUB, SUB)
+        return pl.multiple_of(notes_ref[0, p] & -SUB, SUB)
 
     def first_of(p):
         return pl.multiple_of(jnp.minimum(start_of(p), rows - span), SUB)
@@ -93,9 +92,10 @@
         for n, (a, b) in enumerate(((probe_hbm, probe_ref), (tab_hbm, tab_ref), (amp_hbm, amp_ref)))
     ]
     rims = []
-    for n, piece in enumerate(pieces):
-        index = class_of(group, STEPS[n // 2], n % 2, parts)
-        rims.append(pltpu.make_async_copy(piece, rim_buf.at[:, :, index], piece_sems.at[n]))
+    for other, ref in enumerate((held_ref, swapped_ref)):
+        for n, step in enumerate(STEPS):
+            index = class_of(group, step, other, parts)
+            rims.append(pltpu.make_async_copy(ref.at[n], rim_buf.at[:, :, index], piece_sems.at[len(rims)]))
     load(0).start()
     for copy in rims + fixed:
         copy.start()
@@ -103,10 +103,10 @@
     lane = lax.broadcasted_iota(jnp.int32, (SUB, size), 1)
     head_row = lax.broadcasted_iota(jnp.int32, (SUB, size), 0)
     column = lax.broadcasted_iota(jnp.int32, (size, size), 1)
-    note = jnp.where(lane == 2 * slots, count, 0)
-    for p in range(slots):
-        note = jnp.where(lane == p, row_ref[p], note)
-        note = jnp.where(lane == slots + p, col_ref[p], note)
+    note = jnp.zeros((SUB, size), jnp.int32)
+    for side in range(2):
+        for n in range(2 * slots + 1):
+            note = jnp.where(jnp.logical_and(head_row == side, lane == n), notes_ref[side, n], note)
     note = note.astype(jnp.float32)
     for part in range(parts):
         stage[part, slots * 2 * depth :] = note
@@ -119,7 +119,7 @@
 
     def pattern(p, _):
         slot = lax.rem(p, 2)
-        row, col = row_ref[p], col_ref[p]
+        row, col = notes_ref[0, p], notes_ref[0, slots + p]
         base = start_of(p)
         shift = row - base
 
@@ -169,19 +169,20 @@
     lax.fori_loop(0, count, stored, 0)
 
 
-def patterns(group, own, pieces, probe, amplitudes, row, col, count):
+def patterns(notes, own, held, swapped, probe, amplitudes):
     rows, size = own.shape[1:]
-    slots, parts = amplitudes.shape[0], len(pieces)
+    slots, parts = amplitudes.shape[0], 2 * held.shape[0]
     depth = size // parts
     length = slots * 2 * depth + SUB
     smem = pl.BlockSpec(memory_space=pltpu.SMEM)
-    hbm = pl.BlockSpec(memory_space=pl.ANY)
+    anywhere = pl.BlockSpec(memory_space=pl.ANY)
+    hbm = pl.BlockSpec(memory_space=pltpu.HBM)
     tab = jnp.asarray(tables(size))
     return pl.pallas_call(
         functools.partial(patterns_kernel, size, rows, parts, slots),
         out_shape=jax.ShapeDtypeStruct((parts, length, size), jnp.float32),
-        in_specs=[smem] * 4 + [hbm] * (4 + parts),
-        out_specs=hbm,
+        in_specs=[smem] + [hbm] * 4 + [anywhere] * 2,
+        out_specs=anywhere,
         scratch_shapes=[
             pltpu.VMEM((2, 2, size + SUB, size), jnp.float32),
             pltpu.VMEM((2, rows // (SUB * parts), parts, SUB, size), jnp.float32),
@@ -197,7 +198,7 @@
         compiler_params=pltpu.CompilerParams(vmem_limit_bytes=40 * MIB),
         cost_estimate=pl.CostEstimate(flops=36 * 2 * size**3 * slots, bytes_accessed=12 * MIB, transcendentals=0),
         name="patterns",
-    )(group, row, col, count, own, probe, amplitudes, tab, *pieces)
+    )(notes, own, probe, amplitudes, tab, held, swapped)
 
 
 def place(row, group, parts):
@@ -218,7 +219,7 @@
     lax.fori_loop(0, notes_ref.shape[0], device, 0)
 
 
-def gather_kernel(size, parts, slots, group_ref, notes_ref, got_ref, here_ref, next_ref, total):
+def gather_kernel(size, parts, slots, group_ref, notes_ref, got_ref, here_ref, next_re_ref, next_im_ref, total):
     depth = size // parts
     group = group_ref[0]
     total[...] = jnp.zeros_like(total)
@@ -240,19 +241,21 @@
     each_live(notes_ref, slots, step)
     kept = here_ref.shape[1]
     here_ref[...] = total[0, :, :kept]
-    next_ref[...] = total[1, :, :kept]
+    next_re_ref[...] = total[1, 0, :kept]
+    next_im_ref[...] = total[1, 1, :kept]
 
 
 def gathered(group, notes, got, slots, kept):
     parts, length, size = got.shape
     smem = pl.BlockSpec(memory_space=pltpu.SMEM)
     vmem = pl.BlockSpec(memory_space=pltpu.VMEM)
-    shape = jax.ShapeDtypeStruct((2, kept, size), jnp.float32)
+    shape = jax.ShapeDtypeStruct((kept, size), jnp.float32)
+    both = jax.ShapeDtypeStruct((2, kept, size), jnp.float32)
     return pl.pallas_call(
         functools.partial(gather_kernel, size, parts, slots),
-        out_shape=(shape, shape),
+        out_shape=(both, shape, shape),
         in_specs=[smem, smem, vmem],
-        out_specs=(vmem, vmem),
+        out_specs=(vmem, vmem, vmem),
         scratch_shapes=[pltpu.VMEM((2, 2, kept + SUB, size), jnp.float32)],
         compiler_params=pltpu.CompilerParams(vmem_limit_bytes=24 * MIB),
         cost_estimate=pl.CostEstimate(flops=2**22, bytes_accessed=6 * MIB, transcendentals=0),
@@ -311,32 +314,33 @@
     )(group, here, before, probe)
 
 
-def assemble_kernel(parts, group_ref, *refs):
-    pieces, out_ref, sems = refs[:-2], refs[-2], refs[-1]
-    group = group_ref[0]
+def assemble_kernel(steps, parts, group_ref, held_ref, swapped_ref, *refs):
+    out_ref, sems = refs[-2:]
     copies = []
-    for n, piece in enumerate(pieces):
-        whole = n < 6
-        index = class_of(group, STEPS[n // 2] if whole else STEPS[3], n % 2, parts)
-        place = out_ref.at[:, :, index] if whole else out_ref.at[(n - 6) // 2, :, index]
-        copies.append(pltpu.make_async_copy(piece, place, sems.at[n]))
+    for other, ref in enumerate((held_ref, swapped_ref)):
+        for n, step in enumerate(steps):
+            index = class_of(group_ref[0], step, other, parts)
+            copies.append(pltpu.make_async_copy(ref.at[n], out_ref.at[n % 2, :, index], sems.at[len(copies)]))
     for copy in copies:
         copy.start()
     for copy in copies:
         copy.wait()
 
 
-def assembled(group, pieces, shape):
+def assembled(group, steps, held, swapped, shape, begun=()):
     parts = shape[2]
+    hbm = pl.BlockSpec(memory_space=pltpu.HBM)
+    vmem = pl.BlockSpec(memory_space=pltpu.VMEM)
     return pl.pallas_call(
-        functools.partial(assemble_kernel, parts),
+        functools.partial(assemble_kernel, steps, parts),
         out_shape=jax.ShapeDtypeStruct(shape, jnp.float32),
-        in_specs=[pl.BlockSpec(memory_space=pltpu.SMEM)] + [pl.BlockSpec(memory_space=pl.ANY)] * len(pieces),
-        out_specs=pl.BlockSpec(memory_space=pl.ANY),
-        scratch_shapes=[pltpu.SemaphoreType.DMA((len(pieces),))],
+        in_specs=[pl.BlockSpec(memory_space=pltpu.SMEM), vmem, vmem] + [hbm] * len(begun),
+        out_specs=hbm,
+        scratch_shapes=[pltpu.SemaphoreType.DMA((2 * len(steps),))],
+        input_output_aliases={3: 0} if begun else {},
         cost_estimate=pl.CostEstimate(flops=0, bytes_accessed=8 * MIB, transcendentals=0),
         name="assembled",
-    )(group, *pieces)
+    )(group, held, swapped, *begun)
 
 
 def passed_along(x, axis, by):
@@ -370,24 +374,26 @@
     near = passed_along(mine, "tile", -1)
     near, opposite = lax.optimization_barrier((near, share((index + 4) % parts)))
     opposite = passed_along(opposite, "tile", -1)
-    before, after = to_chip(near, 1), to_chip(near, -1)
-    pieces = []
-    for piece in (near, before, after, opposite):
-        pieces += [piece, to_core(piece)]
-    sent = patterns(group, object_field, pieces, probe, amplitudes, row_offset, col_offset, counts)
+    held = jnp.stack([near, to_chip(near, 1), to_chip(near, -1), opposite])
+    own_notes = jnp.concatenate([row_offset, col_offset, counts])
+    notes = jnp.stack([own_notes, passed_along(own_notes, "tile", 1), jnp.full_like(own_notes, index)])
+    sent = patterns(notes, object_field, held, to_core(held), probe, amplitudes)
     got = lax.all_to_all(sent, "group", 0, 0)
-    notes = got[:, slots * 2 * (size // parts), : 2 * slots + 1].astype(jnp.int32)
-    notes_before = passed_along(notes, "tile", 1)
-    here, spill = gathered(group, notes, got, slots, kept)
-    spill = passed_along(spill, "tile", 1)
-    weight = illumination(group, notes, notes_before, probe, slots, kept)
-    result = mine + ((here + spill) / weight).reshape(mine.shape)
-    before, after = to_chip(result, 1), to_chip(result, -1)
-    upper, lower = to_chip(before[0], 1), to_chip(after[1], -1)
-    pieces = []
-    for piece in (result, before, after, upper, lower):
-        pieces += [piece, to_core(piece)]
-    return assembled(group, pieces, blocks.shape).reshape(object_field.shape)
+    notes = got[:, slots * 2 * (size // parts) :, : 2 * slots + 1].astype(jnp.int32)
+    notes_here, notes_before = notes[:, 0], notes[:, 1]
+    here, *spills = gathered(group, notes_here, got, slots, kept)
+    weight = illumination(group, notes_here, notes_before, probe, slots, kept)
+    results, before, after = [], [], []
+    for ch, spill in enumerate(spills):
+        grad = here[ch] + passed_along(spill, "tile", 1)
+        results.append(mine[ch] + (grad / weight).reshape(mine.shape[1:]))
+        before.append(to_chip(results[ch], 1))
+        after.append(to_chip(results[ch], -1))
+    first = jnp.stack(results + before + after)
+    last = jnp.stack([to_chip(before[0], 1), to_chip(after[1], -1)])
+    field = assembled(group, (0, 0, -2, -2, 2, 2), first, to_core(first), blocks.shape)
+    field = assembled(group, (4, 4), last, to_core(last), blocks.shape, (field,))
+    return field.reshape(object_field.shape)
 
 
 def solution(mesh):

time: 306 us -> 181 us (0.59)
  the two profiles are of different devices: /device:TPU:449 before, /device:TPU:263 now
where the time goes in v2:
time: 181 us
  starting transfers between devices  54.7 us (30%)
  blocking collectives  54.7 us (30%)
  waiting for transfers between devices  48.9 us (27%)
  Pallas kernels  18.3 us (10%)
  local copies, waits for them, and re-layouts  2.48 us (1%)
    all_to_all x1, blocking collectives, body(): got = lax.all_to_all(sent, 'group', 0, 0)  54.7 us
    ppermute x5, waiting for transfers between devices, passed_along(): return lax.ppermute(x, axis, pairs)  29.1 us
    ppermute x8, starting transfers between devices, to_chip(): lax.ppermute(x, 'group', [(i, (i + 2 * by) % devices) for i in range(devi...  23.6 us
    ppermute x8, waiting for transfers between devices, to_chip(): lax.ppermute(x, 'group', [(i, (i + 2 * by) % devices) for i in range(devi...  19.8 us
    ppermute x5, starting transfers between devices, passed_along(): return lax.ppermute(x, axis, pairs)  17.5 us
    ppermute x3, starting transfers between devices, to_core(): lax.ppermute(x, 'group', [(i, i ^ 1) for i in range(lax.axis_size('group'...  13.6 us
    pallas_call x1, Pallas kernels, patterns(): pl.pallas_call(functools.partial(patterns_kernel, size, rows, parts, slot...  6.85 us
    pallas_call x2, Pallas kernels, assembled(): pl.pallas_call(functools.partial(assemble_kernel, steps, parts), out_shap...  5.83 us
  transfers between devices with their start and end apart: 16, of which 11 were waited for; matrix products, arithmetic and copies ran while one was open for 0% of the time, Pallas kernels for 4%

profile of v2, /device:TPU:263, one launch (start us, length us, event | category | flops | bytes accessed | tf_op | source)
XLA Modules:
  0.0 180.7 jit_solution(3729522571339327579)
XLA Ops:
  0.0 1.5 dynamic-slice_bitcast_fusion
  1.5 4.3 %collective-permute-start.1 = (f32[2,32,8,256]{3,2,1,0:T(8,128)S(1)}, f32[2,32,8,256]{3,2,1,0:T(8,128)S(1)}, u32[]{:S(2)}, u32[]{:S(2)}) collective-permute-start(f32[2,32,8,256]{3,2,1,0:T(8,128)S(1)} %get-tuple-element.16), channel_id=1, source_target_pairs={{8,0},{16,8},{24,16},{32,24},{40,32},{48,40},{56,48},{64,56},{72,6... | collective-permute-start | bytes 1572872 | tf_op jit(solution)/shard_map/ppermute | solution.py:349
  5.8 10.6 %collective-permute-done.1 = f32[2,32,8,256]{3,2,1,0:T(8,128)S(1)} collective-permute-done((f32[2,32,8,256]{3,2,1,0:T(8,128)S(1)}, f32[2,32,8,256]{3,2,1,0:T(8,128)S(1)}, u32[]{:S(2)}, u32[]{:S(2)}) %collective-permute-start.1) | collective-permute-done | bytes 524320 | tf_op jit(solution)/shard_map/ppermute | solution.py:349
  16.4 7.4 %collective-permute-start.4 = (f32[2,32,8,256]{3,2,1,0:T(8,128)S(1)}, f32[2,32,8,256]{3,2,1,0:T(8,128)S(1)}, u32[]{:S(2)}, u32[]{:S(2)}) collective-permute-start(f32[2,32,8,256]{3,2,1,0:T(8,128)S(1)} %get-tuple-element.11), channel_id=1, source_target_pairs={{8,0},{16,8},{24,16},{32,24},{40,32},{48,40},{56,48},{64,56},{72,6... | collective-permute-start | bytes 1572872 | tf_op jit(solution)/shard_map/ppermute | solution.py:349
  23.8 2.5 %collective-permute-start.3 = (f32[2,32,8,256]{3,2,1,0:T(8,128)S(1)}, f32[2,32,8,256]{3,2,1,0:T(8,128)S(1)}, u32[]{:S(2)}, u32[]{:S(2)}) collective-permute-start(f32[2,32,8,256]{3,2,1,0:T(8,128)S(1)} %collective-permute-done.1), channel_id=1, source_target_pairs={{0,6},{1,7},{2,0},{3,1},{4,2},{5,3},{6,4},{7,5},{8,14},{9,15},{10,... | collective-permute-start | bytes 1572872 | tf_op jit(solution)/shard_map/ppermute | solution.py:354
  26.3 4.0 %collective-permute-start.2 = (f32[2,32,8,256]{3,2,1,0:T(8,128)S(1)}, f32[2,32,8,256]{3,2,1,0:T(8,128)S(1)}, u32[]{:S(2)}, u32[]{:S(2)}) collective-permute-start(f32[2,32,8,256]{3,2,1,0:T(8,128)S(1)} %collective-permute-done.1), channel_id=1, source_target_pairs={{0,2},{1,3},{2,4},{3,5},{4,6},{5,7},{6,0},{7,1},{8,10},{9,11},{10,... | collective-permute-start | bytes 1572872 | tf_op jit(solution)/shard_map/ppermute | solution.py:354
  30.3 3.1 %collective-permute-done.4 = f32[2,32,8,256]{3,2,1,0:T(8,128)S(1)} collective-permute-done((f32[2,32,8,256]{3,2,1,0:T(8,128)S(1)}, f32[2,32,8,256]{3,2,1,0:T(8,128)S(1)}, u32[]{:S(2)}, u32[]{:S(2)}) %collective-permute-start.4) | collective-permute-done | bytes 524320 | tf_op jit(solution)/shard_map/ppermute | solution.py:349
  33.5 5.0 %collective-permute-done.3 = f32[2,32,8,256]{3,2,1,0:T(8,128)S(1)} collective-permute-done((f32[2,32,8,256]{3,2,1,0:T(8,128)S(1)}, f32[2,32,8,256]{3,2,1,0:T(8,128)S(1)}, u32[]{:S(2)}, u32[]{:S(2)}) %collective-permute-start.3) | collective-permute-done | bytes 524320 | tf_op jit(solution)/shard_map/ppermute | solution.py:354
  38.5 1.0 collective-permute-done.2
  39.5 0.0 copy-start.3
  39.5 0.1 pad_maximum_fusion.held_ref
  39.7 5.1 %collective-permute-start.5 = (f32[4,2,32,8,256]{4,3,2,1,0:T(8,128)S(1)}, f32[4,2,32,8,256]{4,3,2,1,0:T(8,128)S(1)}, u32[]{:S(2)}, u32[]{:S(2)}) collective-permute-start(f32[4,2,32,8,256]{4,3,2,1,0:T(8,128)S(1)} %pad_maximum_fusion.held_ref), channel_id=1, source_target_pairs={{0,1},{1,0},{2,3},{3,2},{4,5},{5,4},{6,7},{7,6},{8,9},{9,8},{10,11... | collective-permute-start | bytes 6291464 | tf_op jit(solution)/shard_map/ppermute | solution.py:358
  45.4 0.1 pad_add_fusion
  45.5 1.9 %collective-permute-start = (s32[13]{0:T(128)S(1)}, s32[13]{0:T(128)S(1)}, u32[]{:S(2)}, u32[]{:S(2)}) collective-permute-start(s32[13]{0:T(128)S(1)} %pad_add_fusion), channel_id=1, source_target_pairs={{0,8},{8,16},{16,24},{24,32},{32,40},{40,48},{48,56},{56,64},{64,7... | collective-permute-start | bytes 164 | tf_op jit(solution)/shard_map/ppermute | solution.py:349
  47.4 0.1 fusion.5
  47.5 0.1 pad.8.clone
  47.5 5.5 %collective-permute-done = s32[13]{0:T(128)S(1)} collective-permute-done((s32[13]{0:T(128)S(1)}, s32[13]{0:T(128)S(1)}, u32[]{:S(2)}, u32[]{:S(2)}) %collective-permute-start) | collective-permute-done | bytes 84 | tf_op jit(solution)/shard_map/ppermute | solution.py:349
  53.1 0.1 add_add_fusion.notes_ref
  53.1 0.0 collective-permute-done.5.swapped_ref
  53.2 6.8 %patterns.1 = f32[8,392,256]{2,1,0:T(8,128)S(1)} custom-call(s32[3,13]{1,0:T(4,128)S(1)} %add_add_fusion.notes_ref, f32[2,2048,256]{2,1,0:T(8,128)S(1)} %copy-done.1, f32[2,256,256]{2,1,0:T(8,128)S(1)} %copy-done, bf16[6,256,256]{2,1,0:T(8,128)(2,1)S(1)} %copy-done.2, bf16[6,256,256]{2,1,0:T(8,128)(2,1)S(1)} %copy-done.3, ...), custom_call_target="tpu_custom_call" | custom-call | flops 7247757312 | bytes 12582912 | tf_op jit(solution)/shard_map/patterns/pallas_call | solution.py:181
  60.0 54.7 %all_to_all.5.got_ref = f32[8,392,256]{2,1,0:T(8,128)S(1)} all-to-all(f32[8,392,256]{2,1,0:T(8,128)S(1)} %patterns.1), channel_id=1, replica_groups=mesh['tile'=64,'group'=8] {'group'}, dimensions={0} | all-to-all | bytes 6422528 | tf_op jit(solution)/shard_map/all_to_all | solution.py:381
  114.7 1.5 gathered.1
  116.2 1.9 %collective-permute-start.6 = (f32[256,256]{1,0:T(8,128)S(1)}, f32[256,256]{1,0:T(8,128)S(1)}, u32[]{:S(2)}, u32[]{:S(2)}) collective-permute-start(f32[256,256]{1,0:T(8,128)S(1)} %get-tuple-element.13), channel_id=1, source_target_pairs={{0,8},{8,16},{16,24},{24,32},{32,40},{40,48},{48,56},{56,64},{64,7... | collective-permute-start | bytes 786440 | tf_op jit(solution)/shard_map/ppermute | solution.py:349
  118.1 1.9 %collective-permute-start.9 = (f32[256,256]{1,0:T(8,128)S(1)}, f32[256,256]{1,0:T(8,128)S(1)}, u32[]{:S(2)}, u32[]{:S(2)}) collective-permute-start(f32[256,256]{1,0:T(8,128)S(1)} %get-tuple-element.14), channel_id=1, source_target_pairs={{0,8},{8,16},{16,24},{24,32},{32,40},{40,48},{48,56},{56,64},{64,7... | collective-permute-start | bytes 786440 | tf_op jit(solution)/shard_map/ppermute | solution.py:349
  120.1 4.2 %illumination.1 = f32[256,256]{1,0:T(8,128)S(1)} custom-call(s32[1]{0:T(128)} %bitcast.group_ref, s32[8,13]{1,0:T(8,128)S(1)} %bitcast.68, s32[8,13]{1,0:T(8,128)S(1)} %bitcast.69, f32[2,256,256]{2,1,0:T(8,128)S(1)} %copy-done), custom_call_target="tpu_custom_call" | custom-call | flops 4194304 | bytes 8388608 | tf_op jit(solution)/shard_map/illumination/pallas_call | solution.py:302
  124.2 4.3 %collective-permute-done.6 = f32[256,256]{1,0:T(8,128)S(1)} collective-permute-done((f32[256,256]{1,0:T(8,128)S(1)}, f32[256,256]{1,0:T(8,128)S(1)}, u32[]{:S(2)}, u32[]{:S(2)}) %collective-permute-start.6) | collective-permute-done | bytes 262176 | tf_op jit(solution)/shard_map/ppermute | solution.py:349
  128.5 5.6 %collective-permute-done.9 = f32[256,256]{1,0:T(8,128)S(1)} collective-permute-done((f32[256,256]{1,0:T(8,128)S(1)}, f32[256,256]{1,0:T(8,128)S(1)}, u32[]{:S(2)}, u32[]{:S(2)}) %collective-permute-start.9) | collective-permute-done | bytes 262176 | tf_op jit(solution)/shard_map/ppermute | solution.py:349
  134.1 0.1 bitcast_add_fusion.4
  134.3 2.0 %collective-permute-start.14 = (f32[32,8,256]{2,1,0:T(8,128)S(1)}, f32[32,8,256]{2,1,0:T(8,128)S(1)}, u32[]{:S(2)}, u32[]{:S(2)}) collective-permute-start(f32[32,8,256]{2,1,0:T(8,128)S(1)} %get-tuple-element.18), channel_id=1, source_target_pairs={{0,6},{1,7},{2,0},{3,1},{4,2},{5,3},{6,4},{7,5},{8,14},{9,15},{10,... | collective-permute-start | bytes 786440 | tf_op jit(solution)/shard_map/ppermute | solution.py:354
  136.2 4.5 %collective-permute-start.7 = (f32[32,8,256]{2,1,0:T(8,128)S(1)}, f32[32,8,256]{2,1,0:T(8,128)S(1)}, u32[]{:S(2)}, u32[]{:S(2)}) collective-permute-start(f32[32,8,256]{2,1,0:T(8,128)S(1)} %get-tuple-element.18), channel_id=1, source_target_pairs={{0,2},{1,3},{2,4},{3,5},{4,6},{5,7},{6,0},{7,1},{8,10},{9,11},{10,... | collective-permute-start | bytes 786440 | tf_op jit(solution)/shard_map/ppermute | solution.py:354
  140.8 2.5 %collective-permute-start.13 = (f32[32,8,256]{2,1,0:T(8,128)S(1)}, f32[32,8,256]{2,1,0:T(8,128)S(1)}, u32[]{:S(2)}, u32[]{:S(2)}) collective-permute-start(f32[32,8,256]{2,1,0:T(8,128)S(1)} %get-tuple-element.19), channel_id=1, source_target_pairs={{0,2},{1,3},{2,4},{3,5},{4,6},{5,7},{6,0},{7,1},{8,10},{9,11},{10,... | collective-permute-start | bytes 786440 | tf_op jit(solution)/shard_map/ppermute | solution.py:354
  143.3 2.8 %collective-permute-start.10 = (f32[32,8,256]{2,1,0:T(8,128)S(1)}, f32[32,8,256]{2,1,0:T(8,128)S(1)}, u32[]{:S(2)}, u32[]{:S(2)}) collective-permute-start(f32[32,8,256]{2,1,0:T(8,128)S(1)} %get-tuple-element.19), channel_id=1, source_target_pairs={{0,6},{1,7},{2,0},{3,1},{4,2},{5,3},{6,4},{7,5},{8,14},{9,15},{10,... | collective-permute-start | bytes 786440 | tf_op jit(solution)/shard_map/ppermute | solution.py:354
  146.1 0.1 fusion.1
  146.1 0.1 fusion
  146.2 0.0 collective-permute-done.7
  146.3 4.2 %collective-permute-done.13 = f32[32,8,256]{2,1,0:T(8,128)S(1)} collective-permute-done((f32[32,8,256]{2,1,0:T(8,128)S(1)}, f32[32,8,256]{2,1,0:T(8,128)S(1)}, u32[]{:S(2)}, u32[]{:S(2)}) %collective-permute-start.13) | collective-permute-done | bytes 262176 | tf_op jit(solution)/shard_map/ppermute | solution.py:354
  150.4 0.0 collective-permute-done.14
  150.5 1.1 collective-permute-done.10
  151.6 5.5 %collective-permute-start.15 = (f32[6,32,8,256]{3,2,1,0:T(8,128)S(1)}, f32[6,32,8,256]{3,2,1,0:T(8,128)}, u32[]{:S(2)}, u32[]{:S(2)}) collective-permute-start(f32[6,32,8,256]{3,2,1,0:T(8,128)S(1)} %bitcast_dynamic-update-slice_fusion.held_ref), channel_id=1, source_target_pairs={{0,1},{1,0},{2,3},{3,2},{4,5},{5,4},{6,7},{7,6},{8,9},{9,8},{10,11... | collective-permute-start | bytes 4718600 | tf_op jit(solution)/shard_map/ppermute | solution.py:358
  157.2 3.1 %collective-permute-start.8 = (f32[32,8,256]{2,1,0:T(8,128)S(1)}, f32[32,8,256]{2,1,0:T(8,128)S(1)}, u32[]{:S(2)}, u32[]{:S(2)}) collective-permute-start(f32[32,8,256]{2,1,0:T(8,128)S(1)} %collective-permute-done.7), channel_id=1, source_target_pairs={{0,2},{1,3},{2,4},{3,5},{4,6},{5,7},{6,0},{7,1},{8,10},{9,11},{10,... | collective-permute-start | bytes 786440 | tf_op jit(solution)/shard_map/ppermute | solution.py:354
  160.2 2.2 %collective-permute-start.11 = (f32[32,8,256]{2,1,0:T(8,128)S(1)}, f32[32,8,256]{2,1,0:T(8,128)S(1)}, u32[]{:S(2)}, u32[]{:S(2)}) collective-permute-start(f32[32,8,256]{2,1,0:T(8,128)S(1)} %collective-permute-done.10), channel_id=1, source_target_pairs={{0,6},{1,7},{2,0},{3,1},{4,2},{5,3},{6,4},{7,5},{8,14},{9,15},{10,... | collective-permute-start | bytes 786440 | tf_op jit(solution)/shard_map/ppermute | solution.py:354
  162.5 4.5 %collective-permute-done.8 = f32[32,8,256]{2,1,0:T(8,128)S(1)} collective-permute-done((f32[32,8,256]{2,1,0:T(8,128)S(1)}, f32[32,8,256]{2,1,0:T(8,128)S(1)}, u32[]{:S(2)}, u32[]{:S(2)}) %collective-permute-start.8) | collective-permute-done | bytes 262176 | tf_op jit(solution)/shard_map/ppermute | solution.py:354
  167.0 4.0 %collective-permute-done.11 = f32[32,8,256]{2,1,0:T(8,128)S(1)} collective-permute-done((f32[32,8,256]{2,1,0:T(8,128)S(1)}, f32[32,8,256]{2,1,0:T(8,128)S(1)}, u32[]{:S(2)}, u32[]{:S(2)}) %collective-permute-start.11) | collective-permute-done | bytes 262176 | tf_op jit(solution)/shard_map/ppermute | solution.py:354
  171.0 3.0 %collective-permute-start.12 = (f32[2,32,8,256]{3,2,1,0:T(8,128)S(1)}, f32[2,32,8,256]{3,2,1,0:T(8,128)S(1)}, u32[]{:S(2)}, u32[]{:S(2)}) collective-permute-start(f32[2,32,8,256]{3,2,1,0:T(8,128)S(1)} %pad_maximum_fusion.1.held_ref), channel_id=1, source_target_pairs={{0,1},{1,0},{2,3},{3,2},{4,5},{5,4},{6,7},{7,6},{8,9},{9,8},{10,11... | collective-permute-start | bytes 1572872 | tf_op jit(solution)/shard_map/ppermute | solution.py:358
  174.0 0.0 collective-permute-done.15.swapped_ref
  174.0 3.6 %assembled.2.refs_0_ = f32[2,32,8,8,256]{4,3,2,1,0:T(8,128)} custom-call(s32[1]{0:T(128)} %bitcast.group_ref, f32[6,32,8,256]{3,2,1,0:T(8,128)} %copy-done.4, f32[6,32,8,256]{3,2,1,0:T(8,128)} %collective-permute-done.15.swapped_ref), custom_call_target="tpu_custom_call" | custom-call | bytes 8388608 | tf_op jit(solution)/shard_map/assembled/pallas_call | solution.py:334
  177.7 0.8 copy-done.6
  178.5 2.2 %assembled.3 = f32[2,32,8,8,256]{4,3,2,1,0:T(8,128)} custom-call(s32[1]{0:T(128)} %bitcast.group_ref, f32[2,32,8,256]{3,2,1,0:T(8,128)} %copy-done.5, f32[2,32,8,256]{3,2,1,0:T(8,128)} %copy-done.6, f32[2,32,8,8,256]{4,3,2,1,0:T(8,128)} %assembled.2.refs_0_), custom_call_target="tpu_custom_call", output_to_operand_aliasing={{}: (3, {})} | custom-call | bytes 8388608 | tf_op jit(solution)/shard_map/assembled/pallas_call | solution.py:334
  (24 shorter events, 0.2 us)
Async XLA Ops:
  0.0 53.1 %copy-start.1 = (f32[2,2048,256]{2,1,0:T(8,128)S(1)}, f32[2,2048,256]{2,1,0:T(8,128)}, u32[]{:S(2)}) copy-start(f32[2,2048,256]{2,1,0:T(8,128)} %own_ref.1) | copy-start | bytes 12582916
  1.5 14.9 %collective-permute-start.1 = (f32[2,32,8,256]{3,2,1,0:T(8,128)S(1)}, f32[2,32,8,256]{3,2,1,0:T(8,128)S(1)}, u32[]{:S(2)}, u32[]{:S(2)}) collective-permute-start(f32[2,32,8,256]{3,2,1,0:T(8,128)S(1)} %get-tuple-element.16), channel_id=1, source_target_pairs={{8,0},{16,8},{24,16},{32,24},{40,32},{48,40},{56,48},{64,56},{72,6... | collective-permute-start | bytes 1572872 | tf_op jit(solution)/shard_map/ppermute | solution.py:349
  16.4 17.1 %collective-permute-start.4 = (f32[2,32,8,256]{3,2,1,0:T(8,128)S(1)}, f32[2,32,8,256]{3,2,1,0:T(8,128)S(1)}, u32[]{:S(2)}, u32[]{:S(2)}) collective-permute-start(f32[2,32,8,256]{3,2,1,0:T(8,128)S(1)} %get-tuple-element.11), channel_id=1, source_target_pairs={{8,0},{16,8},{24,16},{32,24},{40,32},{48,40},{56,48},{64,56},{72,6... | collective-permute-start | bytes 1572872 | tf_op jit(solution)/shard_map/ppermute | solution.py:349
  23.8 14.7 %collective-permute-start.3 = (f32[2,32,8,256]{3,2,1,0:T(8,128)S(1)}, f32[2,32,8,256]{3,2,1,0:T(8,128)S(1)}, u32[]{:S(2)}, u32[]{:S(2)}) collective-permute-start(f32[2,32,8,256]{3,2,1,0:T(8,128)S(1)} %collective-permute-done.1), channel_id=1, source_target_pairs={{0,6},{1,7},{2,0},{3,1},{4,2},{5,3},{6,4},{7,5},{8,14},{9,15},{10,... | collective-permute-start | bytes 1572872 | tf_op jit(solution)/shard_map/ppermute | solution.py:354
  26.3 13.2 %collective-permute-start.2 = (f32[2,32,8,256]{3,2,1,0:T(8,128)S(1)}, f32[2,32,8,256]{3,2,1,0:T(8,128)S(1)}, u32[]{:S(2)}, u32[]{:S(2)}) collective-permute-start(f32[2,32,8,256]{3,2,1,0:T(8,128)S(1)} %collective-permute-done.1), channel_id=1, source_target_pairs={{0,2},{1,3},{2,4},{3,5},{4,6},{5,7},{6,0},{7,1},{8,10},{9,11},{10,... | collective-permute-start | bytes 1572872 | tf_op jit(solution)/shard_map/ppermute | solution.py:354
  39.5 5.9 %copy-start.7 = (s32[6]{0:T(128)S(1)}, s32[6]{0:T(128)}, u32[]{:S(2)}) copy-start(s32[6]{0:T(128)} %param.11) | copy-start | bytes 76
  39.5 5.9 %copy-start.8 = (s32[6]{0:T(128)S(1)}, s32[6]{0:T(128)}, u32[]{:S(2)}) copy-start(s32[6]{0:T(128)} %param.10) | copy-start | bytes 76
  39.5 13.7 %copy-start = (f32[2,256,256]{2,1,0:T(8,128)S(1)}, f32[2,256,256]{2,1,0:T(8,128)}, u32[]{:S(2)}) copy-start(f32[2,256,256]{2,1,0:T(8,128)} %probe_ref.1) | copy-start | bytes 1572868
  39.5 13.7 %copy-start.2 = (bf16[6,256,256]{2,1,0:T(8,128)(2,1)S(1)}, bf16[6,256,256]{2,1,0:T(8,128)(2,1)}, u32[]{:S(2)}) copy-start(bf16[6,256,256]{2,1,0:T(8,128)(2,1)} %amp_hbm.1) | copy-start | bytes 2359300
  39.5 13.7 %copy-start.3 = (bf16[6,256,256]{2,1,0:T(8,128)(2,1)S(1)}, bf16[6,256,256]{2,1,0:T(8,128)(2,1)}, u32[]{:S(2)}) copy-start(bf16[6,256,256]{2,1,0:T(8,128)(2,1)} %constant.27.clone.tab_hbm) | copy-start | bytes 2359300
  39.7 13.5 %collective-permute-start.5 = (f32[4,2,32,8,256]{4,3,2,1,0:T(8,128)S(1)}, f32[4,2,32,8,256]{4,3,2,1,0:T(8,128)S(1)}, u32[]{:S(2)}, u32[]{:S(2)}) collective-permute-start(f32[4,2,32,8,256]{4,3,2,1,0:T(8,128)S(1)} %pad_maximum_fusion.held_ref), channel_id=1, source_target_pairs={{0,1},{1,0},{2,3},{3,2},{4,5},{5,4},{6,7},{7,6},{8,9},{9,8},{10,11... | collective-permute-start | bytes 6291464 | tf_op jit(solution)/shard_map/ppermute | solution.py:358
  45.5 7.6 %collective-permute-start = (s32[13]{0:T(128)S(1)}, s32[13]{0:T(128)S(1)}, u32[]{:S(2)}, u32[]{:S(2)}) collective-permute-start(s32[13]{0:T(128)S(1)} %pad_add_fusion), channel_id=1, source_target_pairs={{0,8},{8,16},{16,24},{24,32},{32,40},{40,48},{48,56},{56,64},{64,7... | collective-permute-start | bytes 164 | tf_op jit(solution)/shard_map/ppermute | solution.py:349
  116.2 12.3 %collective-permute-start.6 = (f32[256,256]{1,0:T(8,128)S(1)}, f32[256,256]{1,0:T(8,128)S(1)}, u32[]{:S(2)}, u32[]{:S(2)}) collective-permute-start(f32[256,256]{1,0:T(8,128)S(1)} %get-tuple-element.13), channel_id=1, source_target_pairs={{0,8},{8,16},{16,24},{24,32},{32,40},{40,48},{48,56},{56,64},{64,7... | collective-permute-start | bytes 786440 | tf_op jit(solution)/shard_map/ppermute | solution.py:349
  118.1 16.0 %collective-permute-start.9 = (f32[256,256]{1,0:T(8,128)S(1)}, f32[256,256]{1,0:T(8,128)S(1)}, u32[]{:S(2)}, u32[]{:S(2)}) collective-permute-start(f32[256,256]{1,0:T(8,128)S(1)} %get-tuple-element.14), channel_id=1, source_target_pairs={{0,8},{8,16},{16,24},{24,32},{32,40},{40,48},{48,56},{56,64},{64,7... | collective-permute-start | bytes 786440 | tf_op jit(solution)/shard_map/ppermute | solution.py:349
  134.3 16.2 %collective-permute-start.14 = (f32[32,8,256]{2,1,0:T(8,128)S(1)}, f32[32,8,256]{2,1,0:T(8,128)S(1)}, u32[]{:S(2)}, u32[]{:S(2)}) collective-permute-start(f32[32,8,256]{2,1,0:T(8,128)S(1)} %get-tuple-element.18), channel_id=1, source_target_pairs={{0,6},{1,7},{2,0},{3,1},{4,2},{5,3},{6,4},{7,5},{8,14},{9,15},{10,... | collective-permute-start | bytes 786440 | tf_op jit(solution)/shard_map/ppermute | solution.py:354
  136.2 10.0 %collective-permute-start.7 = (f32[32,8,256]{2,1,0:T(8,128)S(1)}, f32[32,8,256]{2,1,0:T(8,128)S(1)}, u32[]{:S(2)}, u32[]{:S(2)}) collective-permute-start(f32[32,8,256]{2,1,0:T(8,128)S(1)} %get-tuple-element.18), channel_id=1, source_target_pairs={{0,2},{1,3},{2,4},{3,5},{4,6},{5,7},{6,0},{7,1},{8,10},{9,11},{10,... | collective-permute-start | bytes 786440 | tf_op jit(solution)/shard_map/ppermute | solution.py:354
  140.8 9.6 %collective-permute-start.13 = (f32[32,8,256]{2,1,0:T(8,128)S(1)}, f32[32,8,256]{2,1,0:T(8,128)S(1)}, u32[]{:S(2)}, u32[]{:S(2)}) collective-permute-start(f32[32,8,256]{2,1,0:T(8,128)S(1)} %get-tuple-element.19), channel_id=1, source_target_pairs={{0,2},{1,3},{2,4},{3,5},{4,6},{5,7},{6,0},{7,1},{8,10},{9,11},{10,... | collective-permute-start | bytes 786440 | tf_op jit(solution)/shard_map/ppermute | solution.py:354
  143.3 8.3 %collective-permute-start.10 = (f32[32,8,256]{2,1,0:T(8,128)S(1)}, f32[32,8,256]{2,1,0:T(8,128)S(1)}, u32[]{:S(2)}, u32[]{:S(2)}) collective-permute-start(f32[32,8,256]{2,1,0:T(8,128)S(1)} %get-tuple-element.19), channel_id=1, source_target_pairs={{0,6},{1,7},{2,0},{3,1},{4,2},{5,3},{6,4},{7,5},{8,14},{9,15},{10,... | collective-permute-start | bytes 786440 | tf_op jit(solution)/shard_map/ppermute | solution.py:354
  151.6 22.4 %copy-start.4 = (f32[6,32,8,256]{3,2,1,0:T(8,128)}, f32[6,32,8,256]{3,2,1,0:T(8,128)S(1)}, u32[]{:S(2)}) copy-start(f32[6,32,8,256]{3,2,1,0:T(8,128)S(1)} %bitcast_dynamic-update-slice_fusion.held_ref) | copy-start | bytes 4718596
  151.6 22.4 %collective-permute-start.15 = (f32[6,32,8,256]{3,2,1,0:T(8,128)S(1)}, f32[6,32,8,256]{3,2,1,0:T(8,128)}, u32[]{:S(2)}, u32[]{:S(2)}) collective-permute-start(f32[6,32,8,256]{3,2,1,0:T(8,128)S(1)} %bitcast_dynamic-update-slice_fusion.held_ref), channel_id=1, source_target_pairs={{0,1},{1,0},{2,3},{3,2},{4,5},{5,4},{6,7},{7,6},{8,9},{9,8},{10,11... | collective-permute-start | bytes 4718600 | tf_op jit(solution)/shard_map/ppermute | solution.py:358
  157.2 9.8 %collective-permute-start.8 = (f32[32,8,256]{2,1,0:T(8,128)S(1)}, f32[32,8,256]{2,1,0:T(8,128)S(1)}, u32[]{:S(2)}, u32[]{:S(2)}) collective-permute-start(f32[32,8,256]{2,1,0:T(8,128)S(1)} %collective-permute-done.7), channel_id=1, source_target_pairs={{0,2},{1,3},{2,4},{3,5},{4,6},{5,7},{6,0},{7,1},{8,10},{9,11},{10,... | collective-permute-start | bytes 786440 | tf_op jit(solution)/shard_map/ppermute | solution.py:354
  160.2 10.7 %collective-permute-start.11 = (f32[32,8,256]{2,1,0:T(8,128)S(1)}, f32[32,8,256]{2,1,0:T(8,128)S(1)}, u32[]{:S(2)}, u32[]{:S(2)}) collective-permute-start(f32[32,8,256]{2,1,0:T(8,128)S(1)} %collective-permute-done.10), channel_id=1, source_target_pairs={{0,6},{1,7},{2,0},{3,1},{4,2},{5,3},{6,4},{7,5},{8,14},{9,15},{10,... | collective-permute-start | bytes 786440 | tf_op jit(solution)/shard_map/ppermute | solution.py:354
  171.0 6.7 %copy-start.5 = (f32[2,32,8,256]{3,2,1,0:T(8,128)}, f32[2,32,8,256]{3,2,1,0:T(8,128)S(1)}, u32[]{:S(2)}) copy-start(f32[2,32,8,256]{3,2,1,0:T(8,128)S(1)} %pad_maximum_fusion.1.held_ref) | copy-start | bytes 1572868
  171.0 6.7 %collective-permute-start.12 = (f32[2,32,8,256]{3,2,1,0:T(8,128)S(1)}, f32[2,32,8,256]{3,2,1,0:T(8,128)S(1)}, u32[]{:S(2)}, u32[]{:S(2)}) collective-permute-start(f32[2,32,8,256]{3,2,1,0:T(8,128)S(1)} %pad_maximum_fusion.1.held_ref), channel_id=1, source_target_pairs={{0,1},{1,0},{2,3},{3,2},{4,5},{5,4},{6,7},{7,6},{8,9},{9,8},{10,11... | collective-permute-start | bytes 1572872 | tf_op jit(solution)/shard_map/ppermute | solution.py:358
  177.7 0.8 copy-start.6

commit v3 on v2

--- a/solution.py
+++ b/solution.py
@@ -18,16 +18,20 @@
 
 
 def tables(length):
-    steps = np.arange(length)
-    angle = (steps[:, None] * steps[None, :] % length) * (2.0 * math.pi / length)
-    factor = 1.0 / math.sqrt(length)
-    cos, sin = np.cos(angle) * factor, np.sin(angle) * factor
+    half = length // 2
+    place, freq = np.arange(half)[:, None], np.arange(half)[None, :]
+    scale = 1.0 / math.sqrt(length)
+    even, odd = [], []
+    for parity, out in ((0, even), (1, odd)):
+        angle = (place * (2 * freq + parity) % length) * (2.0 * math.pi / length)
+        cos, sin = np.cos(angle) * scale, np.sin(angle) * scale
+        by_place = np.block([[cos, -sin], [sin, cos]])
+        out += [by_place, by_place.T, by_place, by_place.T]
     parts = []
-    for table in (cos, cos - sin, cos + sin):
+    for table in [table for pair in zip(even, odd) for table in pair]:
         table = table.astype(np.float32)
         high = table.astype(jnp.bfloat16)
-        low = (table - high.astype(np.float32)).astype(jnp.bfloat16)
-        parts += [high, low]
+        parts += [high, (table - high.astype(np.float32)).astype(jnp.bfloat16)]
     return np.stack(parts)
 
 
@@ -40,26 +44,39 @@
     return jnp.dot(a, b, preferred_element_type=jnp.float32)
 
 
-def right(x, tab, which):
+def right(x, high_tab, low_tab):
     high, low = split(x)
-    th, tl = tab[2 * which], tab[2 * which + 1]
-    return dot(high, th) + dot(low, th) + dot(high, tl)
-
-
-def left(x, tab, which):
+    return dot(high, high_tab) + dot(low, high_tab) + dot(high, low_tab)
+
+
+def left(x, high_tab, low_tab):
     high, low = split(x)
-    th, tl = tab[2 * which], tab[2 * which + 1]
-    return dot(th, high) + dot(th, low) + dot(tl, high)
-
-
-def forward(mul, a, b, tab):
-    both = mul(a + b, tab, 0)
-    return both - mul(b, tab, 1), both - mul(a, tab, 2)
-
-
-def inverse(mul, a, b, tab):
-    both = mul(a + b, tab, 0)
-    return both - mul(b, tab, 2), both - mul(a, tab, 1)
+    return dot(high_tab, high) + dot(high_tab, low) + dot(low_tab, high)
+
+
+def halves(x, axis):
+    half = x.shape[axis] // 2
+    return lax.slice_in_dim(x, 0, half, axis=axis), lax.slice_in_dim(x, half, 2 * half, axis=axis)
+
+
+def join(parts, axis):
+    return jnp.concatenate(parts, axis=axis)
+
+
+def forward(mul, axis, a, b, tabs):
+    (a0, a1), (b0, b1) = halves(a, axis), halves(b, axis)
+    even = mul(join([a0 + a1, b0 + b1], axis), tabs[0], tabs[1])
+    odd = mul(join([a0 - a1, b0 - b1], axis), tabs[2], tabs[3])
+    (a0, b0), (a1, b1) = halves(even, axis), halves(odd, axis)
+    return join([a0, a1], axis), join([b0, b1], axis)
+
+
+def inverse(mul, axis, a, b, tabs):
+    (a0, a1), (b0, b1) = halves(a, axis), halves(b, axis)
+    even = mul(join([a0, b0], axis), tabs[0], tabs[1])
+    odd = mul(join([a1, b1], axis), tabs[2], tabs[3])
+    (a0, b0), (a1, b1) = halves(even, axis), halves(odd, axis)
+    return join([a0 + a1, a0 - a1], axis), join([b0 + b1, b0 - b1], axis)
 
 
 def class_of(group, step, other, parts):
@@ -67,7 +84,7 @@
     return index ^ 1 if other else index
 
 
-def patterns_kernel(size, rows, parts, slots, notes_ref, own_ref, probe_hbm, amp_hbm, tab_hbm, held_ref, swapped_ref, out_ref,
+def patterns_kernel(size, rows, parts, slots, notes_ref, own_ref, probe_hbm, amp_hbm, tab_hbm, held_ref, other_ref, out_ref,
                     own_buf, rim_buf, probe_ref, amp_ref, tab_ref, stage, own_sems, fixed_sems, piece_sems, store_sems):
     count, group = notes_ref[0, 2 * slots], notes_ref[2, 0]
     span = size + SUB
@@ -79,12 +96,16 @@
     def first_of(p):
         return pl.multiple_of(jnp.minimum(start_of(p), rows - span), SUB)
 
-    def load(p):
-        slot = lax.rem(p, 2)
-        return pltpu.make_async_copy(own_ref.at[:, pl.ds(first_of(p), span)], own_buf.at[slot], own_sems.at[slot])
+    def loads(p):
+        slot = 2 * lax.rem(p >> 1, 2)
+        return [
+            pltpu.make_async_copy(
+                own_ref.at[:, pl.ds(first_of(jnp.minimum(p + n, count - 1)), span)], own_buf.at[slot + n], own_sems.at[slot + n])
+            for n in range(2)
+        ]
 
     def store(p):
-        where = pl.ds(pl.multiple_of(p * 2 * depth, 2 * depth), 2 * depth)
+        where = pl.ds(pl.multiple_of(p * 4 * depth, 4 * depth), 4 * depth)
         return pltpu.make_async_copy(stage.at[:, where], out_ref.at[:, where], store_sems.at[p])
 
     fixed = [
@@ -92,12 +113,11 @@
         for n, (a, b) in enumerate(((probe_hbm, probe_ref), (tab_hbm, tab_ref), (amp_hbm, amp_ref)))
     ]
     rims = []
-    for other, ref in enumerate((held_ref, swapped_ref)):
+    for other, ref in enumerate((held_ref, other_ref)):
         for n, step in enumerate(STEPS):
             index = class_of(group, step, other, parts)
             rims.append(pltpu.make_async_copy(ref.at[n], rim_buf.at[:, :, index], piece_sems.at[len(rims)]))
-    load(0).start()
-    for copy in rims + fixed:
+    for copy in loads(0) + rims + fixed:
         copy.start()
 
     lane = lax.broadcasted_iota(jnp.int32, (SUB, size), 1)
@@ -117,19 +137,16 @@
         copy.wait()
     rim = rim_buf.reshape(2, rows, size)
 
-    def pattern(p, _):
-        slot = lax.rem(p, 2)
+    def moved_down(ref, shift):
+        blocks = [pltpu.roll(ref[SUB * n : SUB * (n + 1)], shift, 0) for n in range(size // SUB)]
+        return jnp.concatenate([jnp.where(head_row >= shift, here, above) for here, above in zip(blocks, blocks[-1:] + blocks)], axis=0)
+
+    def prepare(p, slot):
         row, col = notes_ref[0, p], notes_ref[0, slots + p]
         base = start_of(p)
         shift = row - base
-
-        @pl.when(p + 1 < count)
-        def _():
-            load(p + 1).start()
-
-        pr, pi = [pltpu.roll(pltpu.roll(probe_ref[ch], shift, 0), col, 1) for ch in range(2)]
+        pr, pi = [pltpu.roll(moved_down(probe_ref.at[ch], shift), col, 1) for ch in range(2)]
         mine = column >= col
-        load(p).wait()
         lead = pl.multiple_of(base - first_of(p), SUB)
         tail = pl.multiple_of(jnp.minimum(lead + size, size), SUB)
         tail_rim = pl.multiple_of(jnp.minimum(base + size, rows - SUB), SUB)
@@ -141,14 +158,13 @@
             return jnp.concatenate([head, full[SUB:]], axis=0)
 
         o_re, o_im = window(0), window(1)
-        a = pr * o_re - pi * o_im
-        b = pr * o_im + pi * o_re
-        a, b = forward(right, a, b, tab_ref)
-        a, b = forward(left, a, b, tab_ref)
+        return base, pr, pi, pr * o_re - pi * o_im, pr * o_im + pi * o_re
+
+    def constrain(p, a, b):
         factor = amp_ref[p].astype(jnp.float32) * lax.rsqrt(jnp.maximum(a * a + b * b, FLOOR * FLOOR)) - 1.0
-        a, b = a * factor, b * factor
-        a, b = inverse(left, a, b, tab_ref)
-        a, b = inverse(right, a, b, tab_ref)
+        return a * factor, b * factor
+
+    def put(p, base, pr, pi, a, b):
         for ch, g in enumerate((pr * a + pi * b, pr * b - pi * a)):
             for t in range(parts):
                 index = ((base >> 3) + t) & (parts - 1)
@@ -156,22 +172,70 @@
                     at = pl.multiple_of((2 * p + ch) * depth + SUB * m, SUB)
                     block = SUB * (parts * m + t)
                     stage[index, pl.ds(at, SUB)] = g[block : block + SUB]
-        store(p).start()
+
+    def pair(n, _):
+        first = 2 * n
+        second = jnp.minimum(first + 1, count - 1)
+
+        @pl.when(first + 2 < count)
+        def _():
+            for copy in loads(first + 2):
+                copy.start()
+
+        for copy in loads(first):
+            copy.wait()
+        slot = 2 * lax.rem(n, 2)
+        work = [(first, slot), (second, slot + 1)]
+        states = [prepare(p, at) for p, at in work]
+        waves = [state[3:] for state in states]
+        tabs = [[tab_ref[4 * stage + n] for n in range(4)] for stage in range(4)]
+        waves = [forward(right, 1, *wave, tabs[0]) for wave in waves]
+        waves = [forward(left, 0, *wave, tabs[1]) for wave in waves]
+        waves = [constrain(p, *wave) for (p, _), wave in zip(work, waves)]
+        waves = [inverse(left, 0, *wave, tabs[2]) for wave in waves]
+        waves = [inverse(right, 1, *wave, tabs[3]) for wave in waves]
+        for (p, _), state, wave in zip(work, states, waves):
+            put(p, *state[:3], *wave)
+        store(n).start()
         return 0
 
-    lax.fori_loop(0, count, pattern, 0)
+    pairs = (count + 1) >> 1
+    lax.fori_loop(0, pairs, pair, 0)
 
     def stored(p, _):
         store(p).wait()
         return 0
 
     last.wait()
-    lax.fori_loop(0, count, stored, 0)
-
-
-def patterns(notes, own, held, swapped, probe, amplitudes):
+    lax.fori_loop(0, pairs, stored, 0)
+
+
+def ordered_kernel(order_ref, turned_ref, amp_ref, out_ref):
+    order, turned = order_ref[...], turned_ref[...]
+    for p in range(amp_ref.shape[0]):
+        rows = dot(order, amp_ref[p]).astype(jnp.bfloat16)
+        out_ref[p] = dot(rows, turned).astype(jnp.bfloat16)
+
+
+def ordered(amplitudes):
+    size = amplitudes.shape[1]
+    order = np.zeros((size, size), np.float32)
+    order[np.arange(size), np.concatenate([np.arange(0, size, 2), np.arange(1, size, 2)])] = 1.0
+    vmem = pl.BlockSpec(memory_space=pltpu.VMEM)
+    return pl.pallas_call(
+        ordered_kernel,
+        out_shape=jax.ShapeDtypeStruct(amplitudes.shape, amplitudes.dtype),
+        in_specs=[vmem] * 3,
+        out_specs=vmem,
+        compiler_params=pltpu.CompilerParams(vmem_limit_bytes=16 * MIB),
+        cost_estimate=pl.CostEstimate(flops=2**28, bytes_accessed=2 * MIB, transcendentals=0),
+        name="ordered",
+    )(jnp.asarray(order, jnp.bfloat16), jnp.asarray(order.T, jnp.bfloat16), amplitudes)
+
+
+def patterns(notes, own, held, other, probe, amplitudes):
     rows, size = own.shape[1:]
-    slots, parts = amplitudes.shape[0], 2 * held.shape[0]
+    slots, parts = amplitudes.shape[0], 2 * len(STEPS)
     depth = size // parts
     length = slots * 2 * depth + SUB
     smem = pl.BlockSpec(memory_space=pltpu.SMEM)
@@ -184,21 +248,21 @@
         in_specs=[smem] + [hbm] * 4 + [anywhere] * 2,
         out_specs=anywhere,
         scratch_shapes=[
-            pltpu.VMEM((2, 2, size + SUB, size), jnp.float32),
+            pltpu.VMEM((4, 2, size + SUB, size), jnp.float32),
             pltpu.VMEM((2, rows // (SUB * parts), parts, SUB, size), jnp.float32),
             pltpu.VMEM(probe.shape, jnp.float32),
             pltpu.VMEM(amplitudes.shape, amplitudes.dtype),
             pltpu.VMEM(tab.shape, tab.dtype),
             pltpu.VMEM((parts, length, size), jnp.float32),
-            pltpu.SemaphoreType.DMA((2,)),
+            pltpu.SemaphoreType.DMA((4,)),
             pltpu.SemaphoreType.DMA((3,)),
             pltpu.SemaphoreType.DMA((parts,)),
             pltpu.SemaphoreType.DMA((slots + 1,)),
         ],
         compiler_params=pltpu.CompilerParams(vmem_limit_bytes=40 * MIB),
-        cost_estimate=pl.CostEstimate(flops=36 * 2 * size**3 * slots, bytes_accessed=12 * MIB, transcendentals=0),
+        cost_estimate=pl.CostEstimate(flops=24 * 2 * size**3 * slots, bytes_accessed=12 * MIB, transcendentals=0),
         name="patterns",
-    )(notes, own, probe, amplitudes, tab, held, swapped)
+    )(notes, own, probe, amplitudes, tab, held, other)
 
 
 def place(row, group, parts):
@@ -219,7 +283,7 @@
     lax.fori_loop(0, notes_ref.shape[0], device, 0)
 
 
-def gather_kernel(size, parts, slots, group_ref, notes_ref, got_ref, here_ref, next_re_ref, next_im_ref, total):
+def gather_kernel(size, parts, slots, group_ref, notes_ref, got_ref, here_ref, next_ref, total):
     depth = size // parts
     group = group_ref[0]
     total[...] = jnp.zeros_like(total)
@@ -241,21 +305,19 @@
     each_live(notes_ref, slots, step)
     kept = here_ref.shape[1]
     here_ref[...] = total[0, :, :kept]
-    next_re_ref[...] = total[1, 0, :kept]
-    next_im_ref[...] = total[1, 1, :kept]
+    next_ref[...] = total[1, :, :kept]
 
 
 def gathered(group, notes, got, slots, kept):
     parts, length, size = got.shape
     smem = pl.BlockSpec(memory_space=pltpu.SMEM)
     vmem = pl.BlockSpec(memory_space=pltpu.VMEM)
-    shape = jax.ShapeDtypeStruct((kept, size), jnp.float32)
-    both = jax.ShapeDtypeStruct((2, kept, size), jnp.float32)
+    shape = jax.ShapeDtypeStruct((2, kept, size), jnp.float32)
     return pl.pallas_call(
         functools.partial(gather_kernel, size, parts, slots),
-        out_shape=(both, shape, shape),
+        out_shape=(shape, shape),
         in_specs=[smem, smem, vmem],
-        out_specs=(vmem, vmem, vmem),
+        out_specs=(vmem, vmem),
         scratch_shapes=[pltpu.VMEM((2, 2, kept + SUB, size), jnp.float32)],
         compiler_params=pltpu.CompilerParams(vmem_limit_bytes=24 * MIB),
         cost_estimate=pl.CostEstimate(flops=2**22, bytes_accessed=6 * MIB, transcendentals=0),
@@ -314,33 +376,31 @@
     )(group, here, before, probe)
 
 
-def assemble_kernel(steps, parts, group_ref, held_ref, swapped_ref, *refs):
+def assemble_kernel(other, parts, group_ref, ref, *refs):
     out_ref, sems = refs[-2:]
-    copies = []
-    for other, ref in enumerate((held_ref, swapped_ref)):
-        for n, step in enumerate(steps):
-            index = class_of(group_ref[0], step, other, parts)
-            copies.append(pltpu.make_async_copy(ref.at[n], out_ref.at[n % 2, :, index], sems.at[len(copies)]))
+    core = (group_ref[0] & 1) ^ other
+    copies = [pltpu.make_async_copy(ref.at[n], out_ref.at[:, :, 2 * n + core], sems.at[n]) for n in range(parts // 2)]
     for copy in copies:
         copy.start()
     for copy in copies:
         copy.wait()
 
 
-def assembled(group, steps, held, swapped, shape, begun=()):
+def assembled(group, other, shares, shape, begun=()):
     parts = shape[2]
+    anywhere = pl.BlockSpec(memory_space=pl.ANY)
     hbm = pl.BlockSpec(memory_space=pltpu.HBM)
-    vmem = pl.BlockSpec(memory_space=pltpu.VMEM)
     return pl.pallas_call(
-        functools.partial(assemble_kernel, steps, parts),
+        functools.partial(assemble_kernel, other, parts),
         out_shape=jax.ShapeDtypeStruct(shape, jnp.float32),
-        in_specs=[pl.BlockSpec(memory_space=pltpu.SMEM), vmem, vmem] + [hbm] * len(begun),
+        in_specs=[pl.BlockSpec(memory_space=pltpu.SMEM), anywhere] + [hbm] * len(begun),
         out_specs=hbm,
-        scratch_shapes=[pltpu.SemaphoreType.DMA((2 * len(steps),))],
-        input_output_aliases={3: 0} if begun else {},
-        cost_estimate=pl.CostEstimate(flops=0, bytes_accessed=8 * MIB, transcendentals=0),
+        scratch_shapes=[pltpu.SemaphoreType.DMA((parts // 2,))],
+        input_output_aliases={2: 0} if begun else {},
+        compiler_params=pltpu.CompilerParams(vmem_limit_bytes=MIB),
+        cost_estimate=pl.CostEstimate(flops=0, bytes_accessed=4 * MIB, transcendentals=0),
         name="assembled",
-    )(group, held, swapped, *begun)
+    )(group, shares, *begun)
 
 
 def passed_along(x, axis, by):
@@ -371,28 +431,25 @@
         return lax.dynamic_index_in_dim(blocks, which, 2, keepdims=False)
 
     mine = share(index)
-    near = passed_along(mine, "tile", -1)
-    near, opposite = lax.optimization_barrier((near, share((index + 4) % parts)))
-    opposite = passed_along(opposite, "tile", -1)
-    held = jnp.stack([near, to_chip(near, 1), to_chip(near, -1), opposite])
     own_notes = jnp.concatenate([row_offset, col_offset, counts])
-    notes = jnp.stack([own_notes, passed_along(own_notes, "tile", 1), jnp.full_like(own_notes, index)])
-    sent = patterns(notes, object_field, held, to_core(held), probe, amplitudes)
+    near, opposite, notes_before = lax.optimization_barrier(
+        (passed_along(mine, "tile", -1), share((index + 4) % parts), passed_along(own_notes, "tile", 1)))
+    held = jnp.stack([near, to_chip(near, 1), to_chip(near, -1), passed_along(opposite, "tile", -1)])
+    notes = jnp.stack([own_notes, notes_before, jnp.full_like(own_notes, index)])
+    sent = patterns(notes, object_field, held, to_core(held), probe, ordered(amplitudes))
     got = lax.all_to_all(sent, "group", 0, 0)
     notes = got[:, slots * 2 * (size // parts) :, : 2 * slots + 1].astype(jnp.int32)
     notes_here, notes_before = notes[:, 0], notes[:, 1]
-    here, *spills = gathered(group, notes_here, got, slots, kept)
+    here, spill = gathered(group, notes_here, got, slots, kept)
+    spill = passed_along(spill, "tile", 1)
     weight = illumination(group, notes_here, notes_before, probe, slots, kept)
-    results, before, after = [], [], []
-    for ch, spill in enumerate(spills):
-        grad = here[ch] + passed_along(spill, "tile", 1)
-        results.append(mine[ch] + (grad / weight).reshape(mine.shape[1:]))
-        before.append(to_chip(results[ch], 1))
-        after.append(to_chip(results[ch], -1))
-    first = jnp.stack(results + before + after)
-    last = jnp.stack([to_chip(before[0], 1), to_chip(after[1], -1)])
-    field = assembled(group, (0, 0, -2, -2, 2, 2), first, to_core(first), blocks.shape)
-    field = assembled(group, (4, 4), last, to_core(last), blocks.shape, (field,))
+    result = mine + ((here + spill) / weight).reshape(mine.shape)
+    chips = parts // 2
+    same_core = [list(range(core, parts, 2)) for core in range(2)]
+    spread = jnp.broadcast_to(result, (chips, *result.shape))
+    shares = lax.all_to_all(spread, "group", 0, 0, axis_index_groups=same_core)
+    field = assembled(group, 0, shares, blocks.shape)
+    field = assembled(group, 1, to_core(shares), blocks.shape, (field,))
     return field.reshape(object_field.shape)
 
 

time: 181 us -> 156 us (0.86)
  the two profiles are of different devices: /device:TPU:263 before, /device:TPU:449 now
where the time goes in v3:
time: 156 us; the launch traced here: 155 us
  blocking collectives  71.7 us (46%)
  waiting for transfers between devices  35.8 us (23%)
  starting transfers between devices  31.1 us (20%)
  Pallas kernels  13.9 us (9%)
  local copies, waits for them, and re-layouts  1.6 us (1%)
    all_to_all x1, blocking collectives, body(): got = lax.all_to_all(sent, 'group', 0, 0)  44.5 us
    all_to_all x1, blocking collectives, body(): shares = lax.all_to_all(spread, 'group', 0, 0, axis_index_groups=same_core)  27.2 us
    ppermute x4, waiting for transfers between devices, passed_along(): return lax.ppermute(x, axis, pairs)  21.4 us
    ppermute x4, starting transfers between devices, passed_along(): return lax.ppermute(x, axis, pairs)  15.1 us
    ppermute x2, starting transfers between devices, to_core(): lax.ppermute(x, 'group', [(i, i ^ 1) for i in range(lax.axis_size('group'...  9.65 us
    ppermute x2, waiting for transfers between devices, to_chip(): lax.ppermute(x, 'group', [(i, (i + 2 * by) % devices) for i in range(devi...  9.16 us
    ppermute x2, starting transfers between devices, to_chip(): lax.ppermute(x, 'group', [(i, (i + 2 * by) % devices) for i in range(devi...  6.31 us
    ppermute x2, waiting for transfers between devices, to_core(): lax.ppermute(x, 'group', [(i, i ^ 1) for i in range(lax.axis_size('group'...  5.26 us
  transfers between devices with their start and end apart: 8, of which 8 were waited for; matrix products, arithmetic and copies ran while one was open for 0% of the time, Pallas kernels for 4%

profile of v3, /device:TPU:449, one launch (start us, length us, event | category | flops | bytes accessed | tf_op | source)
XLA Modules:
  0.0 155.4 jit_solution(5512863652474190111)
XLA Ops:
  0.0 0.0 copy-start.5
  0.0 0.0 copy-start.6
  0.0 1.3 dynamic-slice_bitcast_fusion
  1.3 5.1 %collective-permute-start = (f32[2,32,8,256]{3,2,1,0:T(8,128)S(1)}, f32[2,32,8,256]{3,2,1,0:T(8,128)S(1)}, u32[]{:S(2)}, u32[]{:S(2)}) collective-permute-start(f32[2,32,8,256]{3,2,1,0:T(8,128)S(1)} %get-tuple-element.16), channel_id=1, source_target_pairs={{8,0},{16,8},{24,16},{32,24},{40,32},{48,40},{56,48},{64,56},{72,6... | collective-permute-start | bytes 1572872 | tf_op jit(solution)/shard_map/ppermute | solution.py:409
  7.1 0.0 copy-done.5
  7.1 0.0 copy-done.6
  7.1 0.1 pad_add_fusion
  7.2 1.9 %collective-permute-start.1 = (s32[13]{0:T(128)S(1)}, s32[13]{0:T(128)S(1)}, u32[]{:S(2)}, u32[]{:S(2)}) collective-permute-start(s32[13]{0:T(128)S(1)} %pad_add_fusion), channel_id=1, source_target_pairs={{0,8},{8,16},{16,24},{24,32},{32,40},{40,48},{48,56},{56,64},{64,7... | collective-permute-start | bytes 164 | tf_op jit(solution)/shard_map/ppermute | solution.py:409
  9.1 4.5 %collective-permute-done.1 = s32[13]{0:T(128)S(1)} collective-permute-done((s32[13]{0:T(128)S(1)}, s32[13]{0:T(128)S(1)}, u32[]{:S(2)}, u32[]{:S(2)}) %collective-permute-start.1) | collective-permute-done | bytes 84 | tf_op jit(solution)/shard_map/ppermute | solution.py:409
  13.5 3.4 %collective-permute-done = f32[2,32,8,256]{3,2,1,0:T(8,128)S(1)} collective-permute-done((f32[2,32,8,256]{3,2,1,0:T(8,128)S(1)}, f32[2,32,8,256]{3,2,1,0:T(8,128)S(1)}, u32[]{:S(2)}, u32[]{:S(2)}) %collective-permute-start) | collective-permute-done | bytes 524320 | tf_op jit(solution)/shard_map/ppermute | solution.py:409
  17.0 6.2 %collective-permute-start.4 = (f32[2,32,8,256]{3,2,1,0:T(8,128)S(1)}, f32[2,32,8,256]{3,2,1,0:T(8,128)S(1)}, u32[]{:S(2)}, u32[]{:S(2)}) collective-permute-start(f32[2,32,8,256]{3,2,1,0:T(8,128)S(1)} %get-tuple-element.12), channel_id=1, source_target_pairs={{8,0},{16,8},{24,16},{32,24},{40,32},{48,40},{56,48},{64,56},{72,6... | collective-permute-start | bytes 1572872 | tf_op jit(solution)/shard_map/ppermute | solution.py:409
  23.2 4.4 %collective-permute-start.3 = (f32[2,32,8,256]{3,2,1,0:T(8,128)S(1)}, f32[2,32,8,256]{3,2,1,0:T(8,128)S(1)}, u32[]{:S(2)}, u32[]{:S(2)}) collective-permute-start(f32[2,32,8,256]{3,2,1,0:T(8,128)S(1)} %collective-permute-done), channel_id=1, source_target_pairs={{0,6},{1,7},{2,0},{3,1},{4,2},{5,3},{6,4},{7,5},{8,14},{9,15},{10,... | collective-permute-start | bytes 1572872 | tf_op jit(solution)/shard_map/ppermute | solution.py:414
  27.6 1.9 %collective-permute-start.2 = (f32[2,32,8,256]{3,2,1,0:T(8,128)S(1)}, f32[2,32,8,256]{3,2,1,0:T(8,128)S(1)}, u32[]{:S(2)}, u32[]{:S(2)}) collective-permute-start(f32[2,32,8,256]{3,2,1,0:T(8,128)S(1)} %collective-permute-done), channel_id=1, source_target_pairs={{0,2},{1,3},{2,4},{3,5},{4,6},{5,7},{6,0},{7,1},{8,10},{9,11},{10,... | collective-permute-start | bytes 1572872 | tf_op jit(solution)/shard_map/ppermute | solution.py:414
  29.5 3.3 %collective-permute-done.4 = f32[2,32,8,256]{3,2,1,0:T(8,128)S(1)} collective-permute-done((f32[2,32,8,256]{3,2,1,0:T(8,128)S(1)}, f32[2,32,8,256]{3,2,1,0:T(8,128)S(1)}, u32[]{:S(2)}, u32[]{:S(2)}) %collective-permute-start.4) | collective-permute-done | bytes 524320 | tf_op jit(solution)/shard_map/ppermute | solution.py:409
  32.9 4.1 %collective-permute-done.3 = f32[2,32,8,256]{3,2,1,0:T(8,128)S(1)} collective-permute-done((f32[2,32,8,256]{3,2,1,0:T(8,128)S(1)}, f32[2,32,8,256]{3,2,1,0:T(8,128)S(1)}, u32[]{:S(2)}, u32[]{:S(2)}) %collective-permute-start.3) | collective-permute-done | bytes 524320 | tf_op jit(solution)/shard_map/ppermute | solution.py:414
  37.0 5.0 %collective-permute-done.2 = f32[2,32,8,256]{3,2,1,0:T(8,128)S(1)} collective-permute-done((f32[2,32,8,256]{3,2,1,0:T(8,128)S(1)}, f32[2,32,8,256]{3,2,1,0:T(8,128)S(1)}, u32[]{:S(2)}, u32[]{:S(2)}) %collective-permute-start.2) | collective-permute-done | bytes 524320 | tf_op jit(solution)/shard_map/ppermute | solution.py:414
  42.0 0.0 copy-start
  42.0 0.0 copy-start.2
  42.0 0.0 copy-start.3
  42.0 0.0 copy-start.1
  42.0 0.0 copy-start.4
  42.0 0.1 pad_maximum_fusion.held_ref
  42.2 5.2 %collective-permute-start.5 = (f32[4,2,32,8,256]{4,3,2,1,0:T(8,128)S(1)}, f32[4,2,32,8,256]{4,3,2,1,0:T(8,128)S(1)}, u32[]{:S(2)}, u32[]{:S(2)}) collective-permute-start(f32[4,2,32,8,256]{4,3,2,1,0:T(8,128)S(1)} %pad_maximum_fusion.held_ref), channel_id=1, source_target_pairs={{0,1},{1,0},{2,3},{3,2},{4,5},{5,4},{6,7},{7,6},{8,9},{9,8},{10,11... | collective-permute-start | bytes 6291464 | tf_op jit(solution)/shard_map/ppermute | solution.py:418
  47.4 0.1 pad.6.clone
  47.5 0.0 copy-done
  47.5 0.0 copy-done.2
  47.5 0.0 copy-done.3
  47.5 0.7 ordered.1.amp_hbm
  48.2 0.1 fusion.1
  48.2 0.1 add_add_fusion.notes_ref
  48.3 2.8 %collective-permute-done.5.other_ref = f32[4,2,32,8,256]{4,3,2,1,0:T(8,128)S(1)} collective-permute-done((f32[4,2,32,8,256]{4,3,2,1,0:T(8,128)S(1)}, f32[4,2,32,8,256]{4,3,2,1,0:T(8,128)S(1)}, u32[]{:S(2)}, u32[]{:S(2)}) %collective-permute-start.5) | collective-permute-done | bytes 2097184 | tf_op jit(solution)/shard_map/ppermute | solution.py:418
  51.2 0.0 copy-done.1
  51.2 0.0 copy-done.4
  51.2 4.2 %patterns.1 = f32[8,392,256]{2,1,0:T(8,128)S(1)} custom-call(s32[3,13]{1,0:T(4,128)S(1)} %add_add_fusion.notes_ref, f32[2,2048,256]{2,1,0:T(8,128)} %own_ref.1, f32[2,256,256]{2,1,0:T(8,128)S(1)} %copy-done.1, bf16[6,256,256]{2,1,0:T(8,128)(2,1)S(1)} %ordered.1.amp_hbm, bf16[16,256,256]{2,1,0:T(8,128)(2,1)S(1)} %copy-done.4, ...), custom_call_target="tpu_custom_call" | custom-call | flops 4831838208 | bytes 12582912 | tf_op jit(solution)/shard_map/patterns/pallas_call | solution.py:245
  55.4 44.5 %all_to_all.10.got_ref = f32[8,392,256]{2,1,0:T(8,128)S(1)} all-to-all(f32[8,392,256]{2,1,0:T(8,128)S(1)} %patterns.1), channel_id=1, replica_groups=mesh['tile'=64,'group'=8] {'group'}, dimensions={0} | all-to-all | bytes 6422528 | tf_op jit(solution)/shard_map/all_to_all | solution.py:440
  99.9 1.7 %gathered.1 = (f32[2,256,256]{2,1,0:T(8,128)S(1)}, f32[2,256,256]{2,1,0:T(8,128)S(1)}) custom-call(s32[1]{0:T(128)} %bitcast.group_ref, s32[8,13]{1,0:T(8,128)S(1)} %bitcast.23, f32[8,392,256]{2,1,0:T(8,128)S(1)} %all_to_all.10.got_ref), custom_call_target="tpu_custom_call" | custom-call | flops 4194304 | bytes 6291456 | tf_op jit(solution)/shard_map/gathered/pallas_call | solution.py:316
  101.6 1.9 %collective-permute-start.6 = (f32[2,256,256]{2,1,0:T(8,128)S(1)}, f32[2,256,256]{2,1,0:T(8,128)S(1)}, u32[]{:S(2)}, u32[]{:S(2)}) collective-permute-start(f32[2,256,256]{2,1,0:T(8,128)S(1)} %get-tuple-element.14), channel_id=1, source_target_pairs={{0,8},{8,16},{16,24},{24,32},{32,40},{40,48},{48,56},{56,64},{64,7... | collective-permute-start | bytes 1572872 | tf_op jit(solution)/shard_map/ppermute | solution.py:409
  103.5 4.6 %illumination.1 = f32[256,256]{1,0:T(8,128)S(1)} custom-call(s32[1]{0:T(128)} %bitcast.group_ref, s32[8,13]{1,0:T(8,128)S(1)} %bitcast.24, s32[8,13]{1,0:T(8,128)S(1)} %bitcast.25, f32[2,256,256]{2,1,0:T(8,128)S(1)} %copy-done.1), custom_call_target="tpu_custom_call" | custom-call | flops 4194304 | bytes 8388608 | tf_op jit(solution)/shard_map/illumination/pallas_call | solution.py:364
  108.1 10.2 %collective-permute-done.6 = f32[2,256,256]{2,1,0:T(8,128)S(1)} collective-permute-done((f32[2,256,256]{2,1,0:T(8,128)S(1)}, f32[2,256,256]{2,1,0:T(8,128)S(1)}, u32[]{:S(2)}, u32[]{:S(2)}) %collective-permute-start.6) | collective-permute-done | bytes 524320 | tf_op jit(solution)/shard_map/ppermute | solution.py:409
  118.3 0.1 bitcast_add_fusion
  118.4 0.2 broadcast_in_dim.8
  118.6 27.2 %all_to_all.11.ref = f32[4,2,32,8,256]{4,3,2,1,0:T(8,128)S(1)} all-to-all(f32[4,2,32,8,256]{4,3,2,1,0:T(8,128)S(1)} %broadcast_in_dim.8), channel_id=1, replica_groups={{0,2,4,6},{1,3,5,7},{8,10,12,14},{9,11,13,15},{16,18,20,22},{17,19,21,2..., dimensions={0} | all-to-all | bytes 4194304 | tf_op jit(solution)/shard_map/all_to_all | solution.py:450
  145.8 4.4 %collective-permute-start.7 = (f32[4,2,32,8,256]{4,3,2,1,0:T(8,128)S(1)}, f32[4,2,32,8,256]{4,3,2,1,0:T(8,128)S(1)}, u32[]{:S(2)}, u32[]{:S(2)}) collective-permute-start(f32[4,2,32,8,256]{4,3,2,1,0:T(8,128)S(1)} %all_to_all.11.ref), channel_id=1, source_target_pairs={{0,1},{1,0},{2,3},{3,2},{4,5},{5,4},{6,7},{7,6},{8,9},{9,8},{10,11... | collective-permute-start | bytes 6291464 | tf_op jit(solution)/shard_map/ppermute | solution.py:418
  150.3 1.3 assembled.2.refs_0_
  151.6 2.4 %collective-permute-done.7.ref = f32[4,2,32,8,256]{4,3,2,1,0:T(8,128)S(1)} collective-permute-done((f32[4,2,32,8,256]{4,3,2,1,0:T(8,128)S(1)}, f32[4,2,32,8,256]{4,3,2,1,0:T(8,128)S(1)}, u32[]{:S(2)}, u32[]{:S(2)}) %collective-permute-start.7) | collective-permute-done | bytes 2097184 | tf_op jit(solution)/shard_map/ppermute | solution.py:418
  154.0 1.3 assembled.3
  (2 shorter events, 0.0 us)
Async XLA Ops:
  0.0 7.1 %copy-start.5 = (s32[6]{0:T(128)S(1)}, s32[6]{0:T(128)}, u32[]{:S(2)}) copy-start(s32[6]{0:T(128)} %param.13) | copy-start | bytes 76
  0.0 7.1 %copy-start.6 = (s32[6]{0:T(128)S(1)}, s32[6]{0:T(128)}, u32[]{:S(2)}) copy-start(s32[6]{0:T(128)} %param.12) | copy-start | bytes 76
  1.3 15.7 %collective-permute-start = (f32[2,32,8,256]{3,2,1,0:T(8,128)S(1)}, f32[2,32,8,256]{3,2,1,0:T(8,128)S(1)}, u32[]{:S(2)}, u32[]{:S(2)}) collective-permute-start(f32[2,32,8,256]{3,2,1,0:T(8,128)S(1)} %get-tuple-element.16), channel_id=1, source_target_pairs={{8,0},{16,8},{24,16},{32,24},{40,32},{48,40},{56,48},{64,56},{72,6... | collective-permute-start | bytes 1572872 | tf_op jit(solution)/shard_map/ppermute | solution.py:409
  7.2 6.4 %collective-permute-start.1 = (s32[13]{0:T(128)S(1)}, s32[13]{0:T(128)S(1)}, u32[]{:S(2)}, u32[]{:S(2)}) collective-permute-start(s32[13]{0:T(128)S(1)} %pad_add_fusion), channel_id=1, source_target_pairs={{0,8},{8,16},{16,24},{24,32},{32,40},{40,48},{48,56},{56,64},{64,7... | collective-permute-start | bytes 164 | tf_op jit(solution)/shard_map/ppermute | solution.py:409
  17.0 15.9 %collective-permute-start.4 = (f32[2,32,8,256]{3,2,1,0:T(8,128)S(1)}, f32[2,32,8,256]{3,2,1,0:T(8,128)S(1)}, u32[]{:S(2)}, u32[]{:S(2)}) collective-permute-start(f32[2,32,8,256]{3,2,1,0:T(8,128)S(1)} %get-tuple-element.12), channel_id=1, source_target_pairs={{8,0},{16,8},{24,16},{32,24},{40,32},{48,40},{56,48},{64,56},{72,6... | collective-permute-start | bytes 1572872 | tf_op jit(solution)/shard_map/ppermute | solution.py:409
  23.2 13.8 %collective-permute-start.3 = (f32[2,32,8,256]{3,2,1,0:T(8,128)S(1)}, f32[2,32,8,256]{3,2,1,0:T(8,128)S(1)}, u32[]{:S(2)}, u32[]{:S(2)}) collective-permute-start(f32[2,32,8,256]{3,2,1,0:T(8,128)S(1)} %collective-permute-done), channel_id=1, source_target_pairs={{0,6},{1,7},{2,0},{3,1},{4,2},{5,3},{6,4},{7,5},{8,14},{9,15},{10,... | collective-permute-start | bytes 1572872 | tf_op jit(solution)/shard_map/ppermute | solution.py:414
  27.6 14.4 %collective-permute-start.2 = (f32[2,32,8,256]{3,2,1,0:T(8,128)S(1)}, f32[2,32,8,256]{3,2,1,0:T(8,128)S(1)}, u32[]{:S(2)}, u32[]{:S(2)}) collective-permute-start(f32[2,32,8,256]{3,2,1,0:T(8,128)S(1)} %collective-permute-done), channel_id=1, source_target_pairs={{0,2},{1,3},{2,4},{3,5},{4,6},{5,7},{6,0},{7,1},{8,10},{9,11},{10,... | collective-permute-start | bytes 1572872 | tf_op jit(solution)/shard_map/ppermute | solution.py:414
  42.0 5.5 %copy-start = (bf16[6,256,256]{2,1,0:T(8,128)(2,1)S(1)}, bf16[6,256,256]{2,1,0:T(8,128)(2,1)}, u32[]{:S(2)}) copy-start(bf16[6,256,256]{2,1,0:T(8,128)(2,1)} %amp_ref.1) | copy-start | bytes 2359300
  42.0 5.5 %copy-start.2 = (bf16[256,256]{1,0:T(8,128)(2,1)S(1)}, bf16[256,256]{1,0:T(8,128)(2,1)}, u32[]{:S(2)}) copy-start(bf16[256,256]{1,0:T(8,128)(2,1)} %constant.32.clone.turned_ref) | copy-start | bytes 393220
  42.0 5.5 %copy-start.3 = (bf16[256,256]{1,0:T(8,128)(2,1)S(1)}, bf16[256,256]{1,0:T(8,128)(2,1)}, u32[]{:S(2)}) copy-start(bf16[256,256]{1,0:T(8,128)(2,1)} %constant.31.clone.order_ref) | copy-start | bytes 393220
  42.0 9.1 %copy-start.1 = (f32[2,256,256]{2,1,0:T(8,128)S(1)}, f32[2,256,256]{2,1,0:T(8,128)}, u32[]{:S(2)}) copy-start(f32[2,256,256]{2,1,0:T(8,128)} %probe_ref.1) | copy-start | bytes 1572868
  42.0 9.1 %copy-start.4 = (bf16[16,256,256]{2,1,0:T(8,128)(2,1)S(1)}, bf16[16,256,256]{2,1,0:T(8,128)(2,1)}, u32[]{:S(2)}) copy-start(bf16[16,256,256]{2,1,0:T(8,128)(2,1)} %constant.33.clone.tab_hbm) | copy-start | bytes 6291460
  42.2 9.0 %collective-permute-start.5 = (f32[4,2,32,8,256]{4,3,2,1,0:T(8,128)S(1)}, f32[4,2,32,8,256]{4,3,2,1,0:T(8,128)S(1)}, u32[]{:S(2)}, u32[]{:S(2)}) collective-permute-start(f32[4,2,32,8,256]{4,3,2,1,0:T(8,128)S(1)} %pad_maximum_fusion.held_ref), channel_id=1, source_target_pairs={{0,1},{1,0},{2,3},{3,2},{4,5},{5,4},{6,7},{7,6},{8,9},{9,8},{10,11... | collective-permute-start | bytes 6291464 | tf_op jit(solution)/shard_map/ppermute | solution.py:418
  101.6 16.7 %collective-permute-start.6 = (f32[2,256,256]{2,1,0:T(8,128)S(1)}, f32[2,256,256]{2,1,0:T(8,128)S(1)}, u32[]{:S(2)}, u32[]{:S(2)}) collective-permute-start(f32[2,256,256]{2,1,0:T(8,128)S(1)} %get-tuple-element.14), channel_id=1, source_target_pairs={{0,8},{8,16},{16,24},{24,32},{32,40},{40,48},{48,56},{56,64},{64,7... | collective-permute-start | bytes 1572872 | tf_op jit(solution)/shard_map/ppermute | solution.py:409
  145.8 8.2 %collective-permute-start.7 = (f32[4,2,32,8,256]{4,3,2,1,0:T(8,128)S(1)}, f32[4,2,32,8,256]{4,3,2,1,0:T(8,128)S(1)}, u32[]{:S(2)}, u32[]{:S(2)}) collective-permute-start(f32[4,2,32,8,256]{4,3,2,1,0:T(8,128)S(1)} %all_to_all.11.ref), channel_id=1, source_target_pairs={{0,1},{1,0},{2,3},{3,2},{4,5},{5,4},{6,7},{7,6},{8,9},{9,8},{10,11... | collective-permute-start | bytes 6291464 | tf_op jit(solution)/shard_map/ppermute | solution.py:418

commit v4 on v3

--- a/solution.py
+++ b/solution.py
@@ -14,7 +14,7 @@
 SUB = 8
 MIB = 2**20
 
-STEPS = (0, -2, 2, 4)
+STEPS = (0, -2, 4, 2)
 
 
 def tables(length):
@@ -84,7 +84,7 @@
     return index ^ 1 if other else index
 
 
-def patterns_kernel(size, rows, parts, slots, notes_ref, own_ref, probe_hbm, amp_hbm, tab_hbm, held_ref, other_ref, out_ref,
+def patterns_kernel(size, rows, parts, slots, notes_ref, own_ref, probe_hbm, amp_hbm, tab_hbm, near_ref, far_ref, other_near_ref, other_far_ref, out_ref,
                     own_buf, rim_buf, probe_ref, amp_ref, tab_ref, stage, own_sems, fixed_sems, piece_sems, store_sems):
     count, group = notes_ref[0, 2 * slots], notes_ref[2, 0]
     span = size + SUB
@@ -113,10 +113,10 @@
         for n, (a, b) in enumerate(((probe_hbm, probe_ref), (tab_hbm, tab_ref), (amp_hbm, amp_ref)))
     ]
     rims = []
-    for other, ref in enumerate((held_ref, other_ref)):
+    for other, refs in enumerate(((near_ref, far_ref), (other_near_ref, other_far_ref))):
         for n, step in enumerate(STEPS):
             index = class_of(group, step, other, parts)
-            rims.append(pltpu.make_async_copy(ref.at[n], rim_buf.at[:, :, index], piece_sems.at[len(rims)]))
+            rims.append(pltpu.make_async_copy(refs[n // 2].at[n % 2], rim_buf.at[:, :, index], piece_sems.at[len(rims)]))
     for copy in loads(0) + rims + fixed:
         copy.start()
 
@@ -233,7 +233,7 @@
     )(jnp.asarray(order, jnp.bfloat16), jnp.asarray(order.T, jnp.bfloat16), amplitudes)
 
 
-def patterns(notes, own, held, other, probe, amplitudes):
+def patterns(notes, own, shares, probe, amplitudes):
     rows, size = own.shape[1:]
     slots, parts = amplitudes.shape[0], 2 * len(STEPS)
     depth = size // parts
@@ -245,7 +245,7 @@
     return pl.pallas_call(
         functools.partial(patterns_kernel, size, rows, parts, slots),
         out_shape=jax.ShapeDtypeStruct((parts, length, size), jnp.float32),
-        in_specs=[smem] + [hbm] * 4 + [anywhere] * 2,
+        in_specs=[smem] + [hbm] * 4 + [anywhere] * 4,
         out_specs=anywhere,
         scratch_shapes=[
             pltpu.VMEM((4, 2, size + SUB, size), jnp.float32),
@@ -262,7 +262,7 @@
         compiler_params=pltpu.CompilerParams(vmem_limit_bytes=40 * MIB),
         cost_estimate=pl.CostEstimate(flops=24 * 2 * size**3 * slots, bytes_accessed=12 * MIB, transcendentals=0),
         name="patterns",
-    )(notes, own, probe, amplitudes, tab, held, other)
+    )(notes, own, probe, amplitudes, tab, *shares)
 
 
 def place(row, group, parts):
@@ -432,11 +432,11 @@
 
     mine = share(index)
     own_notes = jnp.concatenate([row_offset, col_offset, counts])
-    near, opposite, notes_before = lax.optimization_barrier(
-        (passed_along(mine, "tile", -1), share((index + 4) % parts), passed_along(own_notes, "tile", 1)))
-    held = jnp.stack([near, to_chip(near, 1), to_chip(near, -1), passed_along(opposite, "tile", -1)])
+    far = passed_along(jnp.stack([share((index + 4) % parts), share((index + 2) % parts)]), "tile", -1)
+    near, notes_before = lax.optimization_barrier((passed_along(mine, "tile", -1), passed_along(own_notes, "tile", 1)))
+    near = jnp.stack([near, to_chip(near, 1)])
     notes = jnp.stack([own_notes, notes_before, jnp.full_like(own_notes, index)])
-    sent = patterns(notes, object_field, held, to_core(held), probe, ordered(amplitudes))
+    sent = patterns(notes, object_field, (near, far, to_core(near), to_core(far)), probe, ordered(amplitudes))
     got = lax.all_to_all(sent, "group", 0, 0)
     notes = got[:, slots * 2 * (size // parts) :, : 2 * slots + 1].astype(jnp.int32)
     notes_here, notes_before = notes[:, 0], notes[:, 1]

time: 156 us -> 155 us (level)
  waiting for transfers between devices: 35.8 us -> 32.5 us
  blocking collectives: 71.7 us -> 74.9 us
  starting transfers between devices: 31.1 us -> 28.9 us
    ppermute x2 -> x3, starting transfers between devices: 9.65 us -> 13.4 us  [to_core(): lax.ppermute(x, 'group', [(i, i ^ 1) for i in range(lax.axis_size('group'...]
    ppermute x4, waiting for transfers between devices: 21.4 us -> 18 us  [passed_along(): return lax.ppermute(x, axis, pairs)]
    ppermute x2 -> x1, starting transfers between devices: 6.31 us -> 3.11 us  [to_chip(): lax.ppermute(x, 'group', [(i, (i + 2 * by) % devices) for i in range(devi...]
    all_to_all x1, blocking collectives: 44.5 us -> 47.7 us  [body(): got = lax.all_to_all(sent, 'group', 0, 0)]
    ppermute x4, starting transfers between devices: 15.1 us -> 12.4 us  [passed_along(): return lax.ppermute(x, axis, pairs)]
    another operation x0 -> x1, local copies, waits for them, and re-layouts: none -> 1.61 us  [body(): jnp.stack([share((index + 4) % parts), share((index + 2) % parts)])]
    ppermute x2 -> x1, waiting for transfers between devices: 9.16 us -> 10.7 us  [to_chip(): lax.ppermute(x, 'group', [(i, (i + 2 * by) % devices) for i in range(devi...]
    ppermute x2 -> x3, waiting for transfers between devices: 5.26 us -> 3.76 us  [to_core(): lax.ppermute(x, 'group', [(i, i ^ 1) for i in range(lax.axis_size('group'...]
  transfers between devices with their start and end apart: 8 -> 8, of which waited for: 8 -> 7; matrix products, arithmetic and copies ran while one was open for 0% -> 0% of each run, Pallas kernels for 4% -> 4%
where the time goes in v4:
time: 155 us; the launch traced here: 153 us
  blocking collectives  74.9 us (48%)
  waiting for transfers between devices  32.5 us (21%)
  starting transfers between devices  28.9 us (19%)
  Pallas kernels  13.4 us (9%)
  local copies, waits for them, and re-layouts  1.91 us (1%)
    all_to_all x1, blocking collectives, body(): got = lax.all_to_all(sent, 'group', 0, 0)  47.7 us
    all_to_all x1, blocking collectives, body(): shares = lax.all_to_all(spread, 'group', 0, 0, axis_index_groups=same_core)  27.2 us
    ppermute x4, waiting for transfers between devices, passed_along(): return lax.ppermute(x, axis, pairs)  18 us
    ppermute x3, starting transfers between devices, to_core(): lax.ppermute(x, 'group', [(i, i ^ 1) for i in range(lax.axis_size('group'...  13.4 us
    ppermute x4, starting transfers between devices, passed_along(): return lax.ppermute(x, axis, pairs)  12.4 us
    ppermute x1, waiting for transfers between devices, to_chip(): lax.ppermute(x, 'group', [(i, (i + 2 * by) % devices) for i in range(devi...  10.7 us
    pallas_call x1, Pallas kernels, illumination(): pl.pallas_call(functools.partial(illumination_kernel, size, parts, slots)...  4.24 us
    pallas_call x1, Pallas kernels, patterns(): pl.pallas_call(functools.partial(patterns_kernel, size, rows, parts, slot...  4.24 us
  transfers between devices with their start and end apart: 8, of which 7 were waited for; matrix products, arithmetic and copies ran while one was open for 0% of the time, Pallas kernels for 4%

profile of v4, /device:TPU:449, one launch (start us, length us, event | category | flops | bytes accessed | tf_op | source)
XLA Modules:
  0.0 152.9 jit_solution(10687742511956822840)
XLA Ops:
  0.0 0.0 copy-start.5
  0.0 0.0 copy-start.6
  0.0 0.0 copy-start
  0.0 0.0 copy-start.2
  0.0 0.0 copy-start.3
  0.0 1.6 %dynamic-slice_bitcast_fusion.1 = (f32[1,2,32,8,256]{4,3,2,1,0:T(8,128)S(1)}, f32[2,32,8,256]{3,2,1,0:T(8,128)S(1)}, f32[1,2,32,8,256]{4,3,2,1,0:T(8,128)S(1)}) fusion(f32[2,32,8,8,256]{4,3,2,1,0:T(8,128)} %bitcast.28, s32[]{:T(128)S(6)} %select_n.23, s32[]{:T(128)S(6)} %select_n.21, s32[]{:T(128)S(6)} %select_n.25), kind=kLoop, calls=%fused_computation.4 | loop fusion | bytes 3145740 | tf_op jit(solution)/shard_map/stack | solution.py:435
  1.7 0.0 copy-start.1
  1.7 0.0 copy-start.4
  1.7 5.2 %collective-permute-start = (f32[2,32,8,256]{3,2,1,0:T(8,128)S(1)}, f32[2,32,8,256]{3,2,1,0:T(8,128)S(1)}, u32[]{:S(2)}, u32[]{:S(2)}) collective-permute-start(f32[2,32,8,256]{3,2,1,0:T(8,128)S(1)} %get-tuple-element.14), channel_id=1, source_target_pairs={{8,0},{16,8},{24,16},{32,24},{40,32},{48,40},{56,48},{64,56},{72,6... | collective-permute-start | bytes 1572872 | tf_op jit(solution)/shard_map/ppermute | solution.py:409
  6.9 0.1 pad_maximum_fusion.1
  7.0 3.0 %collective-permute-start.3 = (f32[2,2,32,8,256]{4,3,2,1,0:T(8,128)S(1)}, f32[2,2,32,8,256]{4,3,2,1,0:T(8,128)S(1)}, u32[]{:S(2)}, u32[]{:S(2)}) collective-permute-start(f32[2,2,32,8,256]{4,3,2,1,0:T(8,128)S(1)} %pad_maximum_fusion.1), channel_id=1, source_target_pairs={{8,0},{16,8},{24,16},{32,24},{40,32},{48,40},{56,48},{64,56},{72,6... | collective-permute-start | bytes 3145736 | tf_op jit(solution)/shard_map/ppermute | solution.py:409
  10.6 0.0 copy-done.5
  10.6 0.0 copy-done.6
  10.7 0.1 pad_add_fusion
  10.7 2.3 %collective-permute-start.1 = (s32[13]{0:T(128)S(1)}, s32[13]{0:T(128)S(1)}, u32[]{:S(2)}, u32[]{:S(2)}) collective-permute-start(s32[13]{0:T(128)S(1)} %pad_add_fusion), channel_id=1, source_target_pairs={{0,8},{8,16},{16,24},{24,32},{32,40},{40,48},{48,56},{56,64},{64,7... | collective-permute-start | bytes 164 | tf_op jit(solution)/shard_map/ppermute | solution.py:409
  13.0 4.1 %collective-permute-done.1 = s32[13]{0:T(128)S(1)} collective-permute-done((s32[13]{0:T(128)S(1)}, s32[13]{0:T(128)S(1)}, u32[]{:S(2)}, u32[]{:S(2)}) %collective-permute-start.1) | collective-permute-done | bytes 84 | tf_op jit(solution)/shard_map/ppermute | solution.py:409
  17.1 0.4 collective-permute-done
  17.5 3.1 %collective-permute-start.2 = (f32[2,32,8,256]{3,2,1,0:T(8,128)S(1)}, f32[2,32,8,256]{3,2,1,0:T(8,128)S(1)}, u32[]{:S(2)}, u32[]{:S(2)}) collective-permute-start(f32[2,32,8,256]{3,2,1,0:T(8,128)S(1)} %collective-permute-done), channel_id=1, source_target_pairs={{0,2},{1,3},{2,4},{3,5},{4,6},{5,7},{6,0},{7,1},{8,10},{9,11},{10,... | collective-permute-start | bytes 1572872 | tf_op jit(solution)/shard_map/ppermute | solution.py:414
  20.6 10.7 %collective-permute-done.2 = f32[2,32,8,256]{3,2,1,0:T(8,128)S(1)} collective-permute-done((f32[2,32,8,256]{3,2,1,0:T(8,128)S(1)}, f32[2,32,8,256]{3,2,1,0:T(8,128)S(1)}, u32[]{:S(2)}, u32[]{:S(2)}) %collective-permute-start.2) | collective-permute-done | bytes 524320 | tf_op jit(solution)/shard_map/ppermute | solution.py:414
  31.3 0.1 pad_maximum_fusion.near_ref
  31.4 5.5 %collective-permute-start.4 = (f32[2,2,32,8,256]{4,3,2,1,0:T(8,128)S(1)}, f32[2,2,32,8,256]{4,3,2,1,0:T(8,128)S(1)}, u32[]{:S(2)}, u32[]{:S(2)}) collective-permute-start(f32[2,2,32,8,256]{4,3,2,1,0:T(8,128)S(1)} %pad_maximum_fusion.near_ref), channel_id=1, source_target_pairs={{0,1},{1,0},{2,3},{3,2},{4,5},{5,4},{6,7},{7,6},{8,9},{9,8},{10,11... | collective-permute-start | bytes 3145736 | tf_op jit(solution)/shard_map/ppermute | solution.py:418
  36.9 3.0 %collective-permute-done.3.far_ref = f32[2,2,32,8,256]{4,3,2,1,0:T(8,128)S(1)} collective-permute-done((f32[2,2,32,8,256]{4,3,2,1,0:T(8,128)S(1)}, f32[2,2,32,8,256]{4,3,2,1,0:T(8,128)S(1)}, u32[]{:S(2)}, u32[]{:S(2)}) %collective-permute-start.3) | collective-permute-done | bytes 1048608 | tf_op jit(solution)/shard_map/ppermute | solution.py:409
  39.9 3.4 %collective-permute-start.5 = (f32[2,2,32,8,256]{4,3,2,1,0:T(8,128)S(1)}, f32[2,2,32,8,256]{4,3,2,1,0:T(8,128)S(1)}, u32[]{:S(2)}, u32[]{:S(2)}) collective-permute-start(f32[2,2,32,8,256]{4,3,2,1,0:T(8,128)S(1)} %collective-permute-done.3.far_ref), channel_id=1, source_target_pairs={{0,1},{1,0},{2,3},{3,2},{4,5},{5,4},{6,7},{7,6},{8,9},{9,8},{10,11... | collective-permute-start | bytes 3145736 | tf_op jit(solution)/shard_map/ppermute | solution.py:418
  43.4 0.1 pad.6.clone
  43.5 0.0 copy-done
  43.5 0.0 copy-done.2
  43.5 0.0 copy-done.3
  43.5 0.7 ordered.1.amp_hbm
  44.2 0.1 fusion.1
  44.2 0.1 add_add_fusion.notes_ref
  44.3 0.0 collective-permute-done.4.other_near_ref
  44.3 1.3 collective-permute-done.5.other_far_ref
  45.7 0.0 copy-done.1
  45.7 0.0 copy-done.4
  45.7 4.2 %patterns.1 = f32[8,392,256]{2,1,0:T(8,128)S(1)} custom-call(s32[3,13]{1,0:T(4,128)S(1)} %add_add_fusion.notes_ref, f32[2,2048,256]{2,1,0:T(8,128)} %own_ref.1, f32[2,256,256]{2,1,0:T(8,128)S(1)} %copy-done.1, bf16[6,256,256]{2,1,0:T(8,128)(2,1)S(1)} %ordered.1.amp_hbm, bf16[16,256,256]{2,1,0:T(8,128)(2,1)S(1)} %copy-done.4, ...), custom_call_target="tpu_custom_call" | custom-call | flops 4831838208 | bytes 12582912 | tf_op jit(solution)/shard_map/patterns/pallas_call | solution.py:245
  49.9 47.7 %all_to_all.10.got_ref = f32[8,392,256]{2,1,0:T(8,128)S(1)} all-to-all(f32[8,392,256]{2,1,0:T(8,128)S(1)} %patterns.1), channel_id=1, replica_groups=mesh['tile'=64,'group'=8] {'group'}, dimensions={0} | all-to-all | bytes 6422528 | tf_op jit(solution)/shard_map/all_to_all | solution.py:440
  97.6 1.5 gathered.1
  99.1 1.9 %collective-permute-start.6 = (f32[2,256,256]{2,1,0:T(8,128)S(1)}, f32[2,256,256]{2,1,0:T(8,128)S(1)}, u32[]{:S(2)}, u32[]{:S(2)}) collective-permute-start(f32[2,256,256]{2,1,0:T(8,128)S(1)} %get-tuple-element.12), channel_id=1, source_target_pairs={{0,8},{8,16},{16,24},{24,32},{32,40},{40,48},{48,56},{56,64},{64,7... | collective-permute-start | bytes 1572872 | tf_op jit(solution)/shard_map/ppermute | solution.py:409
  101.1 4.2 %illumination.1 = f32[256,256]{1,0:T(8,128)S(1)} custom-call(s32[1]{0:T(128)} %bitcast.group_ref, s32[8,13]{1,0:T(8,128)S(1)} %bitcast.26, s32[8,13]{1,0:T(8,128)S(1)} %bitcast.27, f32[2,256,256]{2,1,0:T(8,128)S(1)} %copy-done.1), custom_call_target="tpu_custom_call" | custom-call | flops 4194304 | bytes 8388608 | tf_op jit(solution)/shard_map/illumination/pallas_call | solution.py:364
  105.3 10.5 %collective-permute-done.6 = f32[2,256,256]{2,1,0:T(8,128)S(1)} collective-permute-done((f32[2,256,256]{2,1,0:T(8,128)S(1)}, f32[2,256,256]{2,1,0:T(8,128)S(1)}, u32[]{:S(2)}, u32[]{:S(2)}) %collective-permute-start.6) | collective-permute-done | bytes 524320 | tf_op jit(solution)/shard_map/ppermute | solution.py:409
  115.9 0.1 bitcast_add_fusion
  116.0 0.2 broadcast_in_dim.8
  116.2 27.2 %all_to_all.11.ref = f32[4,2,32,8,256]{4,3,2,1,0:T(8,128)S(1)} all-to-all(f32[4,2,32,8,256]{4,3,2,1,0:T(8,128)S(1)} %broadcast_in_dim.8), channel_id=1, replica_groups={{0,2,4,6},{1,3,5,7},{8,10,12,14},{9,11,13,15},{16,18,20,22},{17,19,21,2..., dimensions={0} | all-to-all | bytes 4194304 | tf_op jit(solution)/shard_map/all_to_all | solution.py:450
  143.4 4.4 %collective-permute-start.7 = (f32[4,2,32,8,256]{4,3,2,1,0:T(8,128)S(1)}, f32[4,2,32,8,256]{4,3,2,1,0:T(8,128)S(1)}, u32[]{:S(2)}, u32[]{:S(2)}) collective-permute-start(f32[4,2,32,8,256]{4,3,2,1,0:T(8,128)S(1)} %all_to_all.11.ref), channel_id=1, source_target_pairs={{0,1},{1,0},{2,3},{3,2},{4,5},{5,4},{6,7},{7,6},{8,9},{9,8},{10,11... | collective-permute-start | bytes 6291464 | tf_op jit(solution)/shard_map/ppermute | solution.py:418
  147.8 1.3 assembled.2.refs_0_
  149.2 2.4 %collective-permute-done.7.ref = f32[4,2,32,8,256]{4,3,2,1,0:T(8,128)S(1)} collective-permute-done((f32[4,2,32,8,256]{4,3,2,1,0:T(8,128)S(1)}, f32[4,2,32,8,256]{4,3,2,1,0:T(8,128)S(1)}, u32[]{:S(2)}, u32[]{:S(2)}) %collective-permute-start.7) | collective-permute-done | bytes 2097184 | tf_op jit(solution)/shard_map/ppermute | solution.py:418
  151.6 1.3 assembled.3
  (2 shorter events, 0.0 us)
Async XLA Ops:
  0.0 10.6 %copy-start.5 = (s32[6]{0:T(128)S(1)}, s32[6]{0:T(128)}, u32[]{:S(2)}) copy-start(s32[6]{0:T(128)} %param.13) | copy-start | bytes 76
  0.0 10.6 %copy-start.6 = (s32[6]{0:T(128)S(1)}, s32[6]{0:T(128)}, u32[]{:S(2)}) copy-start(s32[6]{0:T(128)} %param.12) | copy-start | bytes 76
  0.0 43.5 %copy-start = (bf16[6,256,256]{2,1,0:T(8,128)(2,1)S(1)}, bf16[6,256,256]{2,1,0:T(8,128)(2,1)}, u32[]{:S(2)}) copy-start(bf16[6,256,256]{2,1,0:T(8,128)(2,1)} %amp_ref.1) | copy-start | bytes 2359300
  0.0 43.5 %copy-start.2 = (bf16[256,256]{1,0:T(8,128)(2,1)S(1)}, bf16[256,256]{1,0:T(8,128)(2,1)}, u32[]{:S(2)}) copy-start(bf16[256,256]{1,0:T(8,128)(2,1)} %constant.40.clone.turned_ref) | copy-start | bytes 393220
  0.0 43.5 %copy-start.3 = (bf16[256,256]{1,0:T(8,128)(2,1)S(1)}, bf16[256,256]{1,0:T(8,128)(2,1)}, u32[]{:S(2)}) copy-start(bf16[256,256]{1,0:T(8,128)(2,1)} %constant.39.clone.order_ref) | copy-start | bytes 393220
  1.7 44.0 %copy-start.1 = (f32[2,256,256]{2,1,0:T(8,128)S(1)}, f32[2,256,256]{2,1,0:T(8,128)}, u32[]{:S(2)}) copy-start(f32[2,256,256]{2,1,0:T(8,128)} %probe_ref.1) | copy-start | bytes 1572868
  1.7 44.0 %copy-start.4 = (bf16[16,256,256]{2,1,0:T(8,128)(2,1)S(1)}, bf16[16,256,256]{2,1,0:T(8,128)(2,1)}, u32[]{:S(2)}) copy-start(bf16[16,256,256]{2,1,0:T(8,128)(2,1)} %constant.41.clone.tab_hbm) | copy-start | bytes 6291460
  1.7 15.8 %collective-permute-start = (f32[2,32,8,256]{3,2,1,0:T(8,128)S(1)}, f32[2,32,8,256]{3,2,1,0:T(8,128)S(1)}, u32[]{:S(2)}, u32[]{:S(2)}) collective-permute-start(f32[2,32,8,256]{3,2,1,0:T(8,128)S(1)} %get-tuple-element.14), channel_id=1, source_target_pairs={{8,0},{16,8},{24,16},{32,24},{40,32},{48,40},{56,48},{64,56},{72,6... | collective-permute-start | bytes 1572872 | tf_op jit(solution)/shard_map/ppermute | solution.py:409
  7.0 32.9 %collective-permute-start.3 = (f32[2,2,32,8,256]{4,3,2,1,0:T(8,128)S(1)}, f32[2,2,32,8,256]{4,3,2,1,0:T(8,128)S(1)}, u32[]{:S(2)}, u32[]{:S(2)}) collective-permute-start(f32[2,2,32,8,256]{4,3,2,1,0:T(8,128)S(1)} %pad_maximum_fusion.1), channel_id=1, source_target_pairs={{8,0},{16,8},{24,16},{32,24},{40,32},{48,40},{56,48},{64,56},{72,6... | collective-permute-start | bytes 3145736 | tf_op jit(solution)/shard_map/ppermute | solution.py:409
  10.7 6.4 %collective-permute-start.1 = (s32[13]{0:T(128)S(1)}, s32[13]{0:T(128)S(1)}, u32[]{:S(2)}, u32[]{:S(2)}) collective-permute-start(s32[13]{0:T(128)S(1)} %pad_add_fusion), channel_id=1, source_target_pairs={{0,8},{8,16},{16,24},{24,32},{32,40},{40,48},{48,56},{56,64},{64,7... | collective-permute-start | bytes 164 | tf_op jit(solution)/shard_map/ppermute | solution.py:409
  17.5 13.8 %collective-permute-start.2 = (f32[2,32,8,256]{3,2,1,0:T(8,128)S(1)}, f32[2,32,8,256]{3,2,1,0:T(8,128)S(1)}, u32[]{:S(2)}, u32[]{:S(2)}) collective-permute-start(f32[2,32,8,256]{3,2,1,0:T(8,128)S(1)} %collective-permute-done), channel_id=1, source_target_pairs={{0,2},{1,3},{2,4},{3,5},{4,6},{5,7},{6,0},{7,1},{8,10},{9,11},{10,... | collective-permute-start | bytes 1572872 | tf_op jit(solution)/shard_map/ppermute | solution.py:414
  31.4 12.9 %collective-permute-start.4 = (f32[2,2,32,8,256]{4,3,2,1,0:T(8,128)S(1)}, f32[2,2,32,8,256]{4,3,2,1,0:T(8,128)S(1)}, u32[]{:S(2)}, u32[]{:S(2)}) collective-permute-start(f32[2,2,32,8,256]{4,3,2,1,0:T(8,128)S(1)} %pad_maximum_fusion.near_ref), channel_id=1, source_target_pairs={{0,1},{1,0},{2,3},{3,2},{4,5},{5,4},{6,7},{7,6},{8,9},{9,8},{10,11... | collective-permute-start | bytes 3145736 | tf_op jit(solution)/shard_map/ppermute | solution.py:418
  39.9 5.7 %collective-permute-start.5 = (f32[2,2,32,8,256]{4,3,2,1,0:T(8,128)S(1)}, f32[2,2,32,8,256]{4,3,2,1,0:T(8,128)S(1)}, u32[]{:S(2)}, u32[]{:S(2)}) collective-permute-start(f32[2,2,32,8,256]{4,3,2,1,0:T(8,128)S(1)} %collective-permute-done.3.far_ref), channel_id=1, source_target_pairs={{0,1},{1,0},{2,3},{3,2},{4,5},{5,4},{6,7},{7,6},{8,9},{9,8},{10,11... | collective-permute-start | bytes 3145736 | tf_op jit(solution)/shard_map/ppermute | solution.py:418
  99.1 16.7 %collective-permute-start.6 = (f32[2,256,256]{2,1,0:T(8,128)S(1)}, f32[2,256,256]{2,1,0:T(8,128)S(1)}, u32[]{:S(2)}, u32[]{:S(2)}) collective-permute-start(f32[2,256,256]{2,1,0:T(8,128)S(1)} %get-tuple-element.12), channel_id=1, source_target_pairs={{0,8},{8,16},{16,24},{24,32},{32,40},{40,48},{48,56},{56,64},{64,7... | collective-permute-start | bytes 1572872 | tf_op jit(solution)/shard_map/ppermute | solution.py:409
  143.4 8.2 %collective-permute-start.7 = (f32[4,2,32,8,256]{4,3,2,1,0:T(8,128)S(1)}, f32[4,2,32,8,256]{4,3,2,1,0:T(8,128)S(1)}, u32[]{:S(2)}, u32[]{:S(2)}) collective-permute-start(f32[4,2,32,8,256]{4,3,2,1,0:T(8,128)S(1)} %all_to_all.11.ref), channel_id=1, source_target_pairs={{0,1},{1,0},{2,3},{3,2},{4,5},{5,4},{6,7},{7,6},{8,9},{9,8},{10,11... | collective-permute-start | bytes 6291464 | tf_op jit(solution)/shard_map/ppermute | solution.py:418

commit v5 on v4

--- a/solution.py
+++ b/solution.py
@@ -84,7 +84,7 @@
     return index ^ 1 if other else index
 
 
-def patterns_kernel(size, rows, parts, slots, notes_ref, own_ref, probe_hbm, amp_hbm, tab_hbm, near_ref, far_ref, other_near_ref, other_far_ref, out_ref,
+def patterns_kernel(size, rows, parts, slots, notes_ref, own_ref, probe_hbm, amp_hbm, tab_hbm, near_ref, far_ref, other_near_ref, other_far_ref, re_ref, im_ref,
                     own_buf, rim_buf, probe_ref, amp_ref, tab_ref, stage, own_sems, fixed_sems, piece_sems, store_sems):
     count, group = notes_ref[0, 2 * slots], notes_ref[2, 0]
     span = size + SUB
@@ -104,9 +104,12 @@
             for n in range(2)
         ]
 
-    def store(p):
-        where = pl.ds(pl.multiple_of(p * 4 * depth, 4 * depth), 4 * depth)
-        return pltpu.make_async_copy(stage.at[:, where], out_ref.at[:, where], store_sems.at[p])
+    def stores(n):
+        where = pl.ds(pl.multiple_of(n * 2 * depth, 2 * depth), 2 * depth)
+        return [
+            pltpu.make_async_copy(stage.at[ch, :, where], ref.at[:, where], store_sems.at[ch, n])
+            for ch, ref in enumerate((re_ref, im_ref))
+        ]
 
     fixed = [
         pltpu.make_async_copy(a, b, fixed_sems.at[n])
@@ -129,9 +132,9 @@
             note = jnp.where(jnp.logical_and(head_row == side, lane == n), notes_ref[side, n], note)
     note = note.astype(jnp.float32)
     for part in range(parts):
-        stage[part, slots * 2 * depth :] = note
-    notes = pl.ds(slots * 2 * depth, SUB)
-    last = pltpu.make_async_copy(stage.at[:, notes], out_ref.at[:, notes], store_sems.at[slots])
+        stage[0, part, slots * depth :] = note
+    notes = pl.ds(slots * depth, SUB)
+    last = pltpu.make_async_copy(stage.at[0, :, notes], re_ref.at[:, notes], store_sems.at[0, slots])
     last.start()
     for copy in fixed + rims:
         copy.wait()
@@ -169,9 +172,9 @@
             for t in range(parts):
                 index = ((base >> 3) + t) & (parts - 1)
                 for m in range(depth // SUB):
-                    at = pl.multiple_of((2 * p + ch) * depth + SUB * m, SUB)
+                    at = pl.multiple_of(p * depth + SUB * m, SUB)
                     block = SUB * (parts * m + t)
-                    stage[index, pl.ds(at, SUB)] = g[block : block + SUB]
+                    stage[ch, index, pl.ds(at, SUB)] = g[block : block + SUB]
 
     def pair(n, _):
         first = 2 * n
@@ -196,14 +199,16 @@
         waves = [inverse(right, 1, *wave, tabs[3]) for wave in waves]
         for (p, _), state, wave in zip(work, states, waves):
             put(p, *state[:3], *wave)
-        store(n).start()
+        for copy in stores(n):
+            copy.start()
         return 0
 
     pairs = (count + 1) >> 1
     lax.fori_loop(0, pairs, pair, 0)
 
-    def stored(p, _):
-        store(p).wait()
+    def stored(n, _):
+        for copy in stores(n):
+            copy.wait()
         return 0
 
     last.wait()
@@ -237,27 +242,27 @@
     rows, size = own.shape[1:]
     slots, parts = amplitudes.shape[0], 2 * len(STEPS)
     depth = size // parts
-    length = slots * 2 * depth + SUB
+    length = slots * depth
     smem = pl.BlockSpec(memory_space=pltpu.SMEM)
     anywhere = pl.BlockSpec(memory_space=pl.ANY)
     hbm = pl.BlockSpec(memory_space=pltpu.HBM)
     tab = jnp.asarray(tables(size))
     return pl.pallas_call(
         functools.partial(patterns_kernel, size, rows, parts, slots),
-        out_shape=jax.ShapeDtypeStruct((parts, length, size), jnp.float32),
+        out_shape=[jax.ShapeDtypeStruct((parts, length + extra, size), jnp.float32) for extra in (SUB, 0)],
         in_specs=[smem] + [hbm] * 4 + [anywhere] * 4,
-        out_specs=anywhere,
+        out_specs=[anywhere] * 2,
         scratch_shapes=[
             pltpu.VMEM((4, 2, size + SUB, size), jnp.float32),
             pltpu.VMEM((2, rows // (SUB * parts), parts, SUB, size), jnp.float32),
             pltpu.VMEM(probe.shape, jnp.float32),
             pltpu.VMEM(amplitudes.shape, amplitudes.dtype),
             pltpu.VMEM(tab.shape, tab.dtype),
-            pltpu.VMEM((parts, length, size), jnp.float32),
+            pltpu.VMEM((2, parts, length + SUB, size), jnp.float32),
             pltpu.SemaphoreType.DMA((4,)),
             pltpu.SemaphoreType.DMA((3,)),
             pltpu.SemaphoreType.DMA((parts,)),
-            pltpu.SemaphoreType.DMA((slots + 1,)),
+            pltpu.SemaphoreType.DMA((2, slots + 1)),
         ],
         compiler_params=pltpu.CompilerParams(vmem_limit_bytes=40 * MIB),
         cost_estimate=pl.CostEstimate(flops=24 * 2 * size**3 * slots, bytes_accessed=12 * MIB, transcendentals=0),
@@ -293,34 +298,33 @@
     def step(d, p, row, col):
         _, at, shift = place(row, group, parts)
         mine = column >= col
-        for ch in range(2):
-            block = got_ref[d, pl.ds(pl.multiple_of((2 * p + ch) * depth, depth), depth)]
-            for side in range(2):
-                part = jnp.where(mine if side == 0 else jnp.logical_not(mine), block, 0.0)
-                head = part[:SUB]
-                total[side, ch, pl.ds(at, SUB)] += jnp.where(head_row >= shift, head, 0.0)
-                total[side, ch, pl.ds(at + SUB, depth - SUB)] += part[SUB:]
-                total[side, ch, pl.ds(at + depth, SUB)] += jnp.where(head_row < shift, head, 0.0)
+        block = got_ref[d, pl.ds(pl.multiple_of(p * depth, depth), depth)]
+        for side in range(2):
+            part = jnp.where(mine if side == 0 else jnp.logical_not(mine), block, 0.0)
+            head = part[:SUB]
+            total[side, pl.ds(at, SUB)] += jnp.where(head_row >= shift, head, 0.0)
+            total[side, pl.ds(at + SUB, depth - SUB)] += part[SUB:]
+            total[side, pl.ds(at + depth, SUB)] += jnp.where(head_row < shift, head, 0.0)
 
     each_live(notes_ref, slots, step)
-    kept = here_ref.shape[1]
-    here_ref[...] = total[0, :, :kept]
-    next_ref[...] = total[1, :, :kept]
+    kept = here_ref.shape[0]
+    here_ref[...] = total[0, :kept]
+    next_ref[...] = total[1, :kept]
 
 
 def gathered(group, notes, got, slots, kept):
-    parts, length, size = got.shape
+    parts, _, size = got.shape
     smem = pl.BlockSpec(memory_space=pltpu.SMEM)
     vmem = pl.BlockSpec(memory_space=pltpu.VMEM)
-    shape = jax.ShapeDtypeStruct((2, kept, size), jnp.float32)
+    shape = jax.ShapeDtypeStruct((kept, size), jnp.float32)
     return pl.pallas_call(
         functools.partial(gather_kernel, size, parts, slots),
         out_shape=(shape, shape),
         in_specs=[smem, smem, vmem],
         out_specs=(vmem, vmem),
-        scratch_shapes=[pltpu.VMEM((2, 2, kept + SUB, size), jnp.float32)],
-        compiler_params=pltpu.CompilerParams(vmem_limit_bytes=24 * MIB),
-        cost_estimate=pl.CostEstimate(flops=2**22, bytes_accessed=6 * MIB, transcendentals=0),
+        scratch_shapes=[pltpu.VMEM((2, kept + SUB, size), jnp.float32)],
+        compiler_params=pltpu.CompilerParams(vmem_limit_bytes=8 * MIB),
+        cost_estimate=pl.CostEstimate(flops=2**21, bytes_accessed=3 * MIB, transcendentals=0),
         name="gathered",
     )(group, notes, got)
 
@@ -370,37 +374,51 @@
             pltpu.VMEM((size + SUB, size), jnp.float32),
             pltpu.VMEM((kept + SUB, size), jnp.float32),
         ],
-        compiler_params=pltpu.CompilerParams(vmem_limit_bytes=16 * MIB),
+        compiler_params=pltpu.CompilerParams(vmem_limit_bytes=4 * MIB),
         cost_estimate=pl.CostEstimate(flops=2**22, bytes_accessed=8 * MIB, transcendentals=0),
         name="illumination",
     )(group, here, before, probe)
 
 
-def assemble_kernel(other, parts, group_ref, ref, *refs):
-    out_ref, sems = refs[-2:]
-    core = (group_ref[0] & 1) ^ other
-    copies = [pltpu.make_async_copy(ref.at[n], out_ref.at[:, :, 2 * n + core], sems.at[n]) for n in range(parts // 2)]
-    for copy in copies:
-        copy.start()
+def assemble_kernel(kinds, parts, staged, group_ref, *refs):
+    sources = list(refs[: len(kinds)])
+    if staged:
+        out_ref, held, load_sems, sems = refs[-4:]
+        loads = [pltpu.make_async_copy(ref, held.at[n], load_sems.at[n]) for n, ref in enumerate(sources)]
+        sources = [held.at[n] for n in range(len(kinds))]
+    else:
+        (out_ref, sems), loads = refs[-2:], []
+    for load in loads:
+        load.start()
+    copies = []
+    for k, (ch, other) in enumerate(kinds):
+        core = (group_ref[0] & 1) ^ other
+        if loads:
+            loads[k].wait()
+        for n in range(parts // 2):
+            copies.append(pltpu.make_async_copy(sources[k].at[n], out_ref.at[ch, :, 2 * n + core], sems.at[len(copies)]))
+            copies[-1].start()
     for copy in copies:
         copy.wait()
 
 
-def assembled(group, other, shares, shape, begun=()):
+def assembled(group, kinds, shares, shape, begun=(), staged=True):
     parts = shape[2]
     anywhere = pl.BlockSpec(memory_space=pl.ANY)
     hbm = pl.BlockSpec(memory_space=pltpu.HBM)
+    count = len(shares)
+    held = [pltpu.VMEM((count, *shares[0].shape), jnp.float32), pltpu.SemaphoreType.DMA((count,))] if staged else []
     return pl.pallas_call(
-        functools.partial(assemble_kernel, other, parts),
+        functools.partial(assemble_kernel, kinds, parts, staged),
         out_shape=jax.ShapeDtypeStruct(shape, jnp.float32),
-        in_specs=[pl.BlockSpec(memory_space=pltpu.SMEM), anywhere] + [hbm] * len(begun),
+        in_specs=[pl.BlockSpec(memory_space=pltpu.SMEM)] + [anywhere] * count + [hbm] * len(begun),
         out_specs=hbm,
-        scratch_shapes=[pltpu.SemaphoreType.DMA((parts // 2,))],
-        input_output_aliases={2: 0} if begun else {},
-        compiler_params=pltpu.CompilerParams(vmem_limit_bytes=MIB),
-        cost_estimate=pl.CostEstimate(flops=0, bytes_accessed=4 * MIB, transcendentals=0),
+        scratch_shapes=held + [pltpu.SemaphoreType.DMA((count * parts // 2,))],
+        input_output_aliases={1 + count: 0} if begun else {},
+        compiler_params=pltpu.CompilerParams(vmem_limit_bytes=5 * MIB if staged else MIB),
+        cost_estimate=pl.CostEstimate(flops=0, bytes_accessed=2 * count * MIB, transcendentals=0),
         name="assembled",
-    )(group, shares, *begun)
+    )(group, *shares, *begun)
 
 
 def passed_along(x, axis, by):
@@ -427,29 +445,36 @@
     kept = rows // parts
     blocks = object_field.reshape(2, kept // SUB, parts, SUB, size)
 
-    def share(which):
-        return lax.dynamic_index_in_dim(blocks, which, 2, keepdims=False)
-
-    mine = share(index)
+    def cut(source, which):
+        return lax.dynamic_index_in_dim(source, which, 2, keepdims=False)
+
     own_notes = jnp.concatenate([row_offset, col_offset, counts])
-    far = passed_along(jnp.stack([share((index + 4) % parts), share((index + 2) % parts)]), "tile", -1)
-    near, notes_before = lax.optimization_barrier((passed_along(mine, "tile", -1), passed_along(own_notes, "tile", 1)))
+    far = passed_along(jnp.stack([cut(blocks, (index + 4) % parts), cut(blocks, (index + 2) % parts)]), "tile", -1)
+    near, notes_before = lax.optimization_barrier((passed_along(cut(blocks, index), "tile", -1), passed_along(own_notes, "tile", 1)))
     near = jnp.stack([near, to_chip(near, 1)])
     notes = jnp.stack([own_notes, notes_before, jnp.full_like(own_notes, index)])
     sent = patterns(notes, object_field, (near, far, to_core(near), to_core(far)), probe, ordered(amplitudes))
-    got = lax.all_to_all(sent, "group", 0, 0)
-    notes = got[:, slots * 2 * (size // parts) :, : 2 * slots + 1].astype(jnp.int32)
+    blocks, first = lax.optimization_barrier((blocks, sent[0]))
+    sent = (first, sent[1])
+    mine = cut(blocks, index)
+    gots = [lax.all_to_all(channel, "group", 0, 0) for channel in sent]
+    notes = gots[0][:, slots * (size // parts) :, : 2 * slots + 1].astype(jnp.int32)
     notes_here, notes_before = notes[:, 0], notes[:, 1]
-    here, spill = gathered(group, notes_here, got, slots, kept)
-    spill = passed_along(spill, "tile", 1)
     weight = illumination(group, notes_here, notes_before, probe, slots, kept)
-    result = mine + ((here + spill) / weight).reshape(mine.shape)
     chips = parts // 2
     same_core = [list(range(core, parts, 2)) for core in range(2)]
-    spread = jnp.broadcast_to(result, (chips, *result.shape))
-    shares = lax.all_to_all(spread, "group", 0, 0, axis_index_groups=same_core)
-    field = assembled(group, 0, shares, blocks.shape)
-    field = assembled(group, 1, to_core(shares), blocks.shape, (field,))
+    spreads = []
+    for ch, got in enumerate(gots):
+        here, spill = gathered(group, notes_here, got, slots, kept)
+        spill = passed_along(spill, "tile", 1)
+        if spreads:
+            spill, _ = lax.optimization_barrier((spill, spreads[0]))
+        result = mine[ch] + ((here + spill) / weight).reshape(mine.shape[1:])
+        spreads.append(jnp.broadcast_to(result, (chips, *result.shape)))
+    shares = [lax.all_to_all(spread, "group", 0, 0, axis_index_groups=same_core) for spread in spreads]
+    others = [to_core(share) for share in shares]
+    field = assembled(group, ((0, 0), (1, 0), (0, 1)), (*shares, others[0]), blocks.shape)
+    field = assembled(group, ((1, 1),), (others[1],), blocks.shape, (field,), staged=False)
     return field.reshape(object_field.shape)
 
 

time: 155 us -> 154 us (level)
  blocking collectives: 74.9 us -> 30.5 us
  starting transfers between devices: 28.9 us -> 47.2 us
  waiting for transfers between devices: 32.5 us -> 48.9 us
  Pallas kernels: 13.4 us -> 16.6 us
  local copies, waits for them, and re-layouts: 1.91 us -> 4.96 us
  other arithmetic: 0.52 us -> 2.44 us
    all_to_all x2 -> x1, blocking collectives: 74.9 us -> 30.5 us  [body(): gots = [lax.all_to_all(channel, 'group', 0, 0) for channel in sent]]
    all_to_all x0 -> x3, waiting for transfers between devices: none -> 14.6 us  [the longest x2 9.12 us: body(): lax.all_to_all(spread, 'group', 0, 0, axis_index_groups=same_core)]
    all_to_all x0 -> x3, starting transfers between devices: none -> 11.6 us  [the longest x2 7.4 us: body(): lax.all_to_all(spread, 'group', 0, 0, axis_index_groups=same_core)]
    ppermute x3 -> x4, starting transfers between devices: 13.4 us -> 17.8 us  [to_core(): lax.ppermute(x, 'group', [(i, i ^ 1) for i in range(lax.axis_size('group'...]
    ppermute x4 -> x5, waiting for transfers between devices: 18 us -> 22.2 us  [passed_along(): return lax.ppermute(x, axis, pairs)]
    ppermute x3 -> x4, waiting for transfers between devices: 3.76 us -> 1.35 us  [to_core(): lax.ppermute(x, 'group', [(i, i ^ 1) for i in range(lax.axis_size('group'...]
    ppermute x4 -> x5, starting transfers between devices: 12.4 us -> 14.7 us  [passed_along(): return lax.ppermute(x, axis, pairs)]
    broadcast_in_dim x1 -> x2, local copies, waits for them, and re-layouts: 0.18 us -> 2.1 us  [body(): spreads.append(jnp.broadcast_to(result, (chips, *result.shape)))]
  transfers between devices with their start and end apart: 8 -> 13, of which waited for: 7 -> 9; matrix products, arithmetic and copies ran while one was open for 0% -> 2% of each run, Pallas kernels for 4% -> 7%
where the time goes in v5:
time: 154 us; the launch traced here: 152 us
  waiting for transfers between devices  48.9 us (32%)
  starting transfers between devices  47.2 us (31%)
  blocking collectives  30.5 us (20%)
  Pallas kernels  16.6 us (11%)
  local copies, waits for them, and re-layouts  4.96 us (3%)
  other arithmetic  2.44 us (2%)
    all_to_all x1, blocking collectives, body(): gots = [lax.all_to_all(channel, 'group', 0, 0) for channel in sent]  30.5 us
    ppermute x5, waiting for transfers between devices, passed_along(): return lax.ppermute(x, axis, pairs)  22.2 us
    ppermute x4, starting transfers between devices, to_core(): lax.ppermute(x, 'group', [(i, i ^ 1) for i in range(lax.axis_size('group'...  17.8 us
    ppermute x5, starting transfers between devices, passed_along(): return lax.ppermute(x, axis, pairs)  14.7 us
    ppermute x1, waiting for transfers between devices, to_chip(): lax.ppermute(x, 'group', [(i, (i + 2 * by) % devices) for i in range(devi...  10.7 us
    all_to_all x2, waiting for transfers between devices, body(): lax.all_to_all(spread, 'group', 0, 0, axis_index_groups=same_core)  9.12 us
    all_to_all x2, starting transfers between devices, body(): lax.all_to_all(spread, 'group', 0, 0, axis_index_groups=same_core)  7.4 us
    all_to_all x1, waiting for transfers between devices, body(): gots = [lax.all_to_all(channel, 'group', 0, 0) for channel in sent]  5.51 us
  transfers between devices with their start and end apart: 13, of which 9 were waited for; matrix products, arithmetic and copies ran while one was open for 2% of the time, Pallas kernels for 7%

profile of v5, /device:TPU:449, one launch (start us, length us, event | category | flops | bytes accessed | tf_op | source)
XLA Modules:
  0.0 151.6 jit_solution(1162433487157912129)
XLA Ops:
  0.1 0.0 copy-start.2
  0.1 0.0 copy-start.6
  0.1 1.7 %dynamic-slice_bitcast_fusion.1 = (f32[1,2,32,8,256]{4,3,2,1,0:T(8,128)S(1)}, f32[2,32,8,256]{3,2,1,0:T(8,128)S(1)}, f32[1,2,32,8,256]{4,3,2,1,0:T(8,128)S(1)}) fusion(f32[2,32,8,8,256]{4,3,2,1,0:T(8,128)} %bitcast.39, s32[]{:T(128)S(6)} %select_n.24, s32[]{:T(128)S(6)} %select_n.22, s32[]{:T(128)S(6)} %select_n.26), kind=kLoop, calls=%fused_computation.3 | loop fusion | bytes 3145740 | tf_op jit(solution)/shard_map/stack | solution.py:452
  1.8 5.1 %collective-permute-start = (f32[2,32,8,256]{3,2,1,0:T(8,128)S(1)}, f32[2,32,8,256]{3,2,1,0:T(8,128)S(1)}, u32[]{:S(2)}, u32[]{:S(2)}) collective-permute-start(f32[2,32,8,256]{3,2,1,0:T(8,128)S(1)} %get-tuple-element.28), channel_id=1, source_target_pairs={{8,0},{16,8},{24,16},{32,24},{40,32},{48,40},{56,48},{64,56},{72,6... | collective-permute-start | bytes 1572872 | tf_op jit(solution)/shard_map/ppermute | solution.py:427
  6.9 0.1 pad_maximum_fusion.1
  7.0 3.0 %collective-permute-start.3 = (f32[2,2,32,8,256]{4,3,2,1,0:T(8,128)S(1)}, f32[2,2,32,8,256]{4,3,2,1,0:T(8,128)S(1)}, u32[]{:S(2)}, u32[]{:S(2)}) collective-permute-start(f32[2,2,32,8,256]{4,3,2,1,0:T(8,128)S(1)} %pad_maximum_fusion.1), channel_id=1, source_target_pairs={{8,0},{16,8},{24,16},{32,24},{40,32},{48,40},{56,48},{64,56},{72,6... | collective-permute-start | bytes 3145736 | tf_op jit(solution)/shard_map/ppermute | solution.py:427
  10.6 0.1 pad_add_fusion
  10.7 2.3 %collective-permute-start.1 = (s32[13]{0:T(128)S(1)}, s32[13]{0:T(128)S(1)}, u32[]{:S(2)}, u32[]{:S(2)}) collective-permute-start(s32[13]{0:T(128)S(1)} %pad_add_fusion), channel_id=1, source_target_pairs={{0,8},{8,16},{16,24},{24,32},{32,40},{40,48},{48,56},{56,64},{64,7... | collective-permute-start | bytes 164 | tf_op jit(solution)/shard_map/ppermute | solution.py:427
  13.0 4.1 %collective-permute-done.1 = s32[13]{0:T(128)S(1)} collective-permute-done((s32[13]{0:T(128)S(1)}, s32[13]{0:T(128)S(1)}, u32[]{:S(2)}, u32[]{:S(2)}) %collective-permute-start.1) | collective-permute-done | bytes 84 | tf_op jit(solution)/shard_map/ppermute | solution.py:427
  17.1 0.4 collective-permute-done
  17.5 3.1 %collective-permute-start.2 = (f32[2,32,8,256]{3,2,1,0:T(8,128)S(1)}, f32[2,32,8,256]{3,2,1,0:T(8,128)S(1)}, u32[]{:S(2)}, u32[]{:S(2)}) collective-permute-start(f32[2,32,8,256]{3,2,1,0:T(8,128)S(1)} %collective-permute-done), channel_id=1, source_target_pairs={{0,2},{1,3},{2,4},{3,5},{4,6},{5,7},{6,0},{7,1},{8,10},{9,11},{10,... | collective-permute-start | bytes 1572872 | tf_op jit(solution)/shard_map/ppermute | solution.py:432
  20.6 10.7 %collective-permute-done.2 = f32[2,32,8,256]{3,2,1,0:T(8,128)S(1)} collective-permute-done((f32[2,32,8,256]{3,2,1,0:T(8,128)S(1)}, f32[2,32,8,256]{3,2,1,0:T(8,128)S(1)}, u32[]{:S(2)}, u32[]{:S(2)}) %collective-permute-start.2) | collective-permute-done | bytes 524320 | tf_op jit(solution)/shard_map/ppermute | solution.py:432
  31.3 0.1 pad_maximum_fusion.near_ref
  31.4 5.5 %collective-permute-start.4 = (f32[2,2,32,8,256]{4,3,2,1,0:T(8,128)S(1)}, f32[2,2,32,8,256]{4,3,2,1,0:T(8,128)S(1)}, u32[]{:S(2)}, u32[]{:S(2)}) collective-permute-start(f32[2,2,32,8,256]{4,3,2,1,0:T(8,128)S(1)} %pad_maximum_fusion.near_ref), channel_id=1, source_target_pairs={{0,1},{1,0},{2,3},{3,2},{4,5},{5,4},{6,7},{7,6},{8,9},{9,8},{10,11... | collective-permute-start | bytes 3145736 | tf_op jit(solution)/shard_map/ppermute | solution.py:436
  36.9 3.0 %collective-permute-done.3.far_ref = f32[2,2,32,8,256]{4,3,2,1,0:T(8,128)S(1)} collective-permute-done((f32[2,2,32,8,256]{4,3,2,1,0:T(8,128)S(1)}, f32[2,2,32,8,256]{4,3,2,1,0:T(8,128)S(1)}, u32[]{:S(2)}, u32[]{:S(2)}) %collective-permute-start.3) | collective-permute-done | bytes 1048608 | tf_op jit(solution)/shard_map/ppermute | solution.py:427
  39.9 3.4 %collective-permute-start.5 = (f32[2,2,32,8,256]{4,3,2,1,0:T(8,128)S(1)}, f32[2,2,32,8,256]{4,3,2,1,0:T(8,128)S(1)}, u32[]{:S(2)}, u32[]{:S(2)}) collective-permute-start(f32[2,2,32,8,256]{4,3,2,1,0:T(8,128)S(1)} %collective-permute-done.3.far_ref), channel_id=1, source_target_pairs={{0,1},{1,0},{2,3},{3,2},{4,5},{5,4},{6,7},{7,6},{8,9},{9,8},{10,11... | collective-permute-start | bytes 3145736 | tf_op jit(solution)/shard_map/ppermute | solution.py:436
  43.4 0.1 pad.6.clone
  43.5 0.7 ordered.1.amp_hbm
  44.1 0.1 fusion.3
  44.2 0.1 add_add_fusion.notes_ref
  44.3 1.3 collective-permute-done.5.other_far_ref
  45.6 4.3 %patterns.1 = (f32[8,200,256]{2,1,0:T(8,128)S(1)}, f32[8,192,256]{2,1,0:T(8,128)S(1)}) custom-call(s32[3,13]{1,0:T(4,128)S(1)} %add_add_fusion.notes_ref, f32[2,2048,256]{2,1,0:T(8,128)} %own_ref.1, f32[2,256,256]{2,1,0:T(8,128)S(1)} %copy-done.2, bf16[6,256,256]{2,1,0:T(8,128)(2,1)S(1)} %ordered.1.amp_hbm, bf16[16,256,256]{2,1,0:T(8,128)(2,1)S(1)} %copy-done.6, ...), custom_call_target="tpu_custom_call" | custom-call | flops 4831838208 | bytes 12582912 | tf_op jit(solution)/shard_map/patterns/pallas_call | solution.py:250
  49.9 0.0 copy-start
  50.0 30.5 %all_to_all.20.got_ref = f32[8,200,256]{2,1,0:T(8,128)S(1)} all-to-all(f32[8,200,256]{2,1,0:T(8,128)S(1)} %get-tuple-element.20), channel_id=1, replica_groups=mesh['tile'=64,'group'=8] {'group'}, dimensions={0} | all-to-all | bytes 3276800 | tf_op jit(solution)/shard_map/all_to_all | solution.py:460
  80.5 4.2 %all-to-all-start.1 = ((f32[8,192,256]{2,1,0:T(8,128)}), f32[8,192,256]{2,1,0:T(8,128)S(1)}, u32[]{:S(2)}, u32[]{:S(2)}) async-start(f32[8,192,256]{2,1,0:T(8,128)} %copy-done), calls=%async_computation.1 | async-start | bytes 3145728 | tf_op jit(solution)/shard_map/all_to_all | solution.py:460
  84.7 1.3 gathered.3
  86.1 2.2 %collective-permute-start.7 = (f32[256,256]{1,0:T(8,128)S(1)}, f32[256,256]{1,0:T(8,128)S(1)}, u32[]{:S(2)}, u32[]{:S(2)}) collective-permute-start(f32[256,256]{1,0:T(8,128)S(1)} %get-tuple-element.25), channel_id=1, source_target_pairs={{0,8},{8,16},{16,24},{24,32},{32,40},{40,48},{48,56},{56,64},{64,7... | collective-permute-start | bytes 786440 | tf_op jit(solution)/shard_map/ppermute | solution.py:427
  88.2 0.0 copy-start.3
  88.3 1.0 copy-done.3
  89.3 4.8 %illumination.1 = f32[256,256]{1,0:T(8,128)S(1)} custom-call(s32[1]{0:T(128)} %bitcast.group_ref, s32[8,13]{1,0:T(8,128)S(1)} %bitcast.36, s32[8,13]{1,0:T(8,128)S(1)} %bitcast.38, f32[2,256,256]{2,1,0:T(8,128)S(1)} %copy-done.3), custom_call_target="tpu_custom_call" | custom-call | flops 4194304 | bytes 8388608 | tf_op jit(solution)/shard_map/illumination/pallas_call | solution.py:368
  94.1 4.8 %collective-permute-done.7 = f32[256,256]{1,0:T(8,128)S(1)} collective-permute-done((f32[256,256]{1,0:T(8,128)S(1)}, f32[256,256]{1,0:T(8,128)S(1)}, u32[]{:S(2)}, u32[]{:S(2)}) %collective-permute-start.7) | collective-permute-done | bytes 262176 | tf_op jit(solution)/shard_map/ppermute | solution.py:427
  98.9 1.0 fusion
  99.9 5.5 %all-to-all-done.1.got_ref = f32[8,192,256]{2,1,0:T(8,128)S(1)} async-done(((f32[8,192,256]{2,1,0:T(8,128)}), f32[8,192,256]{2,1,0:T(8,128)S(1)}, u32[]{:S(2)}, u32[]{:S(2)}) %all-to-all-start.1) | async-done | bytes 1572896 | tf_op jit(solution)/shard_map/all_to_all | solution.py:460
  105.5 1.1 broadcast_in_dim.10
  106.5 3.5 %all-to-all-start.3 = ((f32[4,32,8,256]{3,2,1,0:T(8,128)}), f32[4,32,8,256]{3,2,1,0:T(8,128)S(1)}, u32[]{:S(2)}, u32[]{:S(2)}) async-start(f32[4,32,8,256]{3,2,1,0:T(8,128)} %broadcast_in_dim.10), calls=%async_computation.3 | async-start | bytes 2097152 | tf_op jit(solution)/shard_map/all_to_all | solution.py:474
  110.0 1.3 gathered.2
  111.3 2.2 %collective-permute-start.6 = (f32[256,256]{1,0:T(8,128)S(1)}, f32[256,256]{1,0:T(8,128)S(1)}, u32[]{:S(2)}, u32[]{:S(2)}) collective-permute-start(f32[256,256]{1,0:T(8,128)S(1)} %get-tuple-element.23), channel_id=1, source_target_pairs={{0,8},{8,16},{16,24},{24,32},{32,40},{40,48},{48,56},{56,64},{64,7... | collective-permute-start | bytes 786440 | tf_op jit(solution)/shard_map/ppermute | solution.py:427
  113.5 9.9 %collective-permute-done.6 = f32[256,256]{1,0:T(8,128)S(1)} collective-permute-done((f32[256,256]{1,0:T(8,128)S(1)}, f32[256,256]{1,0:T(8,128)S(1)}, u32[]{:S(2)}, u32[]{:S(2)}) %collective-permute-start.6) | collective-permute-done | bytes 262176 | tf_op jit(solution)/shard_map/ppermute | solution.py:427
  123.4 1.0 fusion.1
  124.5 1.1 broadcast_in_dim.11
  125.5 3.9 %all-to-all-start.2 = ((f32[4,32,8,256]{3,2,1,0:T(8,128)}), f32[4,32,8,256]{3,2,1,0:T(8,128)S(1)}, u32[]{:S(2)}, u32[]{:S(2)}) async-start(f32[4,32,8,256]{3,2,1,0:T(8,128)} %broadcast_in_dim.11), calls=%async_computation.2 | async-start | bytes 2097152 | tf_op jit(solution)/shard_map/all_to_all | solution.py:474
  129.4 3.9 %collective-permute-start.9 = (f32[4,32,8,256]{3,2,1,0:T(8,128)S(1)}, f32[4,32,8,256]{3,2,1,0:T(8,128)}, u32[]{:S(2)}, u32[]{:S(2)}) collective-permute-start(f32[4,32,8,256]{3,2,1,0:T(8,128)S(1)} %all-to-all-done.3.refs_0_), channel_id=1, source_target_pairs={{0,1},{1,0},{2,3},{3,2},{4,5},{5,4},{6,7},{7,6},{8,9},{9,8},{10,11... | collective-permute-start | bytes 3145736 | tf_op jit(solution)/shard_map/ppermute | solution.py:436
  133.4 9.1 %all-to-all-done.2.refs_1_ = f32[4,32,8,256]{3,2,1,0:T(8,128)S(1)} async-done(((f32[4,32,8,256]{3,2,1,0:T(8,128)}), f32[4,32,8,256]{3,2,1,0:T(8,128)S(1)}, u32[]{:S(2)}, u32[]{:S(2)}) %all-to-all-start.2) | async-done | bytes 1048608 | tf_op jit(solution)/shard_map/all_to_all | solution.py:474
  142.5 4.9 %collective-permute-start.8 = (f32[4,32,8,256]{3,2,1,0:T(8,128)S(1)}, f32[4,32,8,256]{3,2,1,0:T(8,128)S(1)}, u32[]{:S(2)}, u32[]{:S(2)}) collective-permute-start(f32[4,32,8,256]{3,2,1,0:T(8,128)S(1)} %all-to-all-done.2.refs_1_), channel_id=1, source_target_pairs={{0,1},{1,0},{2,3},{3,2},{4,5},{5,4},{6,7},{7,6},{8,9},{9,8},{10,11... | collective-permute-start | bytes 3145736 | tf_op jit(solution)/shard_map/ppermute | solution.py:436
  147.4 0.0 collective-permute-done.9.refs_2_
  147.4 3.2 %assembled.2.refs_1_ = f32[2,32,8,8,256]{4,3,2,1,0:T(8,128)} custom-call(s32[1]{0:T(128)} %bitcast.group_ref, f32[4,32,8,256]{3,2,1,0:T(8,128)S(1)} %all-to-all-done.3.refs_0_, f32[4,32,8,256]{3,2,1,0:T(8,128)S(1)} %all-to-all-done.2.refs_1_, f32[4,32,8,256]{3,2,1,0:T(8,128)} %collective-permute-done.9.refs_2_), custom_call_target="tpu_custom_call" | custom-call | bytes 6291456 | tf_op jit(solution)/shard_map/assembled/pallas_call | solution.py:411
  150.6 0.0 collective-permute-done.8.refs_0_
  150.6 1.0 assembled.3
  (17 shorter events, 0.0 us)
Async XLA Ops:
  0.0 43.5 %copy-start.4 = (bf16[256,256]{1,0:T(8,128)(2,1)S(1)}, bf16[256,256]{1,0:T(8,128)(2,1)}, u32[]{:S(2)}) copy-start(bf16[256,256]{1,0:T(8,128)(2,1)} %constant.42.clone.turned_ref) | copy-start | bytes 393220
  0.0 43.5 %copy-start.5 = (bf16[256,256]{1,0:T(8,128)(2,1)S(1)}, bf16[256,256]{1,0:T(8,128)(2,1)}, u32[]{:S(2)}) copy-start(bf16[256,256]{1,0:T(8,128)(2,1)} %constant.41.clone.order_ref) | copy-start | bytes 393220
  0.0 10.6 %copy-start.7 = (s32[6]{0:T(128)S(1)}, s32[6]{0:T(128)}, u32[]{:S(2)}) copy-start(s32[6]{0:T(128)} %param.13) | copy-start | bytes 76
  0.0 10.6 %copy-start.8 = (s32[6]{0:T(128)S(1)}, s32[6]{0:T(128)}, u32[]{:S(2)}) copy-start(s32[6]{0:T(128)} %param.12) | copy-start | bytes 76
  0.0 43.4 %copy-start.1 = (bf16[6,256,256]{2,1,0:T(8,128)(2,1)S(1)}, bf16[6,256,256]{2,1,0:T(8,128)(2,1)}, u32[]{:S(2)}) copy-start(bf16[6,256,256]{2,1,0:T(8,128)(2,1)} %amp_ref.1) | copy-start | bytes 2359300
  0.1 45.6 %copy-start.2 = (f32[2,256,256]{2,1,0:T(8,128)S(1)}, f32[2,256,256]{2,1,0:T(8,128)}, u32[]{:S(2)}) copy-start(f32[2,256,256]{2,1,0:T(8,128)} %probe_ref.1) | copy-start | bytes 1572868
  0.1 45.6 %copy-start.6 = (bf16[16,256,256]{2,1,0:T(8,128)(2,1)S(1)}, bf16[16,256,256]{2,1,0:T(8,128)(2,1)}, u32[]{:S(2)}) copy-start(bf16[16,256,256]{2,1,0:T(8,128)(2,1)} %constant.43.clone.tab_hbm) | copy-start | bytes 6291460
  1.8 15.7 %collective-permute-start = (f32[2,32,8,256]{3,2,1,0:T(8,128)S(1)}, f32[2,32,8,256]{3,2,1,0:T(8,128)S(1)}, u32[]{:S(2)}, u32[]{:S(2)}) collective-permute-start(f32[2,32,8,256]{3,2,1,0:T(8,128)S(1)} %get-tuple-element.28), channel_id=1, source_target_pairs={{8,0},{16,8},{24,16},{32,24},{40,32},{48,40},{56,48},{64,56},{72,6... | collective-permute-start | bytes 1572872 | tf_op jit(solution)/shard_map/ppermute | solution.py:427
  7.0 32.9 %collective-permute-start.3 = (f32[2,2,32,8,256]{4,3,2,1,0:T(8,128)S(1)}, f32[2,2,32,8,256]{4,3,2,1,0:T(8,128)S(1)}, u32[]{:S(2)}, u32[]{:S(2)}) collective-permute-start(f32[2,2,32,8,256]{4,3,2,1,0:T(8,128)S(1)} %pad_maximum_fusion.1), channel_id=1, source_target_pairs={{8,0},{16,8},{24,16},{32,24},{40,32},{48,40},{56,48},{64,56},{72,6... | collective-permute-start | bytes 3145736 | tf_op jit(solution)/shard_map/ppermute | solution.py:427
  10.7 6.4 %collective-permute-start.1 = (s32[13]{0:T(128)S(1)}, s32[13]{0:T(128)S(1)}, u32[]{:S(2)}, u32[]{:S(2)}) collective-permute-start(s32[13]{0:T(128)S(1)} %pad_add_fusion), channel_id=1, source_target_pairs={{0,8},{8,16},{16,24},{24,32},{32,40},{40,48},{48,56},{56,64},{64,7... | collective-permute-start | bytes 164 | tf_op jit(solution)/shard_map/ppermute | solution.py:427
  17.5 13.8 %collective-permute-start.2 = (f32[2,32,8,256]{3,2,1,0:T(8,128)S(1)}, f32[2,32,8,256]{3,2,1,0:T(8,128)S(1)}, u32[]{:S(2)}, u32[]{:S(2)}) collective-permute-start(f32[2,32,8,256]{3,2,1,0:T(8,128)S(1)} %collective-permute-done), channel_id=1, source_target_pairs={{0,2},{1,3},{2,4},{3,5},{4,6},{5,7},{6,0},{7,1},{8,10},{9,11},{10,... | collective-permute-start | bytes 1572872 | tf_op jit(solution)/shard_map/ppermute | solution.py:432
  31.4 12.9 %collective-permute-start.4 = (f32[2,2,32,8,256]{4,3,2,1,0:T(8,128)S(1)}, f32[2,2,32,8,256]{4,3,2,1,0:T(8,128)S(1)}, u32[]{:S(2)}, u32[]{:S(2)}) collective-permute-start(f32[2,2,32,8,256]{4,3,2,1,0:T(8,128)S(1)} %pad_maximum_fusion.near_ref), channel_id=1, source_target_pairs={{0,1},{1,0},{2,3},{3,2},{4,5},{5,4},{6,7},{7,6},{8,9},{9,8},{10,11... | collective-permute-start | bytes 3145736 | tf_op jit(solution)/shard_map/ppermute | solution.py:436
  39.9 5.7 %collective-permute-start.5 = (f32[2,2,32,8,256]{4,3,2,1,0:T(8,128)S(1)}, f32[2,2,32,8,256]{4,3,2,1,0:T(8,128)S(1)}, u32[]{:S(2)}, u32[]{:S(2)}) collective-permute-start(f32[2,2,32,8,256]{4,3,2,1,0:T(8,128)S(1)} %collective-permute-done.3.far_ref), channel_id=1, source_target_pairs={{0,1},{1,0},{2,3},{3,2},{4,5},{5,4},{6,7},{7,6},{8,9},{9,8},{10,11... | collective-permute-start | bytes 3145736 | tf_op jit(solution)/shard_map/ppermute | solution.py:436
  49.9 30.5 %copy-start = (f32[8,192,256]{2,1,0:T(8,128)}, f32[8,192,256]{2,1,0:T(8,128)S(1)}, u32[]{:S(2)}) copy-start(f32[8,192,256]{2,1,0:T(8,128)S(1)} %get-tuple-element.21) | copy-start | bytes 4718596
  80.5 25.0 %all-to-all-start.1 = ((f32[8,192,256]{2,1,0:T(8,128)}), f32[8,192,256]{2,1,0:T(8,128)S(1)}, u32[]{:S(2)}, u32[]{:S(2)}) async-start(f32[8,192,256]{2,1,0:T(8,128)} %copy-done), calls=%async_computation.1 | async-start | bytes 3145728 | tf_op jit(solution)/shard_map/all_to_all | solution.py:460
  86.1 12.8 %collective-permute-start.7 = (f32[256,256]{1,0:T(8,128)S(1)}, f32[256,256]{1,0:T(8,128)S(1)}, u32[]{:S(2)}, u32[]{:S(2)}) collective-permute-start(f32[256,256]{1,0:T(8,128)S(1)} %get-tuple-element.25), channel_id=1, source_target_pairs={{0,8},{8,16},{16,24},{24,32},{32,40},{40,48},{48,56},{56,64},{64,7... | collective-permute-start | bytes 786440 | tf_op jit(solution)/shard_map/ppermute | solution.py:427
  88.2 1.0 copy-start.3
  106.5 18.0 %all-to-all-start.3 = ((f32[4,32,8,256]{3,2,1,0:T(8,128)}), f32[4,32,8,256]{3,2,1,0:T(8,128)S(1)}, u32[]{:S(2)}, u32[]{:S(2)}) async-start(f32[4,32,8,256]{3,2,1,0:T(8,128)} %broadcast_in_dim.10), calls=%async_computation.3 | async-start | bytes 2097152 | tf_op jit(solution)/shard_map/all_to_all | solution.py:474
  111.3 12.1 %collective-permute-start.6 = (f32[256,256]{1,0:T(8,128)S(1)}, f32[256,256]{1,0:T(8,128)S(1)}, u32[]{:S(2)}, u32[]{:S(2)}) collective-permute-start(f32[256,256]{1,0:T(8,128)S(1)} %get-tuple-element.23), channel_id=1, source_target_pairs={{0,8},{8,16},{16,24},{24,32},{32,40},{40,48},{48,56},{56,64},{64,7... | collective-permute-start | bytes 786440 | tf_op jit(solution)/shard_map/ppermute | solution.py:427
  125.5 17.0 %all-to-all-start.2 = ((f32[4,32,8,256]{3,2,1,0:T(8,128)}), f32[4,32,8,256]{3,2,1,0:T(8,128)S(1)}, u32[]{:S(2)}, u32[]{:S(2)}) async-start(f32[4,32,8,256]{3,2,1,0:T(8,128)} %broadcast_in_dim.11), calls=%async_computation.2 | async-start | bytes 2097152 | tf_op jit(solution)/shard_map/all_to_all | solution.py:474
  129.4 18.0 %collective-permute-start.9 = (f32[4,32,8,256]{3,2,1,0:T(8,128)S(1)}, f32[4,32,8,256]{3,2,1,0:T(8,128)}, u32[]{:S(2)}, u32[]{:S(2)}) collective-permute-start(f32[4,32,8,256]{3,2,1,0:T(8,128)S(1)} %all-to-all-done.3.refs_0_), channel_id=1, source_target_pairs={{0,1},{1,0},{2,3},{3,2},{4,5},{5,4},{6,7},{7,6},{8,9},{9,8},{10,11... | collective-permute-start | bytes 3145736 | tf_op jit(solution)/shard_map/ppermute | solution.py:436
  142.5 8.1 %collective-permute-start.8 = (f32[4,32,8,256]{3,2,1,0:T(8,128)S(1)}, f32[4,32,8,256]{3,2,1,0:T(8,128)S(1)}, u32[]{:S(2)}, u32[]{:S(2)}) collective-permute-start(f32[4,32,8,256]{3,2,1,0:T(8,128)S(1)} %all-to-all-done.2.refs_1_), channel_id=1, source_target_pairs={{0,1},{1,0},{2,3},{3,2},{4,5},{5,4},{6,7},{7,6},{8,9},{9,8},{10,11... | collective-permute-start | bytes 3145736 | tf_op jit(solution)/shard_map/ppermute | solution.py:436

commit v6 on v5

--- a/solution.py
+++ b/solution.py
@@ -471,9 +471,13 @@
             spill, _ = lax.optimization_barrier((spill, spreads[0]))
         result = mine[ch] + ((here + spill) / weight).reshape(mine.shape[1:])
         spreads.append(jnp.broadcast_to(result, (chips, *result.shape)))
-    shares = [lax.all_to_all(spread, "group", 0, 0, axis_index_groups=same_core) for spread in spreads]
+    shares = [lax.all_to_all(spreads[0], "group", 0, 0, axis_index_groups=same_core)]
+    shares[0], spreads[1] = lax.optimization_barrier((shares[0], spreads[1]))
+    shares.append(lax.all_to_all(spreads[1], "group", 0, 0, axis_index_groups=same_core))
+    field = assembled(group, ((0, 0),), shares[:1], blocks.shape)
+    shares[1], field = lax.optimization_barrier((shares[1], field))
     others = [to_core(share) for share in shares]
-    field = assembled(group, ((0, 0), (1, 0), (0, 1)), (*shares, others[0]), blocks.shape)
+    field = assembled(group, ((1, 0), (0, 1)), (shares[1], others[0]), blocks.shape, (field,))
     field = assembled(group, ((1, 1),), (others[1],), blocks.shape, (field,), staged=False)
     return field.reshape(object_field.shape)
 

time: 154 us -> 153 us (level)
    pallas_call x2 -> x3, Pallas kernels: 4.2 us -> 4.81 us  [assembled(): pl.pallas_call(functools.partial(assemble_kernel, kinds, parts, staged),...]
  transfers between devices with their start and end apart: 13 -> 13, of which waited for: 9 -> 10; matrix products, arithmetic and copies ran while one was open for 2% -> 2% of each run, Pallas kernels for 7% -> 7%
where the time goes in v6:
time: 153 us; the launch traced here: 151 us
  waiting for transfers between devices  48.8 us (32%)
  starting transfers between devices  46.8 us (31%)
  blocking collectives  30.5 us (20%)
  Pallas kernels  16.4 us (11%)
  local copies, waits for them, and re-layouts  4.98 us (3%)
  other arithmetic  2.44 us (2%)
    all_to_all x1, blocking collectives, body(): gots = [lax.all_to_all(channel, 'group', 0, 0) for channel in sent]  30.5 us
    ppermute x5, waiting for transfers between devices, passed_along(): return lax.ppermute(x, axis, pairs)  22.6 us
    ppermute x4, starting transfers between devices, to_core(): lax.ppermute(x, 'group', [(i, i ^ 1) for i in range(lax.axis_size('group'...  17.8 us
    ppermute x5, starting transfers between devices, passed_along(): return lax.ppermute(x, axis, pairs)  14.4 us
    ppermute x1, waiting for transfers between devices, to_chip(): lax.ppermute(x, 'group', [(i, (i + 2 * by) % devices) for i in range(devi...  10.7 us
    all_to_all x1, waiting for transfers between devices, body(): lax.all_to_all(spreads[1], 'group', 0, 0, axis_index_groups=same_core)  8.03 us
    all_to_all x1, waiting for transfers between devices, body(): gots = [lax.all_to_all(channel, 'group', 0, 0) for channel in sent]  5.88 us
    pallas_call x3, Pallas kernels, assembled(): pl.pallas_call(functools.partial(assemble_kernel, kinds, parts, staged),...  4.81 us
  transfers between devices with their start and end apart: 13, of which 10 were waited for; matrix products, arithmetic and copies ran while one was open for 2% of the time, Pallas kernels for 7%

profile of v6, /device:TPU:449, one launch (start us, length us, event | category | flops | bytes accessed | tf_op | source)
XLA Modules:
  0.0 150.8 jit_solution(11847218857769744267)
XLA Ops:
  0.1 0.0 copy-start.2
  0.1 0.0 copy-start.6
  0.1 1.7 %dynamic-slice_bitcast_fusion.1 = (f32[1,2,32,8,256]{4,3,2,1,0:T(8,128)S(1)}, f32[2,32,8,256]{3,2,1,0:T(8,128)S(1)}, f32[1,2,32,8,256]{4,3,2,1,0:T(8,128)S(1)}) fusion(f32[2,32,8,8,256]{4,3,2,1,0:T(8,128)} %bitcast.39, s32[]{:T(128)S(6)} %select_n.24, s32[]{:T(128)S(6)} %select_n.22, s32[]{:T(128)S(6)} %select_n.26), kind=kLoop, calls=%fused_computation.3 | loop fusion | bytes 3145740 | tf_op jit(solution)/shard_map/stack | solution.py:452
  1.8 5.1 %collective-permute-start = (f32[2,32,8,256]{3,2,1,0:T(8,128)S(1)}, f32[2,32,8,256]{3,2,1,0:T(8,128)S(1)}, u32[]{:S(2)}, u32[]{:S(2)}) collective-permute-start(f32[2,32,8,256]{3,2,1,0:T(8,128)S(1)} %get-tuple-element.36), channel_id=1, source_target_pairs={{8,0},{16,8},{24,16},{32,24},{40,32},{48,40},{56,48},{64,56},{72,6... | collective-permute-start | bytes 1572872 | tf_op jit(solution)/shard_map/ppermute | solution.py:427
  6.9 0.1 pad_maximum_fusion.1
  7.0 3.0 %collective-permute-start.3 = (f32[2,2,32,8,256]{4,3,2,1,0:T(8,128)S(1)}, f32[2,2,32,8,256]{4,3,2,1,0:T(8,128)S(1)}, u32[]{:S(2)}, u32[]{:S(2)}) collective-permute-start(f32[2,2,32,8,256]{4,3,2,1,0:T(8,128)S(1)} %pad_maximum_fusion.1), channel_id=1, source_target_pairs={{8,0},{16,8},{24,16},{32,24},{40,32},{48,40},{56,48},{64,56},{72,6... | collective-permute-start | bytes 3145736 | tf_op jit(solution)/shard_map/ppermute | solution.py:427
  10.6 0.1 pad_add_fusion
  10.7 2.3 %collective-permute-start.1 = (s32[13]{0:T(128)S(1)}, s32[13]{0:T(128)S(1)}, u32[]{:S(2)}, u32[]{:S(2)}) collective-permute-start(s32[13]{0:T(128)S(1)} %pad_add_fusion), channel_id=1, source_target_pairs={{0,8},{8,16},{16,24},{24,32},{32,40},{40,48},{48,56},{56,64},{64,7... | collective-permute-start | bytes 164 | tf_op jit(solution)/shard_map/ppermute | solution.py:427
  13.0 4.1 %collective-permute-done.1 = s32[13]{0:T(128)S(1)} collective-permute-done((s32[13]{0:T(128)S(1)}, s32[13]{0:T(128)S(1)}, u32[]{:S(2)}, u32[]{:S(2)}) %collective-permute-start.1) | collective-permute-done | bytes 84 | tf_op jit(solution)/shard_map/ppermute | solution.py:427
  17.1 0.4 collective-permute-done
  17.5 3.1 %collective-permute-start.2 = (f32[2,32,8,256]{3,2,1,0:T(8,128)S(1)}, f32[2,32,8,256]{3,2,1,0:T(8,128)S(1)}, u32[]{:S(2)}, u32[]{:S(2)}) collective-permute-start(f32[2,32,8,256]{3,2,1,0:T(8,128)S(1)} %collective-permute-done), channel_id=1, source_target_pairs={{0,2},{1,3},{2,4},{3,5},{4,6},{5,7},{6,0},{7,1},{8,10},{9,11},{10,... | collective-permute-start | bytes 1572872 | tf_op jit(solution)/shard_map/ppermute | solution.py:432
  20.6 10.7 %collective-permute-done.2 = f32[2,32,8,256]{3,2,1,0:T(8,128)S(1)} collective-permute-done((f32[2,32,8,256]{3,2,1,0:T(8,128)S(1)}, f32[2,32,8,256]{3,2,1,0:T(8,128)S(1)}, u32[]{:S(2)}, u32[]{:S(2)}) %collective-permute-start.2) | collective-permute-done | bytes 524320 | tf_op jit(solution)/shard_map/ppermute | solution.py:432
  31.3 0.1 pad_maximum_fusion.near_ref
  31.4 5.5 %collective-permute-start.4 = (f32[2,2,32,8,256]{4,3,2,1,0:T(8,128)S(1)}, f32[2,2,32,8,256]{4,3,2,1,0:T(8,128)S(1)}, u32[]{:S(2)}, u32[]{:S(2)}) collective-permute-start(f32[2,2,32,8,256]{4,3,2,1,0:T(8,128)S(1)} %pad_maximum_fusion.near_ref), channel_id=1, source_target_pairs={{0,1},{1,0},{2,3},{3,2},{4,5},{5,4},{6,7},{7,6},{8,9},{9,8},{10,11... | collective-permute-start | bytes 3145736 | tf_op jit(solution)/shard_map/ppermute | solution.py:436
  36.9 3.0 %collective-permute-done.3.far_ref = f32[2,2,32,8,256]{4,3,2,1,0:T(8,128)S(1)} collective-permute-done((f32[2,2,32,8,256]{4,3,2,1,0:T(8,128)S(1)}, f32[2,2,32,8,256]{4,3,2,1,0:T(8,128)S(1)}, u32[]{:S(2)}, u32[]{:S(2)}) %collective-permute-start.3) | collective-permute-done | bytes 1048608 | tf_op jit(solution)/shard_map/ppermute | solution.py:427
  39.9 3.4 %collective-permute-start.5 = (f32[2,2,32,8,256]{4,3,2,1,0:T(8,128)S(1)}, f32[2,2,32,8,256]{4,3,2,1,0:T(8,128)S(1)}, u32[]{:S(2)}, u32[]{:S(2)}) collective-permute-start(f32[2,2,32,8,256]{4,3,2,1,0:T(8,128)S(1)} %collective-permute-done.3.far_ref), channel_id=1, source_target_pairs={{0,1},{1,0},{2,3},{3,2},{4,5},{5,4},{6,7},{7,6},{8,9},{9,8},{10,11... | collective-permute-start | bytes 3145736 | tf_op jit(solution)/shard_map/ppermute | solution.py:436
  43.4 0.1 pad.6.clone
  43.5 0.7 ordered.1.amp_hbm
  44.1 0.1 fusion.3
  44.2 0.1 add_add_fusion.notes_ref
  44.3 1.3 collective-permute-done.5.other_far_ref
  45.6 4.3 %patterns.1 = (f32[8,200,256]{2,1,0:T(8,128)S(1)}, f32[8,192,256]{2,1,0:T(8,128)S(1)}) custom-call(s32[3,13]{1,0:T(4,128)S(1)} %add_add_fusion.notes_ref, f32[2,2048,256]{2,1,0:T(8,128)} %own_ref.1, f32[2,256,256]{2,1,0:T(8,128)S(1)} %copy-done.2, bf16[6,256,256]{2,1,0:T(8,128)(2,1)S(1)} %ordered.1.amp_hbm, bf16[16,256,256]{2,1,0:T(8,128)(2,1)S(1)} %copy-done.6, ...), custom_call_target="tpu_custom_call" | custom-call | flops 4831838208 | bytes 12582912 | tf_op jit(solution)/shard_map/patterns/pallas_call | solution.py:250
  50.0 0.0 copy-start
  50.0 30.5 %all_to_all.20.got_ref = f32[8,200,256]{2,1,0:T(8,128)S(1)} all-to-all(f32[8,200,256]{2,1,0:T(8,128)S(1)} %get-tuple-element.24), channel_id=1, replica_groups=mesh['tile'=64,'group'=8] {'group'}, dimensions={0} | all-to-all | bytes 3276800 | tf_op jit(solution)/shard_map/all_to_all | solution.py:460
  80.5 4.2 %all-to-all-start.2 = ((f32[8,192,256]{2,1,0:T(8,128)}), f32[8,192,256]{2,1,0:T(8,128)S(1)}, u32[]{:S(2)}, u32[]{:S(2)}) async-start(f32[8,192,256]{2,1,0:T(8,128)} %copy-done), calls=%async_computation.2 | async-start | bytes 3145728 | tf_op jit(solution)/shard_map/all_to_all | solution.py:460
  84.8 1.2 gathered.2
  86.0 2.0 %collective-permute-start.6 = (f32[256,256]{1,0:T(8,128)S(1)}, f32[256,256]{1,0:T(8,128)S(1)}, u32[]{:S(2)}, u32[]{:S(2)}) collective-permute-start(f32[256,256]{1,0:T(8,128)S(1)} %get-tuple-element.26), channel_id=1, source_target_pairs={{0,8},{8,16},{16,24},{24,32},{32,40},{40,48},{48,56},{56,64},{64,7... | collective-permute-start | bytes 786440 | tf_op jit(solution)/shard_map/ppermute | solution.py:427
  88.0 0.0 copy-start.3
  88.1 1.0 copy-done.3
  89.1 4.2 %illumination.1 = f32[256,256]{1,0:T(8,128)S(1)} custom-call(s32[1]{0:T(128)} %bitcast.group_ref, s32[8,13]{1,0:T(8,128)S(1)} %bitcast.36, s32[8,13]{1,0:T(8,128)S(1)} %bitcast.38, f32[2,256,256]{2,1,0:T(8,128)S(1)} %copy-done.3), custom_call_target="tpu_custom_call" | custom-call | flops 4194304 | bytes 8388608 | tf_op jit(solution)/shard_map/illumination/pallas_call | solution.py:368
  93.2 5.3 %collective-permute-done.6 = f32[256,256]{1,0:T(8,128)S(1)} collective-permute-done((f32[256,256]{1,0:T(8,128)S(1)}, f32[256,256]{1,0:T(8,128)S(1)}, u32[]{:S(2)}, u32[]{:S(2)}) %collective-permute-start.6) | collective-permute-done | bytes 262176 | tf_op jit(solution)/shard_map/ppermute | solution.py:427
  98.6 1.0 fusion.1
  99.6 5.9 %all-to-all-done.2.got_ref = f32[8,192,256]{2,1,0:T(8,128)S(1)} async-done(((f32[8,192,256]{2,1,0:T(8,128)}), f32[8,192,256]{2,1,0:T(8,128)S(1)}, u32[]{:S(2)}, u32[]{:S(2)}) %all-to-all-start.2) | async-done | bytes 1572896 | tf_op jit(solution)/shard_map/all_to_all | solution.py:460
  105.5 1.1 broadcast_in_dim.10
  106.5 3.5 %all-to-all-start.1 = ((f32[4,32,8,256]{3,2,1,0:T(8,128)}), f32[4,32,8,256]{3,2,1,0:T(8,128)S(1)}, u32[]{:S(2)}, u32[]{:S(2)}) async-start(f32[4,32,8,256]{3,2,1,0:T(8,128)} %broadcast_in_dim.10), calls=%async_computation.1 | async-start | bytes 2097152 | tf_op jit(solution)/shard_map/all_to_all | solution.py:474
  110.1 1.2 gathered.3
  111.3 2.0 %collective-permute-start.7 = (f32[256,256]{1,0:T(8,128)S(1)}, f32[256,256]{1,0:T(8,128)S(1)}, u32[]{:S(2)}, u32[]{:S(2)}) collective-permute-start(f32[256,256]{1,0:T(8,128)S(1)} %get-tuple-element.29), channel_id=1, source_target_pairs={{0,8},{8,16},{16,24},{24,32},{32,40},{40,48},{48,56},{56,64},{64,7... | collective-permute-start | bytes 786440 | tf_op jit(solution)/shard_map/ppermute | solution.py:427
  113.3 9.8 %collective-permute-done.7 = f32[256,256]{1,0:T(8,128)S(1)} collective-permute-done((f32[256,256]{1,0:T(8,128)S(1)}, f32[256,256]{1,0:T(8,128)S(1)}, u32[]{:S(2)}, u32[]{:S(2)}) %collective-permute-start.7) | collective-permute-done | bytes 262176 | tf_op jit(solution)/shard_map/ppermute | solution.py:427
  123.1 1.0 fusion
  124.1 0.2 all-to-all-done.1.refs_0_
  124.3 1.1 broadcast_in_dim.11
  125.4 3.7 %all-to-all-start.3 = ((f32[4,32,8,256]{3,2,1,0:T(8,128)}), f32[4,32,8,256]{3,2,1,0:T(8,128)S(1)}, u32[]{:S(2)}, u32[]{:S(2)}) async-start(f32[4,32,8,256]{3,2,1,0:T(8,128)} %broadcast_in_dim.11), calls=%async_computation.3 | async-start | bytes 2097152 | tf_op jit(solution)/shard_map/all_to_all | solution.py:476
  129.1 3.9 %collective-permute-start.9 = (f32[4,32,8,256]{3,2,1,0:T(8,128)S(1)}, f32[4,32,8,256]{3,2,1,0:T(8,128)}, u32[]{:S(2)}, u32[]{:S(2)}) collective-permute-start(f32[4,32,8,256]{3,2,1,0:T(8,128)S(1)} %all-to-all-done.1.refs_0_), channel_id=1, source_target_pairs={{0,1},{1,0},{2,3},{3,2},{4,5},{5,4},{6,7},{7,6},{8,9},{9,8},{10,11... | collective-permute-start | bytes 3145736 | tf_op jit(solution)/shard_map/ppermute | solution.py:436
  133.0 1.1 assembled.3.refs_2_
  134.1 8.0 %all-to-all-done.3.refs_0_ = f32[4,32,8,256]{3,2,1,0:T(8,128)S(1)} async-done(((f32[4,32,8,256]{3,2,1,0:T(8,128)}), f32[4,32,8,256]{3,2,1,0:T(8,128)S(1)}, u32[]{:S(2)}, u32[]{:S(2)}) %all-to-all-start.3) | async-done | bytes 1048608 | tf_op jit(solution)/shard_map/all_to_all | solution.py:476
  142.2 4.9 %collective-permute-start.8 = (f32[4,32,8,256]{3,2,1,0:T(8,128)S(1)}, f32[4,32,8,256]{3,2,1,0:T(8,128)S(1)}, u32[]{:S(2)}, u32[]{:S(2)}) collective-permute-start(f32[4,32,8,256]{3,2,1,0:T(8,128)S(1)} %all-to-all-done.3.refs_0_), channel_id=1, source_target_pairs={{0,1},{1,0},{2,3},{3,2},{4,5},{5,4},{6,7},{7,6},{8,9},{9,8},{10,11... | collective-permute-start | bytes 3145736 | tf_op jit(solution)/shard_map/ppermute | solution.py:436
  147.0 2.7 %assembled.4.refs_1_ = f32[2,32,8,8,256]{4,3,2,1,0:T(8,128)} custom-call(s32[1]{0:T(128)} %bitcast.group_ref, f32[4,32,8,256]{3,2,1,0:T(8,128)S(1)} %all-to-all-done.3.refs_0_, f32[4,32,8,256]{3,2,1,0:T(8,128)} %collective-permute-done.9.refs_1_, f32[2,32,8,8,256]{4,3,2,1,0:T(8,128)} %assembled.3.refs_2_), custom_call_target="tpu_custom_call", output_to_operand_aliasing={{}: (3, {})} | custom-call | bytes 4194304 | tf_op jit(solution)/shard_map/assembled/pallas_call | solution.py:411
  149.8 1.0 assembled.5
  (18 shorter events, 0.0 us)
Async XLA Ops:
  0.0 43.5 %copy-start.4 = (bf16[256,256]{1,0:T(8,128)(2,1)S(1)}, bf16[256,256]{1,0:T(8,128)(2,1)}, u32[]{:S(2)}) copy-start(bf16[256,256]{1,0:T(8,128)(2,1)} %constant.42.clone.turned_ref) | copy-start | bytes 393220
  0.0 43.5 %copy-start.5 = (bf16[256,256]{1,0:T(8,128)(2,1)S(1)}, bf16[256,256]{1,0:T(8,128)(2,1)}, u32[]{:S(2)}) copy-start(bf16[256,256]{1,0:T(8,128)(2,1)} %constant.41.clone.order_ref) | copy-start | bytes 393220
  0.0 10.6 %copy-start.7 = (s32[6]{0:T(128)S(1)}, s32[6]{0:T(128)}, u32[]{:S(2)}) copy-start(s32[6]{0:T(128)} %param.13) | copy-start | bytes 76
  0.0 10.6 %copy-start.8 = (s32[6]{0:T(128)S(1)}, s32[6]{0:T(128)}, u32[]{:S(2)}) copy-start(s32[6]{0:T(128)} %param.12) | copy-start | bytes 76
  0.0 43.4 %copy-start.1 = (bf16[6,256,256]{2,1,0:T(8,128)(2,1)S(1)}, bf16[6,256,256]{2,1,0:T(8,128)(2,1)}, u32[]{:S(2)}) copy-start(bf16[6,256,256]{2,1,0:T(8,128)(2,1)} %amp_ref.1) | copy-start | bytes 2359300
  0.1 45.6 %copy-start.2 = (f32[2,256,256]{2,1,0:T(8,128)S(1)}, f32[2,256,256]{2,1,0:T(8,128)}, u32[]{:S(2)}) copy-start(f32[2,256,256]{2,1,0:T(8,128)} %probe_ref.1) | copy-start | bytes 1572868
  0.1 45.6 %copy-start.6 = (bf16[16,256,256]{2,1,0:T(8,128)(2,1)S(1)}, bf16[16,256,256]{2,1,0:T(8,128)(2,1)}, u32[]{:S(2)}) copy-start(bf16[16,256,256]{2,1,0:T(8,128)(2,1)} %constant.43.clone.tab_hbm) | copy-start | bytes 6291460
  1.8 15.7 %collective-permute-start = (f32[2,32,8,256]{3,2,1,0:T(8,128)S(1)}, f32[2,32,8,256]{3,2,1,0:T(8,128)S(1)}, u32[]{:S(2)}, u32[]{:S(2)}) collective-permute-start(f32[2,32,8,256]{3,2,1,0:T(8,128)S(1)} %get-tuple-element.36), channel_id=1, source_target_pairs={{8,0},{16,8},{24,16},{32,24},{40,32},{48,40},{56,48},{64,56},{72,6... | collective-permute-start | bytes 1572872 | tf_op jit(solution)/shard_map/ppermute | solution.py:427
  7.0 32.9 %collective-permute-start.3 = (f32[2,2,32,8,256]{4,3,2,1,0:T(8,128)S(1)}, f32[2,2,32,8,256]{4,3,2,1,0:T(8,128)S(1)}, u32[]{:S(2)}, u32[]{:S(2)}) collective-permute-start(f32[2,2,32,8,256]{4,3,2,1,0:T(8,128)S(1)} %pad_maximum_fusion.1), channel_id=1, source_target_pairs={{8,0},{16,8},{24,16},{32,24},{40,32},{48,40},{56,48},{64,56},{72,6... | collective-permute-start | bytes 3145736 | tf_op jit(solution)/shard_map/ppermute | solution.py:427
  10.7 6.4 %collective-permute-start.1 = (s32[13]{0:T(128)S(1)}, s32[13]{0:T(128)S(1)}, u32[]{:S(2)}, u32[]{:S(2)}) collective-permute-start(s32[13]{0:T(128)S(1)} %pad_add_fusion), channel_id=1, source_target_pairs={{0,8},{8,16},{16,24},{24,32},{32,40},{40,48},{48,56},{56,64},{64,7... | collective-permute-start | bytes 164 | tf_op jit(solution)/shard_map/ppermute | solution.py:427
  17.5 13.8 %collective-permute-start.2 = (f32[2,32,8,256]{3,2,1,0:T(8,128)S(1)}, f32[2,32,8,256]{3,2,1,0:T(8,128)S(1)}, u32[]{:S(2)}, u32[]{:S(2)}) collective-permute-start(f32[2,32,8,256]{3,2,1,0:T(8,128)S(1)} %collective-permute-done), channel_id=1, source_target_pairs={{0,2},{1,3},{2,4},{3,5},{4,6},{5,7},{6,0},{7,1},{8,10},{9,11},{10,... | collective-permute-start | bytes 1572872 | tf_op jit(solution)/shard_map/ppermute | solution.py:432
  31.4 12.9 %collective-permute-start.4 = (f32[2,2,32,8,256]{4,3,2,1,0:T(8,128)S(1)}, f32[2,2,32,8,256]{4,3,2,1,0:T(8,128)S(1)}, u32[]{:S(2)}, u32[]{:S(2)}) collective-permute-start(f32[2,2,32,8,256]{4,3,2,1,0:T(8,128)S(1)} %pad_maximum_fusion.near_ref), channel_id=1, source_target_pairs={{0,1},{1,0},{2,3},{3,2},{4,5},{5,4},{6,7},{7,6},{8,9},{9,8},{10,11... | collective-permute-start | bytes 3145736 | tf_op jit(solution)/shard_map/ppermute | solution.py:436
  39.9 5.7 %collective-permute-start.5 = (f32[2,2,32,8,256]{4,3,2,1,0:T(8,128)S(1)}, f32[2,2,32,8,256]{4,3,2,1,0:T(8,128)S(1)}, u32[]{:S(2)}, u32[]{:S(2)}) collective-permute-start(f32[2,2,32,8,256]{4,3,2,1,0:T(8,128)S(1)} %collective-permute-done.3.far_ref), channel_id=1, source_target_pairs={{0,1},{1,0},{2,3},{3,2},{4,5},{5,4},{6,7},{7,6},{8,9},{9,8},{10,11... | collective-permute-start | bytes 3145736 | tf_op jit(solution)/shard_map/ppermute | solution.py:436
  50.0 30.5 %copy-start = (f32[8,192,256]{2,1,0:T(8,128)}, f32[8,192,256]{2,1,0:T(8,128)S(1)}, u32[]{:S(2)}) copy-start(f32[8,192,256]{2,1,0:T(8,128)S(1)} %get-tuple-element.27) | copy-start | bytes 4718596
  80.5 25.0 %all-to-all-start.2 = ((f32[8,192,256]{2,1,0:T(8,128)}), f32[8,192,256]{2,1,0:T(8,128)S(1)}, u32[]{:S(2)}, u32[]{:S(2)}) async-start(f32[8,192,256]{2,1,0:T(8,128)} %copy-done), calls=%async_computation.2 | async-start | bytes 3145728 | tf_op jit(solution)/shard_map/all_to_all | solution.py:460
  86.0 12.6 %collective-permute-start.6 = (f32[256,256]{1,0:T(8,128)S(1)}, f32[256,256]{1,0:T(8,128)S(1)}, u32[]{:S(2)}, u32[]{:S(2)}) collective-permute-start(f32[256,256]{1,0:T(8,128)S(1)} %get-tuple-element.26), channel_id=1, source_target_pairs={{0,8},{8,16},{16,24},{24,32},{32,40},{40,48},{48,56},{56,64},{64,7... | collective-permute-start | bytes 786440 | tf_op jit(solution)/shard_map/ppermute | solution.py:427
  88.0 1.0 copy-start.3
  106.5 17.8 %all-to-all-start.1 = ((f32[4,32,8,256]{3,2,1,0:T(8,128)}), f32[4,32,8,256]{3,2,1,0:T(8,128)S(1)}, u32[]{:S(2)}, u32[]{:S(2)}) async-start(f32[4,32,8,256]{3,2,1,0:T(8,128)} %broadcast_in_dim.10), calls=%async_computation.1 | async-start | bytes 2097152 | tf_op jit(solution)/shard_map/all_to_all | solution.py:474
  111.3 11.8 %collective-permute-start.7 = (f32[256,256]{1,0:T(8,128)S(1)}, f32[256,256]{1,0:T(8,128)S(1)}, u32[]{:S(2)}, u32[]{:S(2)}) collective-permute-start(f32[256,256]{1,0:T(8,128)S(1)} %get-tuple-element.29), channel_id=1, source_target_pairs={{0,8},{8,16},{16,24},{24,32},{32,40},{40,48},{48,56},{56,64},{64,7... | collective-permute-start | bytes 786440 | tf_op jit(solution)/shard_map/ppermute | solution.py:427
  125.4 16.8 %all-to-all-start.3 = ((f32[4,32,8,256]{3,2,1,0:T(8,128)}), f32[4,32,8,256]{3,2,1,0:T(8,128)S(1)}, u32[]{:S(2)}, u32[]{:S(2)}) async-start(f32[4,32,8,256]{3,2,1,0:T(8,128)} %broadcast_in_dim.11), calls=%async_computation.3 | async-start | bytes 2097152 | tf_op jit(solution)/shard_map/all_to_all | solution.py:476
  129.1 18.0 %collective-permute-start.9 = (f32[4,32,8,256]{3,2,1,0:T(8,128)S(1)}, f32[4,32,8,256]{3,2,1,0:T(8,128)}, u32[]{:S(2)}, u32[]{:S(2)}) collective-permute-start(f32[4,32,8,256]{3,2,1,0:T(8,128)S(1)} %all-to-all-done.1.refs_0_), channel_id=1, source_target_pairs={{0,1},{1,0},{2,3},{3,2},{4,5},{5,4},{6,7},{7,6},{8,9},{9,8},{10,11... | collective-permute-start | bytes 3145736 | tf_op jit(solution)/shard_map/ppermute | solution.py:436
  142.2 7.6 %collective-permute-start.8 = (f32[4,32,8,256]{3,2,1,0:T(8,128)S(1)}, f32[4,32,8,256]{3,2,1,0:T(8,128)S(1)}, u32[]{:S(2)}, u32[]{:S(2)}) collective-permute-start(f32[4,32,8,256]{3,2,1,0:T(8,128)S(1)} %all-to-all-done.3.refs_0_), channel_id=1, source_target_pairs={{0,1},{1,0},{2,3},{3,2},{4,5},{5,4},{6,7},{7,6},{8,9},{9,8},{10,11... | collective-permute-start | bytes 3145736 | tf_op jit(solution)/shard_map/ppermute | solution.py:436

commit v7 on v6

--- a/solution.py
+++ b/solution.py
@@ -381,19 +381,19 @@
 
 
 def assemble_kernel(kinds, parts, staged, group_ref, *refs):
-    sources = list(refs[: len(kinds)])
+    sources, loads = list(refs[: len(kinds)]), {}
     if staged:
         out_ref, held, load_sems, sems = refs[-4:]
-        loads = [pltpu.make_async_copy(ref, held.at[n], load_sems.at[n]) for n, ref in enumerate(sources)]
-        sources = [held.at[n] for n in range(len(kinds))]
+        for n, k in enumerate(staged):
+            loads[k] = pltpu.make_async_copy(sources[k], held.at[n], load_sems.at[n])
+            loads[k].start()
+            sources[k] = held.at[n]
     else:
-        (out_ref, sems), loads = refs[-2:], []
-    for load in loads:
-        load.start()
+        out_ref, sems = refs[-2:]
     copies = []
     for k, (ch, other) in enumerate(kinds):
         core = (group_ref[0] & 1) ^ other
-        if loads:
+        if k in loads:
             loads[k].wait()
         for n in range(parts // 2):
             copies.append(pltpu.make_async_copy(sources[k].at[n], out_ref.at[ch, :, 2 * n + core], sems.at[len(copies)]))
@@ -402,12 +402,12 @@
         copy.wait()
 
 
-def assembled(group, kinds, shares, shape, begun=(), staged=True):
+def assembled(group, kinds, shares, shape, begun=(), staged=()):
     parts = shape[2]
     anywhere = pl.BlockSpec(memory_space=pl.ANY)
     hbm = pl.BlockSpec(memory_space=pltpu.HBM)
     count = len(shares)
-    held = [pltpu.VMEM((count, *shares[0].shape), jnp.float32), pltpu.SemaphoreType.DMA((count,))] if staged else []
+    held = [pltpu.VMEM((len(staged), *shares[0].shape), jnp.float32), pltpu.SemaphoreType.DMA((len(staged),))] if staged else []
     return pl.pallas_call(
         functools.partial(assemble_kernel, kinds, parts, staged),
         out_shape=jax.ShapeDtypeStruct(shape, jnp.float32),
@@ -474,11 +474,11 @@
     shares = [lax.all_to_all(spreads[0], "group", 0, 0, axis_index_groups=same_core)]
     shares[0], spreads[1] = lax.optimization_barrier((shares[0], spreads[1]))
     shares.append(lax.all_to_all(spreads[1], "group", 0, 0, axis_index_groups=same_core))
-    field = assembled(group, ((0, 0),), shares[:1], blocks.shape)
+    field = assembled(group, ((0, 0),), shares[:1], blocks.shape, staged=(0,))
     shares[1], field = lax.optimization_barrier((shares[1], field))
     others = [to_core(share) for share in shares]
-    field = assembled(group, ((1, 0), (0, 1)), (shares[1], others[0]), blocks.shape, (field,))
-    field = assembled(group, ((1, 1),), (others[1],), blocks.shape, (field,), staged=False)
+    field = assembled(group, ((1, 0), (0, 1)), (shares[1], others[0]), blocks.shape, (field,), staged=(1,))
+    field = assembled(group, ((1, 1),), (others[1],), blocks.shape, (field,))
     return field.reshape(object_field.shape)
 
 

time: 153 us -> 153 us (level)
  waiting for transfers between devices: 48.8 us -> 53.9 us
  blocking collectives: 30.5 us -> 26.2 us
    ppermute x5, waiting for transfers between devices: 22.6 us -> 32.7 us  [passed_along(): return lax.ppermute(x, axis, pairs)]
    all_to_all x1, waiting for transfers between devices: 5.88 us -> 1.15 us  [body(): gots = [lax.all_to_all(channel, 'group', 0, 0) for channel in sent]]
    all_to_all x1, blocking collectives: 30.5 us -> 26.2 us  [body(): gots = [lax.all_to_all(channel, 'group', 0, 0) for channel in sent]]
  transfers between devices with their start and end apart: 13 -> 13, of which waited for: 10 -> 9; matrix products, arithmetic and copies ran while one was open for 2% -> 2% of each run, Pallas kernels for 7% -> 7%
where the time goes in v7:
time: 153 us; the launch traced here: 151 us
  waiting for transfers between devices  53.9 us (35%)
  starting transfers between devices  47.4 us (31%)
  blocking collectives  26.2 us (17%)
  Pallas kernels  15.2 us (10%)
  local copies, waits for them, and re-layouts  4.98 us (3%)
  other arithmetic  2.44 us (2%)
    ppermute x5, waiting for transfers between devices, passed_along(): return lax.ppermute(x, axis, pairs)  32.7 us
    all_to_all x1, blocking collectives, body(): gots = [lax.all_to_all(channel, 'group', 0, 0) for channel in sent]  26.2 us
    ppermute x4, starting transfers between devices, to_core(): lax.ppermute(x, 'group', [(i, i ^ 1) for i in range(lax.axis_size('group'...  17.8 us
    ppermute x5, starting transfers between devices, passed_along(): return lax.ppermute(x, axis, pairs)  14.9 us
    ppermute x1, waiting for transfers between devices, to_chip(): lax.ppermute(x, 'group', [(i, (i + 2 * by) % devices) for i in range(devi...  10.7 us
    all_to_all x1, waiting for transfers between devices, body(): lax.all_to_all(spreads[1], 'group', 0, 0, axis_index_groups=same_core)  8.03 us
    pallas_call x3, Pallas kernels, assembled(): pl.pallas_call(functools.partial(assemble_kernel, kinds, parts, staged),...  4.73 us
    pallas_call x1, Pallas kernels, patterns(): pl.pallas_call(functools.partial(patterns_kernel, size, rows, parts, slot...  4.34 us
  transfers between devices with their start and end apart: 13, of which 9 were waited for; matrix products, arithmetic and copies ran while one was open for 2% of the time, Pallas kernels for 7%

profile of v7, /device:TPU:449, one launch (start us, length us, event | category | flops | bytes accessed | tf_op | source)
XLA Modules:
  0.0 151.1 jit_solution(9288486537006456689)
XLA Ops:
  0.1 0.0 copy-start.2
  0.1 0.0 copy-start.6
  0.1 1.7 %dynamic-slice_bitcast_fusion.1 = (f32[1,2,32,8,256]{4,3,2,1,0:T(8,128)S(1)}, f32[2,32,8,256]{3,2,1,0:T(8,128)S(1)}, f32[1,2,32,8,256]{4,3,2,1,0:T(8,128)S(1)}) fusion(f32[2,32,8,8,256]{4,3,2,1,0:T(8,128)} %bitcast.39, s32[]{:T(128)S(6)} %select_n.24, s32[]{:T(128)S(6)} %select_n.22, s32[]{:T(128)S(6)} %select_n.26), kind=kLoop, calls=%fused_computation.3 | loop fusion | bytes 3145740 | tf_op jit(solution)/shard_map/stack | solution.py:452
  1.8 5.1 %collective-permute-start = (f32[2,32,8,256]{3,2,1,0:T(8,128)S(1)}, f32[2,32,8,256]{3,2,1,0:T(8,128)S(1)}, u32[]{:S(2)}, u32[]{:S(2)}) collective-permute-start(f32[2,32,8,256]{3,2,1,0:T(8,128)S(1)} %get-tuple-element.36), channel_id=1, source_target_pairs={{8,0},{16,8},{24,16},{32,24},{40,32},{48,40},{56,48},{64,56},{72,6... | collective-permute-start | bytes 1572872 | tf_op jit(solution)/shard_map/ppermute | solution.py:427
  6.9 0.1 pad_maximum_fusion.1
  7.0 3.0 %collective-permute-start.3 = (f32[2,2,32,8,256]{4,3,2,1,0:T(8,128)S(1)}, f32[2,2,32,8,256]{4,3,2,1,0:T(8,128)S(1)}, u32[]{:S(2)}, u32[]{:S(2)}) collective-permute-start(f32[2,2,32,8,256]{4,3,2,1,0:T(8,128)S(1)} %pad_maximum_fusion.1), channel_id=1, source_target_pairs={{8,0},{16,8},{24,16},{32,24},{40,32},{48,40},{56,48},{64,56},{72,6... | collective-permute-start | bytes 3145736 | tf_op jit(solution)/shard_map/ppermute | solution.py:427
  10.6 0.1 pad_add_fusion
  10.7 2.3 %collective-permute-start.1 = (s32[13]{0:T(128)S(1)}, s32[13]{0:T(128)S(1)}, u32[]{:S(2)}, u32[]{:S(2)}) collective-permute-start(s32[13]{0:T(128)S(1)} %pad_add_fusion), channel_id=1, source_target_pairs={{0,8},{8,16},{16,24},{24,32},{32,40},{40,48},{48,56},{56,64},{64,7... | collective-permute-start | bytes 164 | tf_op jit(solution)/shard_map/ppermute | solution.py:427
  13.0 4.1 %collective-permute-done.1 = s32[13]{0:T(128)S(1)} collective-permute-done((s32[13]{0:T(128)S(1)}, s32[13]{0:T(128)S(1)}, u32[]{:S(2)}, u32[]{:S(2)}) %collective-permute-start.1) | collective-permute-done | bytes 84 | tf_op jit(solution)/shard_map/ppermute | solution.py:427
  17.1 0.4 collective-permute-done
  17.5 3.1 %collective-permute-start.2 = (f32[2,32,8,256]{3,2,1,0:T(8,128)S(1)}, f32[2,32,8,256]{3,2,1,0:T(8,128)S(1)}, u32[]{:S(2)}, u32[]{:S(2)}) collective-permute-start(f32[2,32,8,256]{3,2,1,0:T(8,128)S(1)} %collective-permute-done), channel_id=1, source_target_pairs={{0,2},{1,3},{2,4},{3,5},{4,6},{5,7},{6,0},{7,1},{8,10},{9,11},{10,... | collective-permute-start | bytes 1572872 | tf_op jit(solution)/shard_map/ppermute | solution.py:432
  20.6 10.7 %collective-permute-done.2 = f32[2,32,8,256]{3,2,1,0:T(8,128)S(1)} collective-permute-done((f32[2,32,8,256]{3,2,1,0:T(8,128)S(1)}, f32[2,32,8,256]{3,2,1,0:T(8,128)S(1)}, u32[]{:S(2)}, u32[]{:S(2)}) %collective-permute-start.2) | collective-permute-done | bytes 524320 | tf_op jit(solution)/shard_map/ppermute | solution.py:432
  31.3 0.1 pad_maximum_fusion.near_ref
  31.4 5.5 %collective-permute-start.4 = (f32[2,2,32,8,256]{4,3,2,1,0:T(8,128)S(1)}, f32[2,2,32,8,256]{4,3,2,1,0:T(8,128)S(1)}, u32[]{:S(2)}, u32[]{:S(2)}) collective-permute-start(f32[2,2,32,8,256]{4,3,2,1,0:T(8,128)S(1)} %pad_maximum_fusion.near_ref), channel_id=1, source_target_pairs={{0,1},{1,0},{2,3},{3,2},{4,5},{5,4},{6,7},{7,6},{8,9},{9,8},{10,11... | collective-permute-start | bytes 3145736 | tf_op jit(solution)/shard_map/ppermute | solution.py:436
  36.9 3.0 %collective-permute-done.3.far_ref = f32[2,2,32,8,256]{4,3,2,1,0:T(8,128)S(1)} collective-permute-done((f32[2,2,32,8,256]{4,3,2,1,0:T(8,128)S(1)}, f32[2,2,32,8,256]{4,3,2,1,0:T(8,128)S(1)}, u32[]{:S(2)}, u32[]{:S(2)}) %collective-permute-start.3) | collective-permute-done | bytes 1048608 | tf_op jit(solution)/shard_map/ppermute | solution.py:427
  39.9 3.4 %collective-permute-start.5 = (f32[2,2,32,8,256]{4,3,2,1,0:T(8,128)S(1)}, f32[2,2,32,8,256]{4,3,2,1,0:T(8,128)S(1)}, u32[]{:S(2)}, u32[]{:S(2)}) collective-permute-start(f32[2,2,32,8,256]{4,3,2,1,0:T(8,128)S(1)} %collective-permute-done.3.far_ref), channel_id=1, source_target_pairs={{0,1},{1,0},{2,3},{3,2},{4,5},{5,4},{6,7},{7,6},{8,9},{9,8},{10,11... | collective-permute-start | bytes 3145736 | tf_op jit(solution)/shard_map/ppermute | solution.py:436
  43.4 0.1 pad.6.clone
  43.5 0.7 ordered.1.amp_hbm
  44.1 0.1 fusion.3
  44.2 0.1 add_add_fusion.notes_ref
  44.3 0.0 collective-permute-done.4.other_near_ref
  44.3 1.3 collective-permute-done.5.other_far_ref
  45.6 4.3 %patterns.1 = (f32[8,200,256]{2,1,0:T(8,128)S(1)}, f32[8,192,256]{2,1,0:T(8,128)S(1)}) custom-call(s32[3,13]{1,0:T(4,128)S(1)} %add_add_fusion.notes_ref, f32[2,2048,256]{2,1,0:T(8,128)} %own_ref.1, f32[2,256,256]{2,1,0:T(8,128)S(1)} %copy-done.2, bf16[6,256,256]{2,1,0:T(8,128)(2,1)S(1)} %ordered.1.amp_hbm, bf16[16,256,256]{2,1,0:T(8,128)(2,1)S(1)} %copy-done.6, ...), custom_call_target="tpu_custom_call" | custom-call | flops 4831838208 | bytes 12582912 | tf_op jit(solution)/shard_map/patterns/pallas_call | solution.py:250
  50.0 0.0 copy-start
  50.0 26.2 %all_to_all.20.got_ref = f32[8,200,256]{2,1,0:T(8,128)S(1)} all-to-all(f32[8,200,256]{2,1,0:T(8,128)S(1)} %get-tuple-element.24), channel_id=1, replica_groups=mesh['tile'=64,'group'=8] {'group'}, dimensions={0} | all-to-all | bytes 3276800 | tf_op jit(solution)/shard_map/all_to_all | solution.py:460
  76.2 4.2 %all-to-all-start.2 = ((f32[8,192,256]{2,1,0:T(8,128)}), f32[8,192,256]{2,1,0:T(8,128)S(1)}, u32[]{:S(2)}, u32[]{:S(2)}) async-start(f32[8,192,256]{2,1,0:T(8,128)} %copy-done), calls=%async_computation.2 | async-start | bytes 3145728 | tf_op jit(solution)/shard_map/all_to_all | solution.py:460
  80.4 1.1 gathered.2
  81.5 2.3 %collective-permute-start.6 = (f32[256,256]{1,0:T(8,128)S(1)}, f32[256,256]{1,0:T(8,128)S(1)}, u32[]{:S(2)}, u32[]{:S(2)}) collective-permute-start(f32[256,256]{1,0:T(8,128)S(1)} %get-tuple-element.26), channel_id=1, source_target_pairs={{0,8},{8,16},{16,24},{24,32},{32,40},{40,48},{48,56},{56,64},{64,7... | collective-permute-start | bytes 786440 | tf_op jit(solution)/shard_map/ppermute | solution.py:427
  83.8 0.0 copy-start.3
  83.8 1.0 copy-done.3
  84.9 3.3 %illumination.1 = f32[256,256]{1,0:T(8,128)S(1)} custom-call(s32[1]{0:T(128)} %bitcast.group_ref, s32[8,13]{1,0:T(8,128)S(1)} %bitcast.36, s32[8,13]{1,0:T(8,128)S(1)} %bitcast.38, f32[2,256,256]{2,1,0:T(8,128)S(1)} %copy-done.3), custom_call_target="tpu_custom_call" | custom-call | flops 4194304 | bytes 8388608 | tf_op jit(solution)/shard_map/illumination/pallas_call | solution.py:368
  88.2 10.8 %collective-permute-done.6 = f32[256,256]{1,0:T(8,128)S(1)} collective-permute-done((f32[256,256]{1,0:T(8,128)S(1)}, f32[256,256]{1,0:T(8,128)S(1)}, u32[]{:S(2)}, u32[]{:S(2)}) %collective-permute-start.6) | collective-permute-done | bytes 262176 | tf_op jit(solution)/shard_map/ppermute | solution.py:427
  99.0 1.0 fusion.1
  100.0 1.1 all-to-all-done.2.got_ref
  101.1 1.1 broadcast_in_dim.10
  102.2 3.5 %all-to-all-start.1 = ((f32[4,32,8,256]{3,2,1,0:T(8,128)}), f32[4,32,8,256]{3,2,1,0:T(8,128)S(1)}, u32[]{:S(2)}, u32[]{:S(2)}) async-start(f32[4,32,8,256]{3,2,1,0:T(8,128)} %broadcast_in_dim.10), calls=%async_computation.1 | async-start | bytes 2097152 | tf_op jit(solution)/shard_map/all_to_all | solution.py:474
  105.7 1.1 gathered.3
  106.8 2.3 %collective-permute-start.7 = (f32[256,256]{1,0:T(8,128)S(1)}, f32[256,256]{1,0:T(8,128)S(1)}, u32[]{:S(2)}, u32[]{:S(2)}) collective-permute-start(f32[256,256]{1,0:T(8,128)S(1)} %get-tuple-element.29), channel_id=1, source_target_pairs={{0,8},{8,16},{16,24},{24,32},{32,40},{40,48},{48,56},{56,64},{64,7... | collective-permute-start | bytes 786440 | tf_op jit(solution)/shard_map/ppermute | solution.py:427
  109.1 14.4 %collective-permute-done.7 = f32[256,256]{1,0:T(8,128)S(1)} collective-permute-done((f32[256,256]{1,0:T(8,128)S(1)}, f32[256,256]{1,0:T(8,128)S(1)}, u32[]{:S(2)}, u32[]{:S(2)}) %collective-permute-start.7) | collective-permute-done | bytes 262176 | tf_op jit(solution)/shard_map/ppermute | solution.py:427
  123.5 1.0 fusion
  124.5 1.1 broadcast_in_dim.11
  125.6 3.9 %all-to-all-start.3 = ((f32[4,32,8,256]{3,2,1,0:T(8,128)}), f32[4,32,8,256]{3,2,1,0:T(8,128)S(1)}, u32[]{:S(2)}, u32[]{:S(2)}) async-start(f32[4,32,8,256]{3,2,1,0:T(8,128)} %broadcast_in_dim.11), calls=%async_computation.3 | async-start | bytes 2097152 | tf_op jit(solution)/shard_map/all_to_all | solution.py:476
  129.5 3.9 %collective-permute-start.9 = (f32[4,32,8,256]{3,2,1,0:T(8,128)S(1)}, f32[4,32,8,256]{3,2,1,0:T(8,128)}, u32[]{:S(2)}, u32[]{:S(2)}) collective-permute-start(f32[4,32,8,256]{3,2,1,0:T(8,128)S(1)} %all-to-all-done.1.refs_0_), channel_id=1, source_target_pairs={{0,1},{1,0},{2,3},{3,2},{4,5},{5,4},{6,7},{7,6},{8,9},{9,8},{10,11... | collective-permute-start | bytes 3145736 | tf_op jit(solution)/shard_map/ppermute | solution.py:436
  133.4 1.1 assembled.3.refs_2_
  134.5 8.0 %all-to-all-done.3.refs_0_ = f32[4,32,8,256]{3,2,1,0:T(8,128)S(1)} async-done(((f32[4,32,8,256]{3,2,1,0:T(8,128)}), f32[4,32,8,256]{3,2,1,0:T(8,128)S(1)}, u32[]{:S(2)}, u32[]{:S(2)}) %all-to-all-start.3) | async-done | bytes 1048608 | tf_op jit(solution)/shard_map/all_to_all | solution.py:476
  142.6 4.9 %collective-permute-start.8 = (f32[4,32,8,256]{3,2,1,0:T(8,128)S(1)}, f32[4,32,8,256]{3,2,1,0:T(8,128)S(1)}, u32[]{:S(2)}, u32[]{:S(2)}) collective-permute-start(f32[4,32,8,256]{3,2,1,0:T(8,128)S(1)} %all-to-all-done.3.refs_0_), channel_id=1, source_target_pairs={{0,1},{1,0},{2,3},{3,2},{4,5},{5,4},{6,7},{7,6},{8,9},{9,8},{10,11... | collective-permute-start | bytes 3145736 | tf_op jit(solution)/shard_map/ppermute | solution.py:436
  147.4 2.6 %assembled.4.refs_1_ = f32[2,32,8,8,256]{4,3,2,1,0:T(8,128)} custom-call(s32[1]{0:T(128)} %bitcast.group_ref, f32[4,32,8,256]{3,2,1,0:T(8,128)S(1)} %all-to-all-done.3.refs_0_, f32[4,32,8,256]{3,2,1,0:T(8,128)} %collective-permute-done.9.refs_1_, f32[2,32,8,8,256]{4,3,2,1,0:T(8,128)} %assembled.3.refs_2_), custom_call_target="tpu_custom_call", output_to_operand_aliasing={{}: (3, {})} | custom-call | bytes 4194304 | tf_op jit(solution)/shard_map/assembled/pallas_call | solution.py:411
  150.1 1.0 assembled.5
  (18 shorter events, 0.0 us)
Async XLA Ops:
  0.0 43.5 %copy-start.4 = (bf16[256,256]{1,0:T(8,128)(2,1)S(1)}, bf16[256,256]{1,0:T(8,128)(2,1)}, u32[]{:S(2)}) copy-start(bf16[256,256]{1,0:T(8,128)(2,1)} %constant.42.clone.turned_ref) | copy-start | bytes 393220
  0.0 43.5 %copy-start.5 = (bf16[256,256]{1,0:T(8,128)(2,1)S(1)}, bf16[256,256]{1,0:T(8,128)(2,1)}, u32[]{:S(2)}) copy-start(bf16[256,256]{1,0:T(8,128)(2,1)} %constant.41.clone.order_ref) | copy-start | bytes 393220
  0.0 10.6 %copy-start.7 = (s32[6]{0:T(128)S(1)}, s32[6]{0:T(128)}, u32[]{:S(2)}) copy-start(s32[6]{0:T(128)} %param.13) | copy-start | bytes 76
  0.0 10.6 %copy-start.8 = (s32[6]{0:T(128)S(1)}, s32[6]{0:T(128)}, u32[]{:S(2)}) copy-start(s32[6]{0:T(128)} %param.12) | copy-start | bytes 76
  0.0 43.4 %copy-start.1 = (bf16[6,256,256]{2,1,0:T(8,128)(2,1)S(1)}, bf16[6,256,256]{2,1,0:T(8,128)(2,1)}, u32[]{:S(2)}) copy-start(bf16[6,256,256]{2,1,0:T(8,128)(2,1)} %amp_ref.1) | copy-start | bytes 2359300
  0.1 45.6 %copy-start.2 = (f32[2,256,256]{2,1,0:T(8,128)S(1)}, f32[2,256,256]{2,1,0:T(8,128)}, u32[]{:S(2)}) copy-start(f32[2,256,256]{2,1,0:T(8,128)} %probe_ref.1) | copy-start | bytes 1572868
  0.1 45.6 %copy-start.6 = (bf16[16,256,256]{2,1,0:T(8,128)(2,1)S(1)}, bf16[16,256,256]{2,1,0:T(8,128)(2,1)}, u32[]{:S(2)}) copy-start(bf16[16,256,256]{2,1,0:T(8,128)(2,1)} %constant.43.clone.tab_hbm) | copy-start | bytes 6291460
  1.8 15.7 %collective-permute-start = (f32[2,32,8,256]{3,2,1,0:T(8,128)S(1)}, f32[2,32,8,256]{3,2,1,0:T(8,128)S(1)}, u32[]{:S(2)}, u32[]{:S(2)}) collective-permute-start(f32[2,32,8,256]{3,2,1,0:T(8,128)S(1)} %get-tuple-element.36), channel_id=1, source_target_pairs={{8,0},{16,8},{24,16},{32,24},{40,32},{48,40},{56,48},{64,56},{72,6... | collective-permute-start | bytes 1572872 | tf_op jit(solution)/shard_map/ppermute | solution.py:427
  7.0 32.9 %collective-permute-start.3 = (f32[2,2,32,8,256]{4,3,2,1,0:T(8,128)S(1)}, f32[2,2,32,8,256]{4,3,2,1,0:T(8,128)S(1)}, u32[]{:S(2)}, u32[]{:S(2)}) collective-permute-start(f32[2,2,32,8,256]{4,3,2,1,0:T(8,128)S(1)} %pad_maximum_fusion.1), channel_id=1, source_target_pairs={{8,0},{16,8},{24,16},{32,24},{40,32},{48,40},{56,48},{64,56},{72,6... | collective-permute-start | bytes 3145736 | tf_op jit(solution)/shard_map/ppermute | solution.py:427
  10.7 6.4 %collective-permute-start.1 = (s32[13]{0:T(128)S(1)}, s32[13]{0:T(128)S(1)}, u32[]{:S(2)}, u32[]{:S(2)}) collective-permute-start(s32[13]{0:T(128)S(1)} %pad_add_fusion), channel_id=1, source_target_pairs={{0,8},{8,16},{16,24},{24,32},{32,40},{40,48},{48,56},{56,64},{64,7... | collective-permute-start | bytes 164 | tf_op jit(solution)/shard_map/ppermute | solution.py:427
  17.5 13.8 %collective-permute-start.2 = (f32[2,32,8,256]{3,2,1,0:T(8,128)S(1)}, f32[2,32,8,256]{3,2,1,0:T(8,128)S(1)}, u32[]{:S(2)}, u32[]{:S(2)}) collective-permute-start(f32[2,32,8,256]{3,2,1,0:T(8,128)S(1)} %collective-permute-done), channel_id=1, source_target_pairs={{0,2},{1,3},{2,4},{3,5},{4,6},{5,7},{6,0},{7,1},{8,10},{9,11},{10,... | collective-permute-start | bytes 1572872 | tf_op jit(solution)/shard_map/ppermute | solution.py:432
  31.4 12.9 %collective-permute-start.4 = (f32[2,2,32,8,256]{4,3,2,1,0:T(8,128)S(1)}, f32[2,2,32,8,256]{4,3,2,1,0:T(8,128)S(1)}, u32[]{:S(2)}, u32[]{:S(2)}) collective-permute-start(f32[2,2,32,8,256]{4,3,2,1,0:T(8,128)S(1)} %pad_maximum_fusion.near_ref), channel_id=1, source_target_pairs={{0,1},{1,0},{2,3},{3,2},{4,5},{5,4},{6,7},{7,6},{8,9},{9,8},{10,11... | collective-permute-start | bytes 3145736 | tf_op jit(solution)/shard_map/ppermute | solution.py:436
  39.9 5.7 %collective-permute-start.5 = (f32[2,2,32,8,256]{4,3,2,1,0:T(8,128)S(1)}, f32[2,2,32,8,256]{4,3,2,1,0:T(8,128)S(1)}, u32[]{:S(2)}, u32[]{:S(2)}) collective-permute-start(f32[2,2,32,8,256]{4,3,2,1,0:T(8,128)S(1)} %collective-permute-done.3.far_ref), channel_id=1, source_target_pairs={{0,1},{1,0},{2,3},{3,2},{4,5},{5,4},{6,7},{7,6},{8,9},{9,8},{10,11... | collective-permute-start | bytes 3145736 | tf_op jit(solution)/shard_map/ppermute | solution.py:436
  50.0 26.2 %copy-start = (f32[8,192,256]{2,1,0:T(8,128)}, f32[8,192,256]{2,1,0:T(8,128)S(1)}, u32[]{:S(2)}) copy-start(f32[8,192,256]{2,1,0:T(8,128)S(1)} %get-tuple-element.27) | copy-start | bytes 4718596
  76.2 25.0 %all-to-all-start.2 = ((f32[8,192,256]{2,1,0:T(8,128)}), f32[8,192,256]{2,1,0:T(8,128)S(1)}, u32[]{:S(2)}, u32[]{:S(2)}) async-start(f32[8,192,256]{2,1,0:T(8,128)} %copy-done), calls=%async_computation.2 | async-start | bytes 3145728 | tf_op jit(solution)/shard_map/all_to_all | solution.py:460
  81.5 17.4 %collective-permute-start.6 = (f32[256,256]{1,0:T(8,128)S(1)}, f32[256,256]{1,0:T(8,128)S(1)}, u32[]{:S(2)}, u32[]{:S(2)}) collective-permute-start(f32[256,256]{1,0:T(8,128)S(1)} %get-tuple-element.26), channel_id=1, source_target_pairs={{0,8},{8,16},{16,24},{24,32},{32,40},{40,48},{48,56},{56,64},{64,7... | collective-permute-start | bytes 786440 | tf_op jit(solution)/shard_map/ppermute | solution.py:427
  83.8 1.0 copy-start.3
  102.2 22.3 %all-to-all-start.1 = ((f32[4,32,8,256]{3,2,1,0:T(8,128)}), f32[4,32,8,256]{3,2,1,0:T(8,128)S(1)}, u32[]{:S(2)}, u32[]{:S(2)}) async-start(f32[4,32,8,256]{3,2,1,0:T(8,128)} %broadcast_in_dim.10), calls=%async_computation.1 | async-start | bytes 2097152 | tf_op jit(solution)/shard_map/all_to_all | solution.py:474
  106.8 16.7 %collective-permute-start.7 = (f32[256,256]{1,0:T(8,128)S(1)}, f32[256,256]{1,0:T(8,128)S(1)}, u32[]{:S(2)}, u32[]{:S(2)}) collective-permute-start(f32[256,256]{1,0:T(8,128)S(1)} %get-tuple-element.29), channel_id=1, source_target_pairs={{0,8},{8,16},{16,24},{24,32},{32,40},{40,48},{48,56},{56,64},{64,7... | collective-permute-start | bytes 786440 | tf_op jit(solution)/shard_map/ppermute | solution.py:427
  125.6 17.0 %all-to-all-start.3 = ((f32[4,32,8,256]{3,2,1,0:T(8,128)}), f32[4,32,8,256]{3,2,1,0:T(8,128)S(1)}, u32[]{:S(2)}, u32[]{:S(2)}) async-start(f32[4,32,8,256]{3,2,1,0:T(8,128)} %broadcast_in_dim.11), calls=%async_computation.3 | async-start | bytes 2097152 | tf_op jit(solution)/shard_map/all_to_all | solution.py:476
  129.5 18.0 %collective-permute-start.9 = (f32[4,32,8,256]{3,2,1,0:T(8,128)S(1)}, f32[4,32,8,256]{3,2,1,0:T(8,128)}, u32[]{:S(2)}, u32[]{:S(2)}) collective-permute-start(f32[4,32,8,256]{3,2,1,0:T(8,128)S(1)} %all-to-all-done.1.refs_0_), channel_id=1, source_target_pairs={{0,1},{1,0},{2,3},{3,2},{4,5},{5,4},{6,7},{7,6},{8,9},{9,8},{10,11... | collective-permute-start | bytes 3145736 | tf_op jit(solution)/shard_map/ppermute | solution.py:436
  142.6 7.5 %collective-permute-start.8 = (f32[4,32,8,256]{3,2,1,0:T(8,128)S(1)}, f32[4,32,8,256]{3,2,1,0:T(8,128)S(1)}, u32[]{:S(2)}, u32[]{:S(2)}) collective-permute-start(f32[4,32,8,256]{3,2,1,0:T(8,128)S(1)} %all-to-all-done.3.refs_0_), channel_id=1, source_target_pairs={{0,1},{1,0},{2,3},{3,2},{4,5},{5,4},{6,7},{7,6},{8,9},{9,8},{10,11... | collective-permute-start | bytes 3145736 | tf_op jit(solution)/shard_map/ppermute | solution.py:436
